TPU v7x, 128 devices: a whole 4x4x4 slice. The times are simulated.
128 devices in a mesh: rows: 4 (over y), cents: 32 (over x, z, core).
Axes of the slice: x: 4, y: 4, z: 4, core: 2. Of those that a mesh axis runs over, the one named last changes fastest.
Arguments:
- vectors: bfloat16 [8192, 1024], P(('rows', 'cents')), may hold values from -24 to 24, as said below
- centroids: bfloat16 [65536, 1024], P('cents'), may hold values from -0.1875 to 0.1875
Outputs:
- updated: bfloat16 [65536, 1024], P('cents', 'rows')
- masses: float32 [65536], P('cents')
Inputs may be any that keep to these rules, and one draw needn't show every extreme that they name: `vectors`: entries are real-valued and of order one, with rows of differing scales.
All inputs are finite; a program needn't handle non-finite values.
Results may differ from a plain program's by a relative error of at most 0.015.
Values may be sent and summed in bfloat16 or wider, within the bound.
No kernel may reach another device: no remote copies, remote signals or barrier semaphores. Data moves between devices by JAX's collectives and lax.ppermute only.
A program may use at most 128 MiB of HBM per device.

v0:
```python
import jax
import jax.numpy as jnp
from jax import lax
from jax.sharding import PartitionSpec as P

ROUNDS = 3


SHARP = 0.75


def body(vectors, centroids):
    group = lax.all_gather(vectors, "cents", axis=0, tiled=True)
    logits = lax.dot_general(
        group, centroids, (((1,), (1,)), ((), ())), preferred_element_type=jnp.float32
    )
    weights = jnp.exp(SHARP * logits)
    groups_count = lax.axis_size("rows")
    shards_count = lax.axis_size("cents")
    target = group.shape[0] * groups_count / (centroids.shape[0] * shards_count)
    row_scale = jnp.ones((group.shape[0],), jnp.float32)
    col_scale = jnp.ones((centroids.shape[0],), jnp.float32)
    for step in range(ROUNDS):
        colmass = lax.psum(jnp.dot(row_scale, weights, precision=lax.Precision.HIGHEST), "rows")
        col_scale = target / colmass
        rowmass = lax.psum(jnp.dot(weights, col_scale, precision=lax.Precision.HIGHEST), "cents")
        row_scale = 1.0 / rowmass
    plan = weights * row_scale[:, None] * col_scale[None, :]
    masses = lax.psum(jnp.sum(plan, axis=0), "rows")
    plan_low = plan.astype(jnp.bfloat16)
    partial_value = lax.dot_general(
        plan_low, group, (((0,), (0,)), ((), ())), preferred_element_type=jnp.float32
    )
    share = centroids.shape[1] // groups_count
    offset = lax.axis_index("rows") * share
    totals = lax.psum(partial_value.astype(jnp.bfloat16), "rows").astype(jnp.float32)
    sums = lax.dynamic_slice_in_dim(totals, offset, share, 1)
    own_cols = lax.dynamic_slice_in_dim(centroids, offset, share, 1).astype(jnp.float32)
    updated = 0.5 * own_cols + 0.5 * sums / masses[:, None]
    return (updated.astype(jnp.bfloat16), masses)


def solution(mesh):
    return jax.shard_map(
        body,
        mesh=mesh,
        in_specs=(P(("rows", "cents"), None), P("cents", None)),
        out_specs=(P("cents", "rows"), P("cents")),
        check_vma=False,
    )
```

profile of v0, /device:TPU:0, one launch (start us, length us, event | category | flops | bytes accessed | tf_op | source)
XLA Modules:
  0.0 495.0 jit_solution(11898089071760647466)
XLA Ops:
  7.2 0.0 all-gather.2.cloned.1.call-start
  7.2 0.7 all-gather.2.cloned.1.call-update
  7.9 0.0 all-reduce.2.cloned.1.call-start
  7.9 51.2 %all-gather.2.cloned.1.call-done = bf16[2048,1024]{1,0:T(8,128)(2,1)} async-done(((bf16[64,1024]{1,0:T(8,128)(2,1)}), bf16[2048,1024]{1,0:T(8,128)(2,1)}) %all-gather.2.cloned.1.call-update) | async-done | bytes 4194320 | tf_op jit(solution)/shard_map/all_gather | solution.py:13
  59.1 12.8 %multiply_exponential_fusion = f32[2048,2048]{1,0:T(8,128)S(1)} fusion(bf16[2048,1024]{1,0:T(8,128)(2,1)} %all-gather.2.cloned.1.call-done, bf16[2048,1024]{1,0:T(8,128)(2,1)} %param.3), kind=kOutput, calls=%fused_computation.1 | convolution fusion | flops 8594128896 | bytes 25165824 | tf_op jit(solution)/shard_map/dot_general | solution.py:14
  71.9 0.0 copy-start
  72.0 5.7 %copy-done = f32[2048,2048]{1,0:T(8,128)} copy-done((f32[2048,2048]{1,0:T(8,128)}, f32[2048,2048]{1,0:T(8,128)S(1)}, u32[]{:S(2)}) %copy-start) | copy-done | bytes 16777240
  77.7 7.9 %fusion.9 = f32[1,2048]{1,0:T(1,128)S(1)} fusion(f32[2048,2048]{1,0:T(8,128)S(1)} %multiply_exponential_fusion), kind=kOutput, calls=%fused_computation.9 | convolution fusion | flops 50331648 | bytes 16785408 | tf_op jit(solution)/shard_map/dot_general | solution.py:24
  85.6 10.6 %psum.56 = f32[2048]{0:T(1024)S(1)} all-reduce(f32[2048]{0:T(1024)S(1)} %bitcast.35), channel_id=1, replica_groups=mesh['rows'=4,'cents'=32] {'rows'}, use_global_device_ids=true, to_apply=%region_0.0 | all-reduce | flops 2048 | bytes 16384 | tf_op jit(solution)/shard_map/psum | solution.py:24
  96.2 17.7 %fusion.12 = f32[1,2048]{1,0:T(1,128)S(1)} fusion(f32[2048,2048]{1,0:T(8,128)} %copy-done, f32[2048,1]{0,1:T(1,128)S(1)} %bitcast.29), kind=kOutput, calls=%fused_computation.18 | convolution fusion | flops 50331648 | bytes 16793600 | tf_op jit(solution)/shard_map/dot_general | solution.py:26
  113.9 64.2 %psum.57 = f32[2048]{0:T(1024)S(1)} all-reduce(f32[2048]{0:T(1024)S(1)} %bitcast.26), channel_id=1, replica_groups=mesh['rows'=4,'cents'=32] {'cents'}, use_global_device_ids=true, to_apply=%region_1.0 | all-reduce | flops 2048 | bytes 16384 | tf_op jit(solution)/shard_map/psum | solution.py:26
  178.1 11.5 %fusion.13 = f32[1,2048]{1,0:T(1,128)S(1)} fusion(f32[2048,1]{0,1:T(1,128)S(1)} %bitcast.30, f32[2048,2048]{1,0:T(8,128)} %copy-done), kind=kOutput, calls=%fused_computation.19 | convolution fusion | flops 50331648 | bytes 16793600 | tf_op jit(solution)/shard_map/dot_general | solution.py:24
  189.5 7.9 %psum.58 = f32[2048]{0:T(1024)S(1)} all-reduce(f32[2048]{0:T(1024)S(1)} %bitcast.31), channel_id=1, replica_groups=mesh['rows'=4,'cents'=32] {'rows'}, use_global_device_ids=true, to_apply=%region_2.0 | all-reduce | flops 2048 | bytes 16384 | tf_op jit(solution)/shard_map/psum | solution.py:24
  197.4 17.7 %fusion.14 = f32[1,2048]{1,0:T(1,128)S(1)} fusion(f32[2048,2048]{1,0:T(8,128)} %copy-done, f32[2048,1]{0,1:T(1,128)S(1)} %bitcast.32), kind=kOutput, calls=%fused_computation.20 | convolution fusion | flops 50331648 | bytes 16793600 | tf_op jit(solution)/shard_map/dot_general | solution.py:26
  215.1 63.7 %psum.59 = f32[2048]{0:T(1024)S(1)} all-reduce(f32[2048]{0:T(1024)S(1)} %bitcast.27), channel_id=1, replica_groups=mesh['rows'=4,'cents'=32] {'cents'}, use_global_device_ids=true, to_apply=%region_3.0 | all-reduce | flops 2048 | bytes 16384 | tf_op jit(solution)/shard_map/psum | solution.py:26
  278.8 11.5 %fusion.15 = f32[1,2048]{1,0:T(1,128)S(1)} fusion(f32[2048,1]{0,1:T(1,128)S(1)} %bitcast.33, f32[2048,2048]{1,0:T(8,128)} %copy-done), kind=kOutput, calls=%fused_computation.21 | convolution fusion | flops 50331648 | bytes 16793600 | tf_op jit(solution)/shard_map/dot_general | solution.py:24
  290.3 9.8 %psum.60 = f32[2048]{0:T(1024)S(1)} all-reduce(f32[2048]{0:T(1024)S(1)} %bitcast.34), channel_id=1, replica_groups=mesh['rows'=4,'cents'=32] {'rows'}, use_global_device_ids=true, to_apply=%region_4.0 | all-reduce | flops 2048 | bytes 16384 | tf_op jit(solution)/shard_map/psum | solution.py:24
  300.1 17.8 %fusion.16 = f32[1,2048]{1,0:T(1,128)S(1)} fusion(f32[2048,2048]{1,0:T(8,128)} %copy-done, f32[2048,1]{0,1:T(1,128)S(1)} %bitcast.25), kind=kOutput, calls=%fused_computation.22 | convolution fusion | flops 50331648 | bytes 16793600 | tf_op jit(solution)/shard_map/dot_general | solution.py:26
  317.9 63.7 %psum.61 = f32[2048]{0:T(1024)S(1)} all-reduce(f32[2048]{0:T(1024)S(1)} %bitcast.28), channel_id=1, replica_groups=mesh['rows'=4,'cents'=32] {'cents'}, use_global_device_ids=true, to_apply=%region_5.0 | all-reduce | flops 2048 | bytes 16384 | tf_op jit(solution)/shard_map/psum | solution.py:26
  381.6 16.0 %fusion.6 = bf16[2048,1024]{1,0:T(8,128)(2,1)} fusion(bf16[2048,1024]{1,0:T(8,128)(2,1)} %all-gather.2.cloned.1.call-done, f32[2048,2048]{1,0:T(8,128)} %copy-done, f32[2048]{0:T(1024)S(1)} %broadcast_divide_fusion, f32[2048]{0:T(1024)S(1)} %broadcast_divide_fusion.5), kind=kOutput, calls=%fused_computation.7 | convolution fusion | flops 8604614656 | bytes 25182208 | tf_op jit(solution)/shard_map/dot_general | solution.py:31
  397.6 0.0 all-reduce.2.cloned.1.call-update
  397.6 8.3 %fusion = f32[2048]{0:T(1024)S(1)} fusion(f32[2048,2048]{1,0:T(8,128)} %copy-done, f32[2048]{0:T(1024)S(1)} %broadcast_divide_fusion, f32[2048]{0:T(1024)S(1)} %broadcast_divide_fusion.5), kind=kLoop, calls=%fused_computation.2 | loop fusion | flops 12580864 | bytes 16801792 | tf_op jit(solution)/shard_map/reduce_sum | solution.py:29
  405.9 8.2 %psum.63 = f32[2048]{0:T(1024)S(1)} all-reduce(f32[2048]{0:T(1024)S(1)} %fusion), channel_id=1, replica_groups=mesh['rows'=4,'cents'=32] {'rows'}, use_global_device_ids=true, to_apply=%region_8.0 | all-reduce | flops 2048 | bytes 16384 | tf_op jit(solution)/shard_map/psum | solution.py:29
  414.0 0.0 copy-start.1
  414.1 70.6 %all-reduce.2.cloned.1.call-done = bf16[2048,1024]{1,0:T(8,128)(2,1)} async-done(((bf16[2048,1024]{1,0:T(8,128)(2,1)}), bf16[2048,1024]{1,0:T(8,128)(2,1)}) %all-reduce.2.cloned.1.call-update) | async-done | bytes 4194320 | tf_op jit(solution)/shard_map/psum | solution.py:36
  484.7 3.0 add_convert_fusion
  487.7 0.0 copy-done.1
  (6 shorter events, 0.0 us)
Async XLA Ops:
  7.2 52.0 %all-gather.2.cloned.1.call-start = ((), (), s32[]{:S(2)}) async-start(), calls=%async_computation | async-start | bytes 4325376 | tf_op jit(solution)/shard_map/all_gather | solution.py:13
  7.9 476.8 %all-reduce.2.cloned.1.call-start = ((), (), s32[]{:S(2)}) async-start(), calls=%async_computation.1 | async-start | bytes 8388608 | tf_op jit(solution)/shard_map/psum | solution.py:36
  71.9 5.7 %copy-start = (f32[2048,2048]{1,0:T(8,128)}, f32[2048,2048]{1,0:T(8,128)S(1)}, u32[]{:S(2)}) copy-start(f32[2048,2048]{1,0:T(8,128)S(1)} %multiply_exponential_fusion) | copy-start | bytes 50331652
  414.0 73.7 %copy-start.1 = (f32[2048]{0:T(1024)}, f32[2048]{0:T(1024)S(1)}, u32[]{:S(2)}) copy-start(f32[2048]{0:T(1024)S(1)} %psum.63) | copy-start | bytes 24580
Sparse Core Ops, SparseCore 0:
  10.3 48.8 all-gather.1
  397.7 86.9 all-reduce.1
where the time goes:
time: 500 us; the launch traced here: 495 us
  blocking collectives  228 us (46%)
  waiting for transfers between devices  123 us (25%)
  matrix products  113 us (23%)
  between operations  14.7 us (3%)
  other arithmetic  11.3 us (2%)
  local copies, waits for them, and re-layouts  5.71 us (1%)
    psum x3, blocking collectives, body(): lax.psum(jnp.dot(weights, col_scale, precision=lax.Precision.HIGHEST), 'c...  192 us
    psum x1, waiting for transfers between devices, body(): lax.psum(partial_value.astype(jnp.bfloat16), 'rows').astype(jnp.float32)  70.6 us
    dot_general x3, matrix products, body(): jnp.dot(weights, col_scale, precision=lax.Precision.HIGHEST)  53.2 us
    all_gather x1, waiting for transfers between devices, body(): group = lax.all_gather(vectors, 'cents', axis=0, tiled=True)  51.2 us
    dot_general x3, matrix products, body(): jnp.dot(row_scale, weights, precision=lax.Precision.HIGHEST)  30.8 us
    psum x3, blocking collectives, body(): lax.psum(jnp.dot(row_scale, weights, precision=lax.Precision.HIGHEST), 'r...  28.2 us
    dot_general x1, matrix products, body(): lax.dot_general(plan_low, group, (((0,), (0,)), ((), ())), preferred_elem...  16 us
    dot_general x1, matrix products, body(): lax.dot_general(group, centroids, (((1,), (1,)), ((), ())), preferred_ele...  12.8 us
  transfers between devices with their start and end apart: 2, of which 2 were waited for; matrix products, arithmetic and copies ran while one was open for 2% of the time, Pallas kernels for 0%

commit v1 on v0

v1 whole, which is shorter than its diff:
```python
import jax
import jax.numpy as jnp
from jax import lax
from jax.experimental import pallas as pl
from jax.experimental.pallas import tpu as pltpu
from jax.sharding import Mesh, PartitionSpec as P

ROUNDS = 3
SHARP = 0.75
LOG2E = 1.4426950408889634
CENTS = ("x", "z", "core")
LANES = 128
TAIL = 32
WEIGH_VMEM = 10 * 1024 * 1024
PLAN_VMEM = 10 * 1024 * 1024
SUM_VMEM = 8 * 1024 * 1024

VM = pl.BlockSpec(memory_space=pltpu.VMEM)
SM = pl.BlockSpec(memory_space=pltpu.SMEM)


def params(vmem):
    return pltpu.CompilerParams(vmem_limit_bytes=vmem)


def held(x):
    return pltpu.with_memory_space_constraint(x, pltpu.VMEM)


def row_of(block):
    return jnp.sum(block.T, axis=0, keepdims=True)


def down(row):
    return jnp.broadcast_to(row, (LANES, LANES)).T


def weigh_kernel(cents_ref, vecs_ref, w_ref, mass_ref, acc_ref):
    n, m = w_ref.shape
    rows, cols = min(n, 512), min(m, 512)
    for k in range(0, n, rows):
        acc = None
        for i in range(0, m, cols):
            logits = lax.dot_general(
                cents_ref[k : k + rows, :],
                vecs_ref[i : i + cols, :],
                (((1,), (1,)), ((), ())),
                preferred_element_type=jnp.float32,
            )
            w = jnp.exp2(logits * (SHARP * LOG2E))
            w_ref[k : k + rows, i : i + cols] = w
            for j in range(0, cols, LANES):
                acc = w[:, j : j + LANES] if acc is None else acc + w[:, j : j + LANES]
        acc_ref[k : k + rows, :] = acc
    for g in range(n // LANES):
        mass_ref[g : g + 1, :] = row_of(acc_ref[g * LANES : (g + 1) * LANES, :])


def weigh(cents, vecs):
    n, d = cents.shape
    m = vecs.shape[0]
    return pl.pallas_call(
        weigh_kernel,
        in_specs=[VM, VM],
        out_specs=[VM, VM],
        out_shape=[pltpu.VMEM((n, m), jnp.float32), jax.ShapeDtypeStruct((n // LANES, LANES), jnp.float32)],
        scratch_shapes=[pltpu.VMEM((n, LANES), jnp.float32)],
        compiler_params=params(WEIGH_VMEM),
        cost_estimate=pl.CostEstimate(flops=2 * n * m * d, bytes_accessed=2 * (n + m) * d, transcendentals=n * m),
        name="weigh",
    )(held(cents), held(vecs))


def row_kernel(target, core_ref, w0_ref, w1_ref, a_ref, b_ref, c_ref, d_ref, out_ref, scale_ref):
    scale_ref[...] = target / ((a_ref[...] + b_ref[...]) + (c_ref[...] + d_ref[...]))
    tiles = w0_ref.shape[1] // LANES
    accs = [None] * (2 * tiles)
    for b in range(w0_ref.shape[0] // LANES):
        part = slice(b * LANES, (b + 1) * LANES)
        s = down(scale_ref[b : b + 1, :])
        for j in range(2 * tiles):
            ref, t = (w0_ref, j) if j < tiles else (w1_ref, j - tiles)
            p = ref[part, t * LANES : (t + 1) * LANES] * s
            p = jnp.sum(p.reshape(LANES // 8, 8, LANES), axis=0)
            accs[j] = p if b == 0 else accs[j] + p
    rows = [jnp.sum(a, axis=0, keepdims=True) for a in accs]
    here = jnp.concatenate(rows[:tiles], axis=0)
    there = jnp.concatenate(rows[tiles:], axis=0)
    first = core_ref[0] == 0
    value = jnp.concatenate([jnp.where(first, here, there), jnp.where(first, there, here)], axis=0)
    for q in range(out_ref.shape[0]):
        out_ref[q] = value


def row_pass(target, core, w, masses, peers):
    n = w[0].shape[0]
    lines = (w[0].shape[1] + w[1].shape[1]) // LANES
    return pl.pallas_call(
        lambda *refs: row_kernel(target, *refs),
        in_specs=[SM] + [VM] * 6,
        out_specs=[VM, VM],
        out_shape=[
            jax.ShapeDtypeStruct((peers, lines, LANES), jnp.float32),
            jax.ShapeDtypeStruct((n // LANES, LANES), jnp.float32),
        ],
        compiler_params=params(8 * 1024 * 1024),
        name="row_pass",
    )(core, held(w[0]), held(w[1]), *masses)


def local_scale(core_ref, sums_ref):
    total = sums_ref[0]
    for q in range(1, sums_ref.shape[0]):
        total = total + sums_ref[q]
    scale = 1.0 / total
    half = scale.shape[0] // 2
    first = core_ref[0] == 0
    a, b = scale[:half], scale[half:]
    return jnp.concatenate([jnp.where(first, a, b), jnp.where(first, b, a)], axis=0)


def col_kernel(core_ref, w0_ref, w1_ref, sums_ref, out_ref):
    scale = local_scale(core_ref, sums_ref)
    tiles = w0_ref.shape[1] // LANES

    for b in range(w0_ref.shape[0] // LANES):
        part = slice(b * LANES, (b + 1) * LANES)
        acc = None
        for j in range(2 * tiles):
            ref, t = (w0_ref, j) if j < tiles else (w1_ref, j - tiles)
            p = ref[part, t * LANES : (t + 1) * LANES] * scale[j : j + 1, :]
            acc = p if acc is None else acc + p
        out_ref[b : b + 1, :] = row_of(acc)


def col_pass(core, w, sums):
    n = w[0].shape[0]
    return pl.pallas_call(
        col_kernel,
        in_specs=[SM] + [VM] * 3,
        out_specs=VM,
        out_shape=jax.ShapeDtypeStruct((n // LANES, LANES), jnp.float32),
        compiler_params=params(8 * 1024 * 1024),
        name="col_pass",
    )(core, held(w[0]), held(w[1]), sums)


def product(plan_ref, v0_ref, v1_ref, rows, cols):
    m = v0_ref.shape[0]
    a = jnp.dot(plan_ref[rows, :m], v0_ref[:, cols], preferred_element_type=jnp.float32)
    return a + jnp.dot(plan_ref[rows, m:], v1_ref[:, cols], preferred_element_type=jnp.float32)


def split(x):
    hi = x.astype(jnp.bfloat16)
    rest = x - hi.astype(jnp.float32)
    mid = rest.astype(jnp.bfloat16)
    return hi, mid, (rest - mid.astype(jnp.float32)).astype(jnp.bfloat16)


def put_tail(ref, x):
    hi, mid, lo = split(x)
    top, lines = ref.shape[0] - TAIL, x.shape[0]
    ref[top : top + lines, :LANES] = hi
    ref[top : top + lines, LANES:] = mid
    ref[top + lines :, :LANES] = lo
    ref[top + lines :, LANES:] = jnp.zeros_like(lo)


def get_tail(ref):
    f32, top, lines = jnp.float32, ref.shape[0] - TAIL, TAIL // 2
    hi, mid = ref[top : top + lines, :LANES].astype(f32), ref[top : top + lines, LANES:].astype(f32)
    return (hi + mid) + ref[top + lines :, :LANES].astype(f32)


def plan_kernel(
    share, place_ref, w0_ref, w1_ref, sums_ref, scale_ref, v0_ref, v1_ref, plan_ref, mass_ref, fa_ref, fb_ref
):
    scale = local_scale(place_ref, sums_ref)
    tiles = w0_ref.shape[1] // LANES
    n = w0_ref.shape[0]
    rows = 2 * LANES
    cols = pl.ds(pl.multiple_of(place_ref[1] * share, share), share)

    def half(first, o_ref):
        def body(b, carry):
            top = first + b * rows
            for g in range(rows // LANES):
                part = pl.ds(pl.multiple_of(top + g * LANES, LANES), LANES)
                line = pl.ds(top // LANES + g, 1)
                s = down(scale_ref[line, :])
                acc = None
                for j in range(2 * tiles):
                    ref, t = (w0_ref, j) if j < tiles else (w1_ref, j - tiles)
                    p = ref[part, t * LANES : (t + 1) * LANES] * scale[j : j + 1, :]
                    acc = p if acc is None else acc + p
                    plan_ref[part, j * LANES : (j + 1) * LANES] = (p * s).astype(jnp.bfloat16)
                mass_ref[line, :] = row_of(acc)
            out = product(plan_ref, v0_ref, v1_ref, pl.ds(pl.multiple_of(top, rows), rows), cols)
            o_ref[pl.ds(pl.multiple_of(b * rows, rows), rows), :] = out.astype(o_ref.dtype)
            return carry

        lax.fori_loop(0, n // 2 // rows, body, 0, unroll=2)

    half(0, fa_ref)
    half(n // 2, fb_ref)
    put_tail(fa_ref, mass_ref[...])
    put_tail(fb_ref, mass_ref[...])


def make_plan(place, w, sums, scale, vecs, share):
    n, m = w[0].shape
    part = jax.ShapeDtypeStruct((n // 2 + TAIL, share), jnp.bfloat16)
    return pl.pallas_call(
        lambda *refs: plan_kernel(share, *refs),
        in_specs=[SM] + [VM] * 6,
        out_specs=[VM] * 4,
        out_shape=[
            pltpu.VMEM((n, 2 * m), jnp.bfloat16),
            jax.ShapeDtypeStruct((n // LANES, LANES), jnp.float32),
            part,
            part,
        ],
        compiler_params=params(PLAN_VMEM),
        name="make_plan",
    )(place, held(w[0]), held(w[1]), sums, scale, held(vecs[0]), held(vecs[1]))


def sum_kernel(first, count, turn, share, planes, place_ref, plan_ref, v0_ref, v1_ref, *refs):
    out_ref = refs[-1]
    rows = 512
    cols = pl.ds(pl.multiple_of(lax.rem(place_ref[1] + turn, planes) * share, share), share)
    for at in range(0, count, rows):
        out = product(plan_ref, v0_ref, v1_ref, slice(first + at, first + at + rows), cols)
        if len(refs) > 1:
            out = out + refs[0][at : at + rows, :].astype(jnp.float32)
        out_ref[at : at + rows, :] = out.astype(out_ref.dtype)
    if len(refs) > 1:
        out_ref[count:, :] = refs[0][count:, :]


def slice_sum(place, plan, vecs, planes, turn, first, count, dtype, arrived=None):
    more = [] if arrived is None else [arrived]
    m, d = vecs[0].shape
    share = d // planes
    return pl.pallas_call(
        lambda *refs: sum_kernel(first, count, turn, share, planes, *refs),
        in_specs=[SM] + [VM] * (3 + len(more)),
        out_specs=VM,
        out_shape=jax.ShapeDtypeStruct((count + (TAIL if more else 0), share), dtype),
        compiler_params=params(SUM_VMEM),
        cost_estimate=pl.CostEstimate(
            flops=4 * count * m * share, bytes_accessed=4 * (count + m) * share, transcendentals=0
        ),
        name="slice_sum",
    )(place, held(plan), held(vecs[0]), held(vecs[1]), *more)


def finish_kernel(share, place_ref, cents_ref, own_ref, scale_ref, m_ref, fa, fb, ua, ub, da, db, out_ref, mass_ref):
    mass_ref[...] = scale_ref[...] * ((m_ref[...] + get_tail(ua)) + (get_tail(fa) + get_tail(fb)))
    n = out_ref.shape[0]
    half = n // 2
    f32 = jnp.float32
    for line in range(n // LANES):
        part = slice(line * LANES, (line + 1) * LANES)
        up, dn, at = (ua, da, 0) if line * LANES < half else (ub, db, half)
        there = slice(part.start - at, part.stop - at)
        sums = own_ref[part, :] + (up[there, :].astype(f32) + dn[there, :].astype(f32))
        inverse = down(0.5 / mass_ref[line : line + 1, :])
        for j in range(0, share, LANES):
            value = 0.5 * cents_ref[part, j : j + LANES].astype(f32) + sums[:, j : j + LANES] * inverse
            out_ref[part, j : j + LANES] = value.astype(out_ref.dtype)


def finish(place, centroids, own, scale, mass, arrived):
    n, share = own.shape
    return pl.pallas_call(
        lambda *refs: finish_kernel(share, *refs),
        grid_spec=pltpu.PrefetchScalarGridSpec(
            num_scalar_prefetch=1,
            grid=(1,),
            in_specs=[pl.BlockSpec((n, share), lambda i, place: (0, place[2]))] + [VM] * 9,
            out_specs=[VM, VM],
        ),
        out_shape=[
            jax.ShapeDtypeStruct((n, share), jnp.bfloat16),
            jax.ShapeDtypeStruct(scale.shape, jnp.float32),
        ],
        compiler_params=params(16 * 1024 * 1024),
        name="finish",
    )(place, centroids, own, scale, mass, *arrived)


def move(x, axis, by):
    n = lax.axis_size(axis)
    return lax.ppermute(x, axis, [(i, (i + by) % n) for i in range(n)])


def row_peers(x):
    return x, move(x, "y", 2), move(x, "y", 1), move(x, "y", 3)


def body(vectors, centroids):
    planes = lax.axis_size("y")
    core, y = lax.axis_index("core"), lax.axis_index("y")
    place = jnp.stack([core, lax.rem(y + 2, planes), y]).astype(jnp.int32)
    side = lax.axis_size("x") * lax.axis_size("z")
    peers = side * lax.axis_size("core")
    n, d = centroids.shape
    share = d // planes
    target = vectors.shape[0] * planes * peers / (n * peers)

    copies = jnp.broadcast_to(vectors[None], (side,) + vectors.shape)
    mine = lax.all_to_all(copies, ("x", "z"), 0, 0, tiled=True).reshape(side * vectors.shape[0], d)
    other = move(mine, "core", 1)
    vecs = (mine, other)
    w0, mass0 = weigh(centroids, mine)
    w1, mass1 = weigh(centroids, other)
    w = (w0, w1)

    colmass = mass0 + mass1
    for step in range(ROUNDS):
        sums, scale = row_pass(target, place, w, row_peers(colmass), peers)
        sums = lax.all_to_all(sums, CENTS, 0, 0, tiled=True)
        if step < ROUNDS - 1:
            colmass = col_pass(place, w, sums)

    half = n // 2
    low = jnp.bfloat16

    def part(turn, first, count, dtype, arrived=None):
        return slice_sum(place, plan, vecs, planes, turn, first, count, dtype, arrived)

    plan, colmass, far_a, far_b = make_plan(place, w, sums, scale, vecs, share)
    far_a, far_b = move(far_a, "y", 1), move(far_b, "y", 3)
    up_b = move(part(3, half, half, low), "y", 1)
    down_a = move(part(1, 0, half, low), "y", 3)
    own = part(2, 0, n, jnp.float32)
    own, far_a, far_b = lax.optimization_barrier((own, far_a, far_b))
    up_a = move(part(3, 0, half, low, far_a), "y", 1)
    down_b = move(part(1, half, half, low, far_b), "y", 3)
    updated, masses = finish(place, centroids, own, scale, colmass, (far_a, far_b, up_a, up_b, down_a, down_b))
    return updated, masses.reshape(n)


def solution(mesh):
    sizes = (mesh.shape["rows"], 4, 4, 2)
    torus = Mesh(mesh.devices.reshape(sizes), ("y",) + CENTS)
    return jax.shard_map(
        body,
        mesh=torus,
        in_specs=(P(("y",) + CENTS, None), P(CENTS, None)),
        out_specs=(P(CENTS, "y"), P(CENTS)),
        check_vma=False,
    )
```

time: 500 us -> 179 us (0.36)
  blocking collectives: 228 us -> 73.8 us
  matrix products: 113 us -> 0 us
  waiting for transfers between devices: 123 us -> 29.3 us
  Pallas kernels: 0 us -> 45.8 us
  starting transfers between devices: 0.08 us -> 25 us
  between operations: 14.7 us -> 0.76 us
  other arithmetic: 11.3 us -> 0.08 us
    psum x7 -> x0, blocking collectives: 228 us -> none  [the longest x3 192 us: body(): lax.psum(jnp.dot(weights, col_scale, precision=lax.Precision.HIGHEST), 'c...]
    dot_general x8 -> x0, matrix products: 113 us -> none  [the longest x3 53.2 us: body(): jnp.dot(weights, col_scale, precision=lax.Precision.HIGHEST)]
    all_to_all x0 -> x4, blocking collectives: none -> 73.8 us  [the longest x3 37.8 us: body(): sums = lax.all_to_all(sums, CENTS, 0, 0, tiled=True)]
    psum x1 -> x0, waiting for transfers between devices: 70.6 us -> none  [body(): lax.psum(partial_value.astype(jnp.bfloat16), 'rows').astype(jnp.float32)]
    all_gather x1 -> x0, waiting for transfers between devices: 51.2 us -> none  [body(): group = lax.all_gather(vectors, 'cents', axis=0, tiled=True)]
    pallas_call x0 -> x14, Pallas kernels: none -> 45.8 us  [the longest x5 15.4 us: slice_sum(): pl.pallas_call(lambda *refs: sum_kernel(first, count, turn, share, planes...]
    ppermute x0 -> x16, waiting for transfers between devices: none -> 29.3 us  [move(): return lax.ppermute(x, axis, [(i, (i + by) % n) for i in range(n)])]
    ppermute x0 -> x16, starting transfers between devices: none -> 25 us  [move(): return lax.ppermute(x, axis, [(i, (i + by) % n) for i in range(n)])]
  transfers between devices with their start and end apart: 2 -> 16, of which waited for: 2 -> 8; matrix products, arithmetic and copies ran while one was open for 2% -> 0% of each run, Pallas kernels for 0% -> 11%
where the time goes in v1:
time: 179 us; the launch traced here: 178 us
  blocking collectives  73.8 us (41%)
  Pallas kernels  45.8 us (26%)
  waiting for transfers between devices  29.3 us (16%)
  starting transfers between devices  25 us (14%)
  local copies, waits for them, and re-layouts  3.35 us (2%)
    all_to_all x3, blocking collectives, body(): sums = lax.all_to_all(sums, CENTS, 0, 0, tiled=True)  37.8 us
    all_to_all x1, blocking collectives, body(): lax.all_to_all(copies, ('x', 'z'), 0, 0, tiled=True)  36 us
    ppermute x16, waiting for transfers between devices, move(): return lax.ppermute(x, axis, [(i, (i + by) % n) for i in range(n)])  29.3 us
    ppermute x16, starting transfers between devices, move(): return lax.ppermute(x, axis, [(i, (i + by) % n) for i in range(n)])  25 us
    pallas_call x5, Pallas kernels, slice_sum(): pl.pallas_call(lambda *refs: sum_kernel(first, count, turn, share, planes...  15.4 us
    pallas_call x2, Pallas kernels, weigh(): pl.pallas_call(weigh_kernel, in_specs=[VM, VM], out_specs=[VM, VM], out_s...  11.1 us
    pallas_call x1, Pallas kernels, make_plan(): pl.pallas_call(lambda *refs: plan_kernel(share, *refs), in_specs=[SM] + [...  8.31 us
    pallas_call x3, Pallas kernels, row_pass(): pl.pallas_call(lambda *refs: row_kernel(target, *refs), in_specs=[SM] + [...  5.42 us
  transfers between devices with their start and end apart: 16, of which 8 were waited for; matrix products, arithmetic and copies ran while one was open for 0% of the time, Pallas kernels for 11%

profile of v1, /device:TPU:0, one launch (start us, length us, event | category | flops | bytes accessed | tf_op | source)
XLA Modules:
  0.0 178.2 jit_solution(5551185473746827015)
XLA Ops:
  0.6 1.2 broadcast_in_dim.2
  1.8 36.0 %all_to_all.20 = bf16[16,64,1024]{2,1,0:T(8,128)(2,1)S(1)} all-to-all(bf16[16,64,1024]{2,1,0:T(8,128)(2,1)S(1)} %broadcast_in_dim.2), channel_id=1, replica_groups=mesh['y'=4,'x'=4,'z'=4,'core'=2] {'x','z'}, dimensions={0} | all-to-all | bytes 4194304 | tf_op jit(solution)/shard_map/all_to_all | solution.py:314
  37.8 0.0 collective-permute-start
  37.8 0.0 copy-start
  37.8 2.2 %copy-done = bf16[2048,1024]{1,0:T(8,128)(2,1)S(1)} copy-done((bf16[2048,1024]{1,0:T(8,128)(2,1)S(1)}, bf16[2048,1024]{1,0:T(8,128)(2,1)}, u32[]{:S(2)}) %copy-start) | copy-done | bytes 4194328
  40.0 0.0 copy-start.1
  40.0 4.7 %weigh.2 = (f32[2048,1024]{1,0:T(8,128)S(1)}, f32[16,128]{1,0:T(8,128)S(1)}) custom-call(bf16[2048,1024]{1,0:T(8,128)(2,1)S(1)} %copy-done, bf16[1024,1024]{1,0:T(8,128)(2,1)S(1)} %bitcast.6), custom_call_target="tpu_custom_call" | custom-call | flops 4294967296 | bytes 6291456 | tf_op jit(solution)/shard_map/weigh/pallas_call | solution.py:62
  44.7 0.0 collective-permute-done.vecs_ref.refs_6_.refs_3_
  44.7 0.0 copy-done.1
  44.7 6.3 %weigh.3 = (f32[2048,1024]{1,0:T(8,128)S(1)}, f32[16,128]{1,0:T(8,128)S(1)}) custom-call(bf16[2048,1024]{1,0:T(8,128)(2,1)S(1)} %copy-done.1, bf16[1024,1024]{1,0:T(8,128)(2,1)} %collective-permute-done.vecs_ref.refs_6_.refs_3_), custom_call_target="tpu_custom_call" | custom-call | flops 4294967296 | bytes 6291456 | tf_op jit(solution)/shard_map/weigh/pallas_call | solution.py:62
  51.1 3.1 %collective-permute-start.3 = (f32[16,128]{1,0:T(8,128)S(1)}, f32[16,128]{1,0:T(8,128)S(1)}, u32[]{:S(2)}, u32[]{:S(2)}) collective-permute-start(f32[16,128]{1,0:T(8,128)S(1)} %add.7.refs_3_), channel_id=1, source_target_pairs={{0,96},{32,0},{64,32},{96,64},{1,97},{33,1},{65,33},{97,65},{2,98}... | collective-permute-start | bytes 24584 | tf_op jit(solution)/shard_map/ppermute | solution.py:296
  54.2 0.0 collective-permute-start.2
  54.2 2.2 %collective-permute-start.1 = (f32[16,128]{1,0:T(8,128)S(1)}, f32[16,128]{1,0:T(8,128)S(1)}, u32[]{:S(2)}, u32[]{:S(2)}) collective-permute-start(f32[16,128]{1,0:T(8,128)S(1)} %add.7.refs_3_), channel_id=1, source_target_pairs={{0,64},{32,96},{64,0},{96,32},{1,65},{33,97},{65,1},{97,33},{2,66}... | collective-permute-start | bytes 24584 | tf_op jit(solution)/shard_map/ppermute | solution.py:296
  56.4 0.1 pad_add_fusion.refs_0_.core_ref
  56.5 0.0 collective-permute-done.3.refs_6_
  56.5 2.6 %collective-permute-done.2.refs_5_ = f32[16,128]{1,0:T(8,128)S(1)} collective-permute-done((f32[16,128]{1,0:T(8,128)S(1)}, f32[16,128]{1,0:T(8,128)S(1)}, u32[]{:S(2)}, u32[]{:S(2)}) %collective-permute-start.2) | collective-permute-done | bytes 8224 | tf_op jit(solution)/shard_map/ppermute | solution.py:296
  59.0 0.3 collective-permute-done.1.refs_4_
  59.3 1.8 %row_pass.3 = (f32[32,16,128]{2,1,0:T(8,128)S(1)}, f32[16,128]{1,0:T(8,128)}) custom-call(s32[3]{0:T(128)S(1)} %pad_add_fusion.refs_0_.core_ref, f32[2048,1024]{1,0:T(8,128)S(1)} %get-tuple-element.19.refs_1_.w0_ref, f32[2048,1024]{1,0:T(8,128)S(1)} %get-tuple-element.20.refs_2_.w1_ref, f32[16,128]{1,0:T(8,128)S(1)} %add.7.refs_3_, ...), custom_call_target="tpu_custom_call" | custom-call | tf_op jit(solution)/shard_map/row_pass/pallas_call | solution.py:98
  61.1 12.9 %all_to_all.21.sums_ref = f32[32,16,128]{2,1,0:T(8,128)S(1)} all-to-all(f32[32,16,128]{2,1,0:T(8,128)S(1)} %get-tuple-element.23), channel_id=1, replica_groups=mesh['y'=4,'x'=4,'z'=4,'core'=2] {'x','z','core'}, dimensions={0} | all-to-all | bytes 524288 | tf_op jit(solution)/shard_map/all_to_all | solution.py:324
  74.0 1.7 col_pass.2.refs_3_
  75.8 3.3 %collective-permute-start.6 = (f32[16,128]{1,0:T(8,128)S(1)}, f32[16,128]{1,0:T(8,128)S(1)}, u32[]{:S(2)}, u32[]{:S(2)}) collective-permute-start(f32[16,128]{1,0:T(8,128)S(1)} %col_pass.2.refs_3_), channel_id=1, source_target_pairs={{0,96},{32,0},{64,32},{96,64},{1,97},{33,1},{65,33},{97,65},{2,98}... | collective-permute-start | bytes 24584 | tf_op jit(solution)/shard_map/ppermute | solution.py:296
  79.1 0.0 collective-permute-start.5
  79.1 1.5 collective-permute-start.4
  80.6 0.0 collective-permute-done.6.refs_6_
  80.6 3.3 %collective-permute-done.5.refs_5_ = f32[16,128]{1,0:T(8,128)S(1)} collective-permute-done((f32[16,128]{1,0:T(8,128)S(1)}, f32[16,128]{1,0:T(8,128)S(1)}, u32[]{:S(2)}, u32[]{:S(2)}) %collective-permute-start.5) | collective-permute-done | bytes 8224 | tf_op jit(solution)/shard_map/ppermute | solution.py:296
  83.9 0.3 collective-permute-done.4.refs_4_
  84.2 1.8 %row_pass.4 = (f32[32,16,128]{2,1,0:T(8,128)S(1)}, f32[16,128]{1,0:T(8,128)}) custom-call(s32[3]{0:T(128)S(1)} %pad_add_fusion.refs_0_.core_ref, f32[2048,1024]{1,0:T(8,128)S(1)} %get-tuple-element.19.refs_1_.w0_ref, f32[2048,1024]{1,0:T(8,128)S(1)} %get-tuple-element.20.refs_2_.w1_ref, f32[16,128]{1,0:T(8,128)S(1)} %col_pass.2.refs_3_, ...), custom_call_target="tpu_custom_call" | custom-call | tf_op jit(solution)/shard_map/row_pass/pallas_call | solution.py:98
  86.1 12.5 %all_to_all.22.sums_ref = f32[32,16,128]{2,1,0:T(8,128)S(1)} all-to-all(f32[32,16,128]{2,1,0:T(8,128)S(1)} %get-tuple-element.24), channel_id=1, replica_groups=mesh['y'=4,'x'=4,'z'=4,'core'=2] {'x','z','core'}, dimensions={0} | all-to-all | bytes 524288 | tf_op jit(solution)/shard_map/all_to_all | solution.py:324
  98.5 1.7 col_pass.3.refs_3_
  100.3 3.3 %collective-permute-start.9 = (f32[16,128]{1,0:T(8,128)S(1)}, f32[16,128]{1,0:T(8,128)S(1)}, u32[]{:S(2)}, u32[]{:S(2)}) collective-permute-start(f32[16,128]{1,0:T(8,128)S(1)} %col_pass.3.refs_3_), channel_id=1, source_target_pairs={{0,96},{32,0},{64,32},{96,64},{1,97},{33,1},{65,33},{97,65},{2,98}... | collective-permute-start | bytes 24584 | tf_op jit(solution)/shard_map/ppermute | solution.py:296
  103.6 0.0 collective-permute-start.8
  103.6 1.5 collective-permute-start.7
  105.1 0.0 collective-permute-done.9.refs_6_
  105.1 3.3 %collective-permute-done.8.refs_5_ = f32[16,128]{1,0:T(8,128)S(1)} collective-permute-done((f32[16,128]{1,0:T(8,128)S(1)}, f32[16,128]{1,0:T(8,128)S(1)}, u32[]{:S(2)}, u32[]{:S(2)}) %collective-permute-start.8) | collective-permute-done | bytes 8224 | tf_op jit(solution)/shard_map/ppermute | solution.py:296
  108.4 0.3 collective-permute-done.7.refs_4_
  108.7 1.8 %row_pass.5 = (f32[32,16,128]{2,1,0:T(8,128)S(1)}, f32[16,128]{1,0:T(8,128)S(1)}) custom-call(s32[3]{0:T(128)S(1)} %pad_add_fusion.refs_0_.core_ref, f32[2048,1024]{1,0:T(8,128)S(1)} %get-tuple-element.19.refs_1_.w0_ref, f32[2048,1024]{1,0:T(8,128)S(1)} %get-tuple-element.20.refs_2_.w1_ref, f32[16,128]{1,0:T(8,128)S(1)} %col_pass.3.refs_3_, ...), custom_call_target="tpu_custom_call" | custom-call | tf_op jit(solution)/shard_map/row_pass/pallas_call | solution.py:98
  110.5 12.5 %all_to_all.23.refs_3_ = f32[32,16,128]{2,1,0:T(8,128)S(1)} all-to-all(f32[32,16,128]{2,1,0:T(8,128)S(1)} %get-tuple-element.25), channel_id=1, replica_groups=mesh['y'=4,'x'=4,'z'=4,'core'=2] {'x','z','core'}, dimensions={0} | all-to-all | bytes 524288 | tf_op jit(solution)/shard_map/all_to_all | solution.py:324
  123.0 8.3 %make_plan.1 = (bf16[2048,2048]{1,0:T(8,128)(2,1)S(1)}, f32[16,128]{1,0:T(8,128)S(1)}, bf16[1056,256]{1,0:T(8,128)(2,1)S(1)}, bf16[1056,256]{1,0:T(8,128)(2,1)S(1)}) custom-call(s32[3]{0:T(128)S(1)} %pad_add_fusion.refs_0_.core_ref, f32[2048,1024]{1,0:T(8,128)S(1)} %get-tuple-element.19.refs_1_.w0_ref, f32[2048,1024]{1,0:T(8,128)S(1)} %get-tuple-element.20.refs_2_.w1_ref, ...), custom_call_target="tpu_custom_call" | custom-call | tf_op jit(solution)/shard_map/make_plan/pallas_call | solution.py:214
  131.3 0.6 collective-permute-start.10
  131.9 3.0 %collective-permute-start.11 = (bf16[1056,256]{1,0:T(8,128)(2,1)S(1)}, bf16[1056,256]{1,0:T(8,128)(2,1)S(1)}, u32[]{:S(2)}, u32[]{:S(2)}) collective-permute-start(bf16[1056,256]{1,0:T(8,128)(2,1)S(1)} %get-tuple-element.29), channel_id=1, source_target_pairs={{0,96},{32,0},{64,32},{96,64},{1,97},{33,1},{65,33},{97,65},{2,98}... | collective-permute-start | bytes 1622024 | tf_op jit(solution)/shard_map/ppermute | solution.py:296
  134.9 2.9 %slice_sum.7 = bf16[1024,256]{1,0:T(8,128)(2,1)S(1)} custom-call(s32[3]{0:T(128)S(1)} %pad_add_fusion.refs_0_.core_ref, bf16[2048,2048]{1,0:T(8,128)(2,1)S(1)} %get-tuple-element.27.refs_1_, bf16[1024,1024]{1,0:T(8,128)(2,1)S(1)} %bitcast.8, bf16[1024,1024]{1,0:T(8,128)(2,1)} %collective-permute-done.vecs_ref.refs_6_.refs_3_), custom_call_target="tpu_custom_call" | custom-call | flops 1073741824 | bytes 2097152 | tf_op jit(solution)/shard_map/slice_sum/pallas_call | solution.py:246
  137.7 0.1 collective-permute-start.13
  137.8 4.0 %slice_sum.5.refs_2_ = f32[2048,256]{1,0:T(8,128)S(1)} custom-call(s32[3]{0:T(128)S(1)} %pad_add_fusion.refs_0_.core_ref, bf16[2048,2048]{1,0:T(8,128)(2,1)S(1)} %get-tuple-element.27.refs_1_, bf16[1024,1024]{1,0:T(8,128)(2,1)S(1)} %bitcast.9, bf16[1024,1024]{1,0:T(8,128)(2,1)} %collective-permute-done.vecs_ref.refs_6_.refs_3_), custom_call_target="tpu_custom_call" | custom-call | flops 2147483648 | bytes 3145728 | tf_op jit(solution)/shard_map/slice_sum/pallas_call | solution.py:246
  141.8 5.9 %collective-permute-done.10.refs_4_.refs_5_ = bf16[1056,256]{1,0:T(8,128)(2,1)S(1)} collective-permute-done((bf16[1056,256]{1,0:T(8,128)(2,1)S(1)}, bf16[1056,256]{1,0:T(8,128)(2,1)S(1)}, u32[]{:S(2)}, u32[]{:S(2)}) %collective-permute-start.10) | collective-permute-done | bytes 540704 | tf_op jit(solution)/shard_map/ppermute | solution.py:296
  147.7 0.0 collective-permute-done.11.refs_4_.refs_6_
  147.7 2.9 %slice_sum.9 = bf16[1056,256]{1,0:T(8,128)(2,1)S(1)} custom-call(s32[3]{0:T(128)S(1)} %pad_add_fusion.refs_0_.core_ref, bf16[2048,2048]{1,0:T(8,128)(2,1)S(1)} %get-tuple-element.27.refs_1_, bf16[1024,1024]{1,0:T(8,128)(2,1)S(1)} %bitcast.10, bf16[1024,1024]{1,0:T(8,128)(2,1)} %collective-permute-done.vecs_ref.refs_6_.refs_3_, ...), custom_call_target="tpu_custom_call" | custom-call | flops 1073741824 | bytes 2097152 | tf_op jit(solution)/shard_map/slice_sum/pallas_call | solution.py:246
  150.5 3.0 %collective-permute-start.15 = (bf16[1056,256]{1,0:T(8,128)(2,1)S(1)}, bf16[1056,256]{1,0:T(8,128)(2,1)S(1)}, u32[]{:S(2)}, u32[]{:S(2)}) collective-permute-start(bf16[1056,256]{1,0:T(8,128)(2,1)S(1)} %slice_sum.9), channel_id=1, source_target_pairs={{0,96},{32,0},{64,32},{96,64},{1,97},{33,1},{65,33},{97,65},{2,98}... | collective-permute-start | bytes 1622024 | tf_op jit(solution)/shard_map/ppermute | solution.py:296
  153.5 2.9 %slice_sum.6 = bf16[1056,256]{1,0:T(8,128)(2,1)S(1)} custom-call(s32[3]{0:T(128)S(1)} %pad_add_fusion.refs_0_.core_ref, bf16[2048,2048]{1,0:T(8,128)(2,1)S(1)} %get-tuple-element.27.refs_1_, bf16[1024,1024]{1,0:T(8,128)(2,1)S(1)} %bitcast.11, bf16[1024,1024]{1,0:T(8,128)(2,1)} %collective-permute-done.vecs_ref.refs_6_.refs_3_, ...), custom_call_target="tpu_custom_call" | custom-call | flops 1073741824 | bytes 2097152 | tf_op jit(solution)/shard_map/slice_sum/pallas_call | solution.py:246
  156.4 0.1 collective-permute-start.12
  156.5 2.9 %slice_sum.8 = bf16[1024,256]{1,0:T(8,128)(2,1)S(1)} custom-call(s32[3]{0:T(128)S(1)} %pad_add_fusion.refs_0_.core_ref, bf16[2048,2048]{1,0:T(8,128)(2,1)S(1)} %get-tuple-element.27.refs_1_, bf16[1024,1024]{1,0:T(8,128)(2,1)S(1)} %bitcast.12, bf16[1024,1024]{1,0:T(8,128)(2,1)} %collective-permute-done.vecs_ref.refs_6_.refs_3_), custom_call_target="tpu_custom_call" | custom-call | flops 1073741824 | bytes 2097152 | tf_op jit(solution)/shard_map/slice_sum/pallas_call | solution.py:246
  159.3 3.3 %collective-permute-start.14 = (bf16[1024,256]{1,0:T(8,128)(2,1)S(1)}, bf16[1024,256]{1,0:T(8,128)(2,1)S(1)}, u32[]{:S(2)}, u32[]{:S(2)}) collective-permute-start(bf16[1024,256]{1,0:T(8,128)(2,1)S(1)} %slice_sum.8), channel_id=1, source_target_pairs={{0,96},{32,0},{64,32},{96,64},{1,97},{33,1},{65,33},{97,65},{2,98}... | collective-permute-start | bytes 1572872 | tf_op jit(solution)/shard_map/ppermute | solution.py:296
  162.6 0.0 collective-permute-done.13.refs_8_
  162.6 13.4 %collective-permute-done.14.refs_9_ = bf16[1024,256]{1,0:T(8,128)(2,1)S(1)} collective-permute-done((bf16[1024,256]{1,0:T(8,128)(2,1)S(1)}, bf16[1024,256]{1,0:T(8,128)(2,1)S(1)}, u32[]{:S(2)}, u32[]{:S(2)}) %collective-permute-start.14) | collective-permute-done | bytes 524320 | tf_op jit(solution)/shard_map/ppermute | solution.py:296
  176.0 0.0 collective-permute-done.15.refs_10_
  176.0 0.0 collective-permute-done.12.refs_7_
  176.0 2.2 %finish.1 = (bf16[2048,256]{1,0:T(8,128)(2,1)}, f32[16,128]{1,0:T(8,128)}) custom-call(s32[3]{0:T(128)S(1)} %pad_add_fusion.refs_0_.core_ref, bf16[2048,1024]{1,0:T(8,128)(2,1)S(1)} %copy-done.1, f32[2048,256]{1,0:T(8,128)S(1)} %slice_sum.5.refs_2_, f32[16,128]{1,0:T(8,128)S(1)} %get-tuple-element.26.refs_4_.refs_3_, ...), custom_call_target="tpu_custom_call" | custom-call | tf_op jit(solution)/shard_map/finish/pallas_call | solution.py:277
  (1 shorter events, 0.0 us)
Async XLA Ops:
  37.8 6.9 %collective-permute-start = (bf16[1024,1024]{1,0:T(8,128)(2,1)S(1)}, bf16[1024,1024]{1,0:T(8,128)(2,1)}, u32[]{:S(2)}, u32[]{:S(2)}) collective-permute-start(bf16[1024,1024]{1,0:T(8,128)(2,1)S(1)} %bitcast.5), channel_id=1, source_target_pairs={{0,1},{1,0},{2,3},{3,2},{4,5},{5,4},{6,7},{7,6},{8,9},{9,8},{10,11... | collective-permute-start | bytes 6291464 | tf_op jit(solution)/shard_map/ppermute | solution.py:296
  37.8 2.2 %copy-start = (bf16[2048,1024]{1,0:T(8,128)(2,1)S(1)}, bf16[2048,1024]{1,0:T(8,128)(2,1)}, u32[]{:S(2)}) copy-start(bf16[2048,1024]{1,0:T(8,128)(2,1)} %refs_1_.1) | copy-start | bytes 12582916
  40.0 4.7 %copy-start.1 = (bf16[2048,1024]{1,0:T(8,128)(2,1)S(1)}, bf16[2048,1024]{1,0:T(8,128)(2,1)}, u32[]{:S(2)}) copy-start(bf16[2048,1024]{1,0:T(8,128)(2,1)} %refs_1_.1) | copy-start | bytes 12582916
  51.1 5.4 %collective-permute-start.3 = (f32[16,128]{1,0:T(8,128)S(1)}, f32[16,128]{1,0:T(8,128)S(1)}, u32[]{:S(2)}, u32[]{:S(2)}) collective-permute-start(f32[16,128]{1,0:T(8,128)S(1)} %add.7.refs_3_), channel_id=1, source_target_pairs={{0,96},{32,0},{64,32},{96,64},{1,97},{33,1},{65,33},{97,65},{2,98}... | collective-permute-start | bytes 24584 | tf_op jit(solution)/shard_map/ppermute | solution.py:296
  54.2 4.9 %collective-permute-start.2 = (f32[16,128]{1,0:T(8,128)S(1)}, f32[16,128]{1,0:T(8,128)S(1)}, u32[]{:S(2)}, u32[]{:S(2)}) collective-permute-start(f32[16,128]{1,0:T(8,128)S(1)} %add.7.refs_3_), channel_id=1, source_target_pairs={{0,32},{32,64},{64,96},{96,0},{1,33},{33,65},{65,97},{97,1},{2,34}... | collective-permute-start | bytes 24584 | tf_op jit(solution)/shard_map/ppermute | solution.py:296
  54.2 5.2 %collective-permute-start.1 = (f32[16,128]{1,0:T(8,128)S(1)}, f32[16,128]{1,0:T(8,128)S(1)}, u32[]{:S(2)}, u32[]{:S(2)}) collective-permute-start(f32[16,128]{1,0:T(8,128)S(1)} %add.7.refs_3_), channel_id=1, source_target_pairs={{0,64},{32,96},{64,0},{96,32},{1,65},{33,97},{65,1},{97,33},{2,66}... | collective-permute-start | bytes 24584 | tf_op jit(solution)/shard_map/ppermute | solution.py:296
  75.8 4.9 %collective-permute-start.6 = (f32[16,128]{1,0:T(8,128)S(1)}, f32[16,128]{1,0:T(8,128)S(1)}, u32[]{:S(2)}, u32[]{:S(2)}) collective-permute-start(f32[16,128]{1,0:T(8,128)S(1)} %col_pass.2.refs_3_), channel_id=1, source_target_pairs={{0,96},{32,0},{64,32},{96,64},{1,97},{33,1},{65,33},{97,65},{2,98}... | collective-permute-start | bytes 24584 | tf_op jit(solution)/shard_map/ppermute | solution.py:296
  79.1 4.9 %collective-permute-start.5 = (f32[16,128]{1,0:T(8,128)S(1)}, f32[16,128]{1,0:T(8,128)S(1)}, u32[]{:S(2)}, u32[]{:S(2)}) collective-permute-start(f32[16,128]{1,0:T(8,128)S(1)} %col_pass.2.refs_3_), channel_id=1, source_target_pairs={{0,32},{32,64},{64,96},{96,0},{1,33},{33,65},{65,97},{97,1},{2,34}... | collective-permute-start | bytes 24584 | tf_op jit(solution)/shard_map/ppermute | solution.py:296
  79.1 5.2 %collective-permute-start.4 = (f32[16,128]{1,0:T(8,128)S(1)}, f32[16,128]{1,0:T(8,128)S(1)}, u32[]{:S(2)}, u32[]{:S(2)}) collective-permute-start(f32[16,128]{1,0:T(8,128)S(1)} %col_pass.2.refs_3_), channel_id=1, source_target_pairs={{0,64},{32,96},{64,0},{96,32},{1,65},{33,97},{65,1},{97,33},{2,66}... | collective-permute-start | bytes 24584 | tf_op jit(solution)/shard_map/ppermute | solution.py:296
  100.3 4.9 %collective-permute-start.9 = (f32[16,128]{1,0:T(8,128)S(1)}, f32[16,128]{1,0:T(8,128)S(1)}, u32[]{:S(2)}, u32[]{:S(2)}) collective-permute-start(f32[16,128]{1,0:T(8,128)S(1)} %col_pass.3.refs_3_), channel_id=1, source_target_pairs={{0,96},{32,0},{64,32},{96,64},{1,97},{33,1},{65,33},{97,65},{2,98}... | collective-permute-start | bytes 24584 | tf_op jit(solution)/shard_map/ppermute | solution.py:296
  103.6 4.9 %collective-permute-start.8 = (f32[16,128]{1,0:T(8,128)S(1)}, f32[16,128]{1,0:T(8,128)S(1)}, u32[]{:S(2)}, u32[]{:S(2)}) collective-permute-start(f32[16,128]{1,0:T(8,128)S(1)} %col_pass.3.refs_3_), channel_id=1, source_target_pairs={{0,32},{32,64},{64,96},{96,0},{1,33},{33,65},{65,97},{97,1},{2,34}... | collective-permute-start | bytes 24584 | tf_op jit(solution)/shard_map/ppermute | solution.py:296
  103.6 5.2 %collective-permute-start.7 = (f32[16,128]{1,0:T(8,128)S(1)}, f32[16,128]{1,0:T(8,128)S(1)}, u32[]{:S(2)}, u32[]{:S(2)}) collective-permute-start(f32[16,128]{1,0:T(8,128)S(1)} %col_pass.3.refs_3_), channel_id=1, source_target_pairs={{0,64},{32,96},{64,0},{96,32},{1,65},{33,97},{65,1},{97,33},{2,66}... | collective-permute-start | bytes 24584 | tf_op jit(solution)/shard_map/ppermute | solution.py:296
  131.3 16.3 %collective-permute-start.10 = (bf16[1056,256]{1,0:T(8,128)(2,1)S(1)}, bf16[1056,256]{1,0:T(8,128)(2,1)S(1)}, u32[]{:S(2)}, u32[]{:S(2)}) collective-permute-start(bf16[1056,256]{1,0:T(8,128)(2,1)S(1)} %get-tuple-element.28), channel_id=1, source_target_pairs={{0,32},{32,64},{64,96},{96,0},{1,33},{33,65},{65,97},{97,1},{2,34}... | collective-permute-start | bytes 1622024 | tf_op jit(solution)/shard_map/ppermute | solution.py:296
  131.9 15.8 %collective-permute-start.11 = (bf16[1056,256]{1,0:T(8,128)(2,1)S(1)}, bf16[1056,256]{1,0:T(8,128)(2,1)S(1)}, u32[]{:S(2)}, u32[]{:S(2)}) collective-permute-start(bf16[1056,256]{1,0:T(8,128)(2,1)S(1)} %get-tuple-element.29), channel_id=1, source_target_pairs={{0,96},{32,0},{64,32},{96,64},{1,97},{33,1},{65,33},{97,65},{2,98}... | collective-permute-start | bytes 1622024 | tf_op jit(solution)/shard_map/ppermute | solution.py:296
  137.7 24.9 %collective-permute-start.13 = (bf16[1024,256]{1,0:T(8,128)(2,1)S(1)}, bf16[1024,256]{1,0:T(8,128)(2,1)S(1)}, u32[]{:S(2)}, u32[]{:S(2)}) collective-permute-start(bf16[1024,256]{1,0:T(8,128)(2,1)S(1)} %slice_sum.7), channel_id=1, source_target_pairs={{0,32},{32,64},{64,96},{96,0},{1,33},{33,65},{65,97},{97,1},{2,34}... | collective-permute-start | bytes 1572872 | tf_op jit(solution)/shard_map/ppermute | solution.py:296
  150.5 25.5 %collective-permute-start.15 = (bf16[1056,256]{1,0:T(8,128)(2,1)S(1)}, bf16[1056,256]{1,0:T(8,128)(2,1)S(1)}, u32[]{:S(2)}, u32[]{:S(2)}) collective-permute-start(bf16[1056,256]{1,0:T(8,128)(2,1)S(1)} %slice_sum.9), channel_id=1, source_target_pairs={{0,96},{32,0},{64,32},{96,64},{1,97},{33,1},{65,33},{97,65},{2,98}... | collective-permute-start | bytes 1622024 | tf_op jit(solution)/shard_map/ppermute | solution.py:296
  156.4 19.6 %collective-permute-start.12 = (bf16[1056,256]{1,0:T(8,128)(2,1)S(1)}, bf16[1056,256]{1,0:T(8,128)(2,1)S(1)}, u32[]{:S(2)}, u32[]{:S(2)}) collective-permute-start(bf16[1056,256]{1,0:T(8,128)(2,1)S(1)} %slice_sum.6), channel_id=1, source_target_pairs={{0,32},{32,64},{64,96},{96,0},{1,33},{33,65},{65,97},{97,1},{2,34}... | collective-permute-start | bytes 1622024 | tf_op jit(solution)/shard_map/ppermute | solution.py:296
  159.3 16.6 %collective-permute-start.14 = (bf16[1024,256]{1,0:T(8,128)(2,1)S(1)}, bf16[1024,256]{1,0:T(8,128)(2,1)S(1)}, u32[]{:S(2)}, u32[]{:S(2)}) collective-permute-start(bf16[1024,256]{1,0:T(8,128)(2,1)S(1)} %slice_sum.8), channel_id=1, source_target_pairs={{0,96},{32,0},{64,32},{96,64},{1,97},{33,1},{65,33},{97,65},{2,98}... | collective-permute-start | bytes 1572872 | tf_op jit(solution)/shard_map/ppermute | solution.py:296

commit v2 on v0

v2 whole, which is shorter than its diff:
```python
import functools

import jax
import jax.numpy as jnp
from jax import lax
from jax.experimental import pallas as pl
from jax.experimental.pallas import tpu as pltpu
from jax.sharding import Mesh, PartitionSpec as P

ROUNDS = 3
SHARP = 0.75
LOG2E = 1.4426950408889634
CENTS = ("x", "z", "core")
LANES = 128
TAIL = 16
PLACES = 4
LINES = 2
ORDER = ((True, 0), (False, 0), (True, 1), (True, 2), (True, 3), (False, 1), (False, 2), (False, 3))
FLOPS = 3 * 10**10
WEIGH_VMEM = 16 * 1024 * 1024
SUM_VMEM = 10 * 1024 * 1024

VM = pl.BlockSpec(memory_space=pltpu.VMEM)
SM = pl.BlockSpec(memory_space=pltpu.SMEM)


def params(vmem):
    return pltpu.CompilerParams(vmem_limit_bytes=vmem)


def held(x):
    return pltpu.with_memory_space_constraint(x, pltpu.VMEM)


def outside(x):
    return pltpu.with_memory_space_constraint(x, pltpu.HBM)


def row_of(block):
    return jnp.sum(block.T, axis=0, keepdims=True)


def down(row):
    return jnp.broadcast_to(row, (LANES, LANES)).T


def line_of(place_ref, mine, turn):
    core = place_ref[0]
    place, side = (place_ref[2], core) if mine else (place_ref[3], 1 - core)
    return pl.multiple_of((side * PLACES + lax.rem(place + PLACES - turn, PLACES)) * LINES, LINES)


def gather_kernel(place_ref, *refs):
    blocks, out = refs[:-1], refs[-1]
    size = blocks[0].shape[0]
    for turn, block in enumerate(blocks):
        at = lax.rem(place_ref[4] + PLACES - turn, PLACES) * size
        out[pl.ds(pl.multiple_of(at, size), size), :] = block[...]


def in_order(place, blocks):
    size, d = blocks[0].shape
    return pl.pallas_call(
        gather_kernel,
        in_specs=[SM] + [VM] * len(blocks),
        out_specs=VM,
        out_shape=jax.ShapeDtypeStruct((len(blocks) * size, d), blocks[0].dtype),
        compiler_params=params(8 * 1024 * 1024),
        name="in_order",
    )(place, *blocks)


def weigh_kernel(count, cuts, place_ref, cents_ref, *refs):
    blocks, every = refs[:count], refs[count : count + cuts * 2]
    w_ref, mass_ref, *outs = refs[count + cuts * 2 : count + cuts * 3 + 2]
    acc_ref, sem = refs[-2:]
    n = w_ref.shape[0]
    rows = 512
    copies = []
    for k, out in enumerate(outs):
        share = out.shape[1]
        part = pl.ds(pl.multiple_of(lax.rem(place_ref[1] + k, cuts) * share, share), share)
        for i, block in enumerate(every):
            size = block.shape[0]
            copies.append(
                pltpu.make_async_copy(block.at[:, part], out.at[pl.ds(i * size, size)], sem.at[len(copies)])
            )
    for copy in copies:
        copy.start()
    for k in range(0, n, rows):
        acc, at = None, 0
        for block in blocks:
            cols = block.shape[0]
            logits = lax.dot_general(
                cents_ref[k : k + rows, :], block[...], (((1,), (1,)), ((), ())), preferred_element_type=jnp.float32
            )
            w = jnp.exp2(logits * (SHARP * LOG2E))
            w_ref[k : k + rows, at : at + cols] = w
            at += cols
            for j in range(0, cols, LANES):
                acc = w[:, j : j + LANES] if acc is None else acc + w[:, j : j + LANES]
        acc_ref[k : k + rows, :] = acc
    for g in range(n // LANES):
        mass_ref[g : g + 1, :] = row_of(acc_ref[g * LANES : (g + 1) * LANES, :])
    for copy in copies:
        copy.wait()


def weigh(place, cents, blocks, cuts=0, every=()):
    n, d = cents.shape
    m = sum(block.shape[0] for block in blocks)
    total = sum(block.shape[0] for block in every)
    return pl.pallas_call(
        functools.partial(weigh_kernel, len(blocks), cuts),
        in_specs=[SM, VM] + [VM] * len(blocks) + [pl.BlockSpec(memory_space=pl.ANY)] * len(every),
        out_specs=[VM] * (2 + cuts),
        out_shape=[pltpu.VMEM((n, m), jnp.float32), jax.ShapeDtypeStruct((n // LANES, LANES), jnp.float32)]
        + [pltpu.VMEM((total, d // cuts), cents.dtype) for _ in range(cuts)],
        scratch_shapes=[
            pltpu.VMEM((n, LANES), jnp.float32),
            pltpu.SemaphoreType.DMA((max(len(every) * cuts, 1),)),
        ],
        compiler_params=params(WEIGH_VMEM),
        cost_estimate=pl.CostEstimate(flops=FLOPS, bytes_accessed=0, transcendentals=0),
        name="weigh",
    )(place, held(cents), *[held(block) for block in blocks], *every)


def tiles_of(w_refs):
    return [(ref, t) for ref in w_refs for t in range(0, ref.shape[1], LANES)]


def row_kernel(target, place_ref, w0_ref, w1_ref, w2_ref, a_ref, b_ref, c_ref, d_ref, out_ref, scale_ref, lines_ref):
    scale_ref[...] = target / ((a_ref[...] + b_ref[...]) + (c_ref[...] + d_ref[...]))
    tiles = tiles_of((w0_ref, w1_ref, w2_ref))
    accs = [None] * len(tiles)
    for b in range(w0_ref.shape[0] // LANES):
        part = slice(b * LANES, (b + 1) * LANES)
        s = down(scale_ref[b : b + 1, :])
        for j, (ref, t) in enumerate(tiles):
            p = ref[part, t : t + LANES] * s
            p = jnp.sum(p.reshape(LANES // 8, 8, LANES), axis=0)
            accs[j] = p if b == 0 else accs[j] + p
    for block, (mine, turn) in enumerate(ORDER):
        pair = [jnp.sum(a, axis=0, keepdims=True) for a in accs[block * LINES : (block + 1) * LINES]]
        lines_ref[pl.ds(line_of(place_ref, mine, turn), LINES), :] = jnp.concatenate(pair, axis=0)
    value = lines_ref[...].astype(out_ref.dtype)
    for q in range(out_ref.shape[0]):
        out_ref[q] = value


def row_pass(target, place, w, masses, peers):
    n = w[0].shape[0]
    lines = len(ORDER) * LINES
    return pl.pallas_call(
        lambda *refs: row_kernel(target, *refs),
        in_specs=[SM] + [VM] * 7,
        out_specs=[VM, VM],
        out_shape=[
            jax.ShapeDtypeStruct((peers, lines, LANES), jnp.bfloat16),
            jax.ShapeDtypeStruct((n // LANES, LANES), jnp.float32),
        ],
        scratch_shapes=[pltpu.VMEM((lines, LANES), jnp.float32)],
        compiler_params=params(8 * 1024 * 1024),
        name="row_pass",
    )(place, *[held(x) for x in w], *masses)


def local_scale(place_ref, sums_ref, lines_ref):
    total = sums_ref[0].astype(jnp.float32)
    for q in range(1, sums_ref.shape[0]):
        total = total + sums_ref[q].astype(jnp.float32)
    lines_ref[...] = 1.0 / total
    scale = [lines_ref[pl.ds(line_of(place_ref, mine, turn), LINES), :] for mine, turn in ORDER]
    return [pair[i : i + 1, :] for pair in scale for i in range(LINES)]


def col_kernel(place_ref, w0_ref, w1_ref, w2_ref, sums_ref, out_ref, lines_ref):
    scale = local_scale(place_ref, sums_ref, lines_ref)
    tiles = tiles_of((w0_ref, w1_ref, w2_ref))
    for b in range(w0_ref.shape[0] // LANES):
        part = slice(b * LANES, (b + 1) * LANES)
        acc = None
        for j, (ref, t) in enumerate(tiles):
            p = ref[part, t : t + LANES] * scale[j]
            acc = p if acc is None else acc + p
        out_ref[b : b + 1, :] = row_of(acc)


def col_pass(place, w, sums):
    n = w[0].shape[0]
    return pl.pallas_call(
        col_kernel,
        in_specs=[SM] + [VM] * 4,
        out_specs=VM,
        out_shape=jax.ShapeDtypeStruct((n // LANES, LANES), jnp.float32),
        scratch_shapes=[pltpu.VMEM(sums.shape[1:], jnp.float32)],
        compiler_params=params(8 * 1024 * 1024),
        name="col_pass",
    )(place, *[held(x) for x in w], sums)


def split(x):
    hi = x.astype(jnp.bfloat16)
    rest = x - hi.astype(jnp.float32)
    mid = rest.astype(jnp.bfloat16)
    return hi, mid, (rest - mid.astype(jnp.float32)).astype(jnp.bfloat16)


def put_tail(ref, x):
    hi, mid, lo = split(x)
    tail = slice(ref.shape[0] - TAIL, ref.shape[0])
    ref[tail, :LANES] = jnp.concatenate([hi, mid], axis=0)
    ref[tail, LANES:] = jnp.concatenate([lo, jnp.zeros_like(lo)], axis=0)


def get_tail(ref):
    f32 = jnp.float32
    tail = slice(ref.shape[0] - TAIL, ref.shape[0])
    first, second = ref[tail, :LANES].astype(f32), ref[tail, LANES:].astype(f32)
    return (first[: TAIL // 2] + first[TAIL // 2 :]) + second[: TAIL // 2]


def product(plan, v_ref):
    return jnp.dot(plan, v_ref[...], preferred_element_type=jnp.float32)


def call(kernel, name, specs, out_shape, args, scratch=()):
    return pl.pallas_call(
        kernel,
        in_specs=specs,
        out_specs=[VM] * len(out_shape),
        out_shape=out_shape,
        scratch_shapes=list(scratch),
        compiler_params=params(SUM_VMEM),
        cost_estimate=pl.CostEstimate(flops=FLOPS, bytes_accessed=0, transcendentals=0),
        name=name,
    )(*args)


def plan_kernel(
    first, place_ref, w0_ref, w1_ref, w2_ref, sums_ref, scale_ref, mark_ref, u_ref, f_ref, d_ref, *refs
):
    plan_ref, mass_ref, up_ref, down_ref, lines_ref = refs
    scale = local_scale(place_ref, sums_ref, lines_ref)
    tiles = tiles_of((w0_ref, w1_ref, w2_ref))
    rows = 2 * LANES
    n = plan_ref.shape[0]
    half = n // 2
    for top in range(0, n, rows):
        for at in range(top, top + rows, LANES):
            part = slice(first + at, first + at + LANES)
            line = (first + at) // LANES
            s = down(scale_ref[line : line + 1, :])
            acc = None
            for j, (ref, t) in enumerate(tiles):
                p = ref[part, t : t + LANES] * scale[j]
                acc = p if acc is None else acc + p
                plan_ref[at : at + LANES, j * LANES : (j + 1) * LANES] = (p * s).astype(jnp.bfloat16)
            mass_ref[at // LANES : at // LANES + 1, :] = row_of(acc)
        here = plan_ref[top : top + rows, :]
        far, near, at, v_ref = (up_ref, down_ref, top, d_ref) if top < half else (down_ref, up_ref, top - half, u_ref)
        far[at : at + rows, :] = product(here, f_ref).astype(far.dtype)
        near[half + at : half + at + rows, :] = product(here, v_ref).astype(near.dtype)
    put_tail(up_ref, mass_ref[...])
    put_tail(down_ref, mass_ref[...])


def make_plan(place, w, sums, scale, cuts, first, mark):
    n = w[0].shape[0]
    m, share = cuts[0].shape
    part = jax.ShapeDtypeStruct((n // 2 + TAIL, share), jnp.bfloat16)
    return call(
        lambda *refs: plan_kernel(first, *refs),
        "make_plan",
        [SM] + [VM] * 9,
        [pltpu.VMEM((n // 2, m), jnp.bfloat16), jax.ShapeDtypeStruct((n // 2 // LANES, LANES), jnp.float32), part, part],
        (place, *[held(x) for x in w], sums, scale, mark, *[held(v) for v in cuts[1:]]),
        [pltpu.VMEM(sums.shape[1:], jnp.float32)],
    )


def late_kernel(plan_ref, from_below, from_above, u_ref, d_ref, up_ref, down_ref, mark_ref):
    half = plan_ref.shape[0] // 2
    f32 = jnp.float32
    up = product(plan_ref[:half, :], u_ref) + from_below[:half, :].astype(f32)
    up_ref[:half, :] = up.astype(up_ref.dtype)
    below = product(plan_ref[half:, :], d_ref) + from_above[:half, :].astype(f32)
    down_ref[:half, :] = below.astype(down_ref.dtype)
    up_ref[half:, :] = from_below[2 * half :, :]
    down_ref[half:, :] = from_above[2 * half :, :]
    mark_ref[...] = jnp.zeros_like(mark_ref)


def late_sums(plan, from_below, from_above, cuts):
    n = plan.shape[0]
    share = cuts[0].shape[1]
    out = jax.ShapeDtypeStruct((n // 2 + TAIL, share), jnp.bfloat16)
    mark = jax.ShapeDtypeStruct((8, LANES), jnp.float32)
    return call(
        late_kernel,
        "late_sums",
        [VM] * 5,
        [out, out, mark],
        (held(plan), from_below, from_above, held(cuts[1]), held(cuts[3])),
    )


def own_kernel(index, place_ref, plan_ref, from_below, from_above, v_ref, mark_ref, cents_ref, out_ref, block_ref, sem):
    n, share = out_ref.shape
    half = n // 2
    f32 = jnp.float32
    cols = pl.ds(pl.multiple_of(place_ref[1] * share, share), share)
    copy = pltpu.make_async_copy(cents_ref.at[pl.ds(index * n, n), cols], block_ref, sem)
    copy.start()
    out_ref[:half, :] = product(plan_ref[:half, :], v_ref) + from_above[half : 2 * half, :].astype(f32)
    out_ref[half:, :] = product(plan_ref[half:, :], v_ref) + from_below[half : 2 * half, :].astype(f32)
    copy.wait()


def own_sums(place, plan, from_below, from_above, cuts, mark, centroids, index):
    n, share = plan.shape[0], cuts[0].shape[1]
    return call(
        functools.partial(own_kernel, index),
        "own_sums",
        [SM] + [VM] * 5 + [pl.BlockSpec(memory_space=pltpu.HBM)],
        [pltpu.VMEM((n, share), jnp.float32), pltpu.VMEM((n, share), centroids.dtype)],
        (place, held(plan), from_below, from_above, held(cuts[0]), mark, outside(centroids)),
        [pltpu.SemaphoreType.DMA],
    )


def finish_kernel(index, place_ref, own_ref, scale_ref, m_ref, below, above, up_ref, down_ref, mark_ref, cents_ref, out_ref, mass_ref):
    lines = mass_ref.shape[0]
    scale = scale_ref[index * lines : (index + 1) * lines, :]
    mass_ref[...] = scale * ((m_ref[...] + get_tail(up_ref)) + (get_tail(below) + get_tail(above)))
    n, share = out_ref.shape
    half = n // 2
    f32 = jnp.float32
    for top in range(0, n, LANES):
        part = slice(top, top + LANES)
        line = top // LANES
        late, start = (up_ref, top) if top < half else (down_ref, top - half)
        sums = own_ref[part, :] + late[start : start + LANES, :].astype(f32)
        inverse = down(0.5 / mass_ref[line : line + 1, :])
        for j in range(0, share, LANES):
            value = 0.5 * cents_ref[part, j : j + LANES].astype(f32) + sums[:, j : j + LANES] * inverse
            out_ref[part, j : j + LANES] = value.astype(out_ref.dtype)


def finish(place, own, scale, mass, below, above, up, under, mark, index, whole=None):
    own, block = own
    n, share = own.shape
    lines = n // LANES
    specs = [VM] * 9
    args = [held(own), scale, mass, below, above, up, under, mark, held(block)]
    kernel = functools.partial(finish_kernel, index)
    if whole is not None:
        specs.append(pl.BlockSpec(memory_space=pl.ANY))
        args.append(whole)

        def kernel(*refs):
            finish_kernel(index, *refs[:10], *refs[11:])

    return pl.pallas_call(
        kernel,
        grid_spec=pltpu.PrefetchScalarGridSpec(
            num_scalar_prefetch=1,
            grid=(1,),
            in_specs=specs,
            out_specs=[pl.BlockSpec((n, share), lambda i, place: (index, 0)), VM],
        ),
        out_shape=[
            jax.ShapeDtypeStruct((2 * n, share), jnp.bfloat16),
            jax.ShapeDtypeStruct((lines, LANES), jnp.float32),
        ],
        input_output_aliases={} if whole is None else {10: 0},
        compiler_params=params(SUM_VMEM),
        cost_estimate=pl.CostEstimate(flops=FLOPS, bytes_accessed=0, transcendentals=0),
        name="finish",
    )(place, *args)


def move(x, axis, by):
    n = lax.axis_size(axis)
    return lax.ppermute(x, axis, [(i, (i + by) % n) for i in range(n)])


def spread(x, turn, first):
    if turn == 0:
        return x
    pairs = []
    for i in range(PLACES):
        for j in range(PLACES):
            for core in range(2):
                by_x = (core == 0) == first
                to = ((i + turn) % PLACES, j) if by_x else (i, (j + turn) % PLACES)
                pairs.append(((i * PLACES + j) * 2 + core, (to[0] * PLACES + to[1]) * 2 + core))
    return lax.ppermute(x, CENTS, pairs)


def row_peers(x):
    return x, move(x, "y", 2), move(x, "y", 1), move(x, "y", 3)


def body(vectors, centroids):
    planes = lax.axis_size("y")
    core, x, z, y = [lax.axis_index(name) for name in ("core", "x", "z", "y")]
    first = core == 0
    place = jnp.stack([core, y, jnp.where(first, z, x), jnp.where(first, x, z), jnp.where(first, x, z)])
    place = place.astype(jnp.int32)
    peers = PLACES * PLACES * lax.axis_size("core")
    n, d = centroids.shape
    target = vectors.shape[0] * planes * peers / (n * peers)

    near = in_order(place, [spread(vectors, turn, True) for turn in range(PLACES)])
    mine = [spread(near, turn, False) for turn in range(PLACES)]
    other = [move(mine[0], "core", 1)]
    w0, mass0 = weigh(place, centroids, (mine[0], other[0]))
    mass0, *mine[1:] = lax.optimization_barrier((mass0, *mine[1:]))
    other += [move(block, "core", 1) for block in mine[1:]]
    every = (mine[0], other[0], *mine[1:], *other[1:])
    w1, mass1 = weigh(place, centroids, mine[1:])
    w2, mass2, *cuts = weigh(place, centroids, other[1:], planes, every)
    w = (w0, w1, w2)

    colmass = mass0 + mass1 + mass2
    for step in range(ROUNDS):
        sums, scale = row_pass(target, place, w, row_peers(colmass), peers)
        sums = lax.all_to_all(sums, CENTS, 0, 0, tiled=True)
        if step < ROUNDS - 1:
            colmass = col_pass(place, w, sums)

    mark = jnp.zeros((8, LANES), jnp.float32)
    plan0, mass0, up0, down0 = make_plan(place, w, sums, scale, cuts, 0, mark)
    up0, down0 = move(up0, "y", 1), move(down0, "y", 3)
    plan1, mass1, up1, down1 = make_plan(place, w, sums, scale, cuts, n // 2, mass0)
    up1, down1 = move(up1, "y", 1), move(down1, "y", 3)
    late_up0, late_down0, mark0 = late_sums(plan0, up0, down0, cuts)
    late_up0, late_down0 = move(late_up0, "y", 1), move(late_down0, "y", 3)
    own0 = own_sums(place, plan0, up0, down0, cuts, mark0, centroids, 0)
    late_up1, late_down1, mark1 = late_sums(plan1, up1, down1, cuts)
    late_up1, late_down1 = move(late_up1, "y", 1), move(late_down1, "y", 3)
    own1 = own_sums(place, plan1, up1, down1, cuts, mark1, centroids, 1)
    half, masses0 = finish(place, own0, scale, mass0, up0, down0, late_up0, late_down0, mark1, 0)
    updated, masses1 = finish(
        place, own1, scale, mass1, up1, down1, late_up1, late_down1, mark1, 1, half
    )
    masses = jnp.concatenate([masses0, masses1], axis=0)
    return updated, masses.reshape(n)


def solution(mesh):
    sizes = (mesh.shape["rows"], 4, 4, 2)
    torus = Mesh(mesh.devices.reshape(sizes), ("y",) + CENTS)
    return jax.shard_map(
        body,
        mesh=torus,
        in_specs=(P(("y",) + CENTS, None), P(CENTS, None)),
        out_specs=(P(CENTS, "y"), P(CENTS)),
        check_vma=False,
    )
```

time: 500 us -> 152 us (0.30)
  blocking collectives: 228 us -> 36.5 us
  matrix products: 113 us -> 0 us
  waiting for transfers between devices: 123 us -> 30.2 us
  starting transfers between devices: 0.08 us -> 41.7 us
  Pallas kernels: 0 us -> 38.7 us
  between operations: 14.7 us -> 0.84 us
  other arithmetic: 11.3 us -> 0.61 us
    psum x7 -> x0, blocking collectives: 228 us -> none  [the longest x3 192 us: body(): lax.psum(jnp.dot(weights, col_scale, precision=lax.Precision.HIGHEST), 'c...]
    dot_general x8 -> x0, matrix products: 113 us -> none  [the longest x3 53.2 us: body(): jnp.dot(weights, col_scale, precision=lax.Precision.HIGHEST)]
    psum x1 -> x0, waiting for transfers between devices: 70.6 us -> none  [body(): lax.psum(partial_value.astype(jnp.bfloat16), 'rows').astype(jnp.float32)]
    all_gather x1 -> x0, waiting for transfers between devices: 51.2 us -> none  [body(): group = lax.all_gather(vectors, 'cents', axis=0, tiled=True)]
    ppermute x0 -> x27, starting transfers between devices: none -> 41.7 us  [the longest x21 29.3 us: move(): return lax.ppermute(x, axis, [(i, (i + by) % n) for i in range(n)])]
    pallas_call x0 -> x17, Pallas kernels: none -> 38.7 us  [the longest x6 13.7 us: call(): pl.pallas_call(kernel, in_specs=specs, out_specs=[VM] * len(out_shape), o...]
    all_to_all x0 -> x3, blocking collectives: none -> 36.5 us  [body(): sums = lax.all_to_all(sums, CENTS, 0, 0, tiled=True)]
    ppermute x0 -> x27, waiting for transfers between devices: none -> 30.2 us  [the longest x21 20 us: move(): return lax.ppermute(x, axis, [(i, (i + by) % n) for i in range(n)])]
  transfers between devices with their start and end apart: 2 -> 27, of which waited for: 2 -> 14; matrix products, arithmetic and copies ran while one was open for 2% -> 0% of each run, Pallas kernels for 0% -> 13%
where the time goes in v2:
time: 152 us
  starting transfers between devices  41.7 us (27%)
  Pallas kernels  38.7 us (25%)
  blocking collectives  36.5 us (24%)
  waiting for transfers between devices  30.2 us (20%)
  local copies, waits for them, and re-layouts  3.18 us (2%)
    all_to_all x3, blocking collectives, body(): sums = lax.all_to_all(sums, CENTS, 0, 0, tiled=True)  36.5 us
    ppermute x21, starting transfers between devices, move(): return lax.ppermute(x, axis, [(i, (i + by) % n) for i in range(n)])  29.3 us
    ppermute x21, waiting for transfers between devices, move(): return lax.ppermute(x, axis, [(i, (i + by) % n) for i in range(n)])  20 us
    pallas_call x6, Pallas kernels, call(): pl.pallas_call(kernel, in_specs=specs, out_specs=[VM] * len(out_shape), o...  13.7 us
    ppermute x6, starting transfers between devices, spread(): return lax.ppermute(x, CENTS, pairs)  12.4 us
    pallas_call x3, Pallas kernels, weigh(): pl.pallas_call(functools.partial(weigh_kernel, len(blocks), cuts), in_spe...  12.2 us
    ppermute x6, waiting for transfers between devices, spread(): return lax.ppermute(x, CENTS, pairs)  10.2 us
    pallas_call x3, Pallas kernels, row_pass(): pl.pallas_call(lambda *refs: row_kernel(target, *refs), in_specs=[SM] + [...  5.38 us
  transfers between devices with their start and end apart: 27, of which 14 were waited for; matrix products, arithmetic and copies ran while one was open for 0% of the time, Pallas kernels for 13%

profile of v2, /device:TPU:0, one launch (start us, length us, event | category | flops | bytes accessed | tf_op | source)
XLA Modules:
  0.0 151.7 jit_solution(8741599658703702125)
XLA Ops:
  0.6 1.6 %collective-permute-start = (bf16[64,1024]{1,0:T(8,128)(2,1)}, bf16[64,1024]{1,0:T(8,128)(2,1)S(1)}, u32[]{:S(2)}, u32[]{:S(2)}) collective-permute-start(bf16[64,1024]{1,0:T(8,128)(2,1)} %refs_0_.1), channel_id=1, source_target_pairs={{0,8},{1,3},{2,10},{3,5},{4,12},{5,7},{6,14},{7,1},{8,16},{9,11},{... | collective-permute-start | bytes 393224 | tf_op jit(solution)/shard_map/ppermute | solution.py:399
  2.3 2.7 %collective-permute-start.1 = (bf16[64,1024]{1,0:T(8,128)(2,1)}, bf16[64,1024]{1,0:T(8,128)(2,1)S(1)}, u32[]{:S(2)}, u32[]{:S(2)}) collective-permute-start(bf16[64,1024]{1,0:T(8,128)(2,1)} %refs_0_.1), channel_id=1, source_target_pairs={{0,16},{1,5},{2,18},{3,7},{4,20},{5,1},{6,22},{7,3},{8,24},{9,13},... | collective-permute-start | bytes 393224 | tf_op jit(solution)/shard_map/ppermute | solution.py:399
  5.0 1.4 collective-permute-start.2
  6.4 0.1 stack.20.place_ref.refs_0_
  6.5 0.6 collective-permute-done.refs_1_
  7.1 2.5 %collective-permute-done.1.refs_2_ = bf16[64,1024]{1,0:T(8,128)(2,1)S(1)} collective-permute-done((bf16[64,1024]{1,0:T(8,128)(2,1)}, bf16[64,1024]{1,0:T(8,128)(2,1)S(1)}, u32[]{:S(2)}, u32[]{:S(2)}) %collective-permute-start.1) | collective-permute-done | bytes 131104 | tf_op jit(solution)/shard_map/ppermute | solution.py:399
  9.6 0.6 collective-permute-done.2.refs_3_
  10.2 0.9 copy-done
  11.1 0.6 in_order.1.refs_0_.refs_3_
  11.7 0.1 collective-permute-start.3
  11.8 2.0 %collective-permute-start.4 = (bf16[256,1024]{1,0:T(8,128)(2,1)S(1)}, bf16[256,1024]{1,0:T(8,128)(2,1)S(1)}, u32[]{:S(2)}, u32[]{:S(2)}) collective-permute-start(bf16[256,1024]{1,0:T(8,128)(2,1)S(1)} %in_order.1.refs_0_.refs_3_), channel_id=1, source_target_pairs={{0,2},{1,9},{2,4},{3,11},{4,6},{5,13},{6,0},{7,15},{8,10},{9,17},{... | collective-permute-start | bytes 1572872 | tf_op jit(solution)/shard_map/ppermute | solution.py:399
  13.8 3.6 %collective-permute-start.5 = (bf16[256,1024]{1,0:T(8,128)(2,1)S(1)}, bf16[256,1024]{1,0:T(8,128)(2,1)S(1)}, u32[]{:S(2)}, u32[]{:S(2)}) collective-permute-start(bf16[256,1024]{1,0:T(8,128)(2,1)S(1)} %in_order.1.refs_0_.refs_3_), channel_id=1, source_target_pairs={{0,4},{1,17},{2,6},{3,19},{4,0},{5,21},{6,2},{7,23},{8,12},{9,25},... | collective-permute-start | bytes 1572872 | tf_op jit(solution)/shard_map/ppermute | solution.py:399
  17.3 1.0 collective-permute-start.6
  18.4 2.2 %copy-done.1 = bf16[2048,1024]{1,0:T(8,128)(2,1)S(1)} copy-done((bf16[2048,1024]{1,0:T(8,128)(2,1)S(1)}, bf16[2048,1024]{1,0:T(8,128)(2,1)}, u32[]{:S(2)}) %copy-start.1) | copy-done | bytes 4194328
  20.5 3.0 %weigh.3 = (f32[2048,512]{1,0:T(8,128)S(1)}, f32[16,128]{1,0:T(8,128)S(1)}) custom-call(s32[5]{0:T(128)S(1)} %stack.20.place_ref.refs_0_, bf16[2048,1024]{1,0:T(8,128)(2,1)S(1)} %copy-done.1, bf16[256,1024]{1,0:T(8,128)(2,1)S(1)} %in_order.1.refs_0_.refs_3_, bf16[256,1024]{1,0:T(8,128)(2,1)S(1)} %collective-permute-done.3.refs_1_.refs_4_), custom_call_target="tpu_custom_call" | custom-call | flops 30000001024 | tf_op jit(solution)/shard_map/weigh/pallas_call | solution.py:113
  23.6 6.5 %collective-permute-done.5.refs_1_.refs_6_ = bf16[256,1024]{1,0:T(8,128)(2,1)S(1)} collective-permute-done((bf16[256,1024]{1,0:T(8,128)(2,1)S(1)}, bf16[256,1024]{1,0:T(8,128)(2,1)S(1)}, u32[]{:S(2)}, u32[]{:S(2)}) %collective-permute-start.5) | collective-permute-done | bytes 524320 | tf_op jit(solution)/shard_map/ppermute | solution.py:399
  30.1 0.5 collective-permute-start.8
  30.6 0.0 collective-permute-start.9
  30.6 4.1 %weigh.4 = (f32[2048,768]{1,0:T(8,128)S(1)}, f32[16,128]{1,0:T(8,128)S(1)}) custom-call(s32[5]{0:T(128)S(1)} %stack.20.place_ref.refs_0_, bf16[2048,1024]{1,0:T(8,128)(2,1)S(1)} %copy-done.1, bf16[256,1024]{1,0:T(8,128)(2,1)S(1)} %collective-permute-done.4.refs_0_.refs_5_, bf16[256,1024]{1,0:T(8,128)(2,1)S(1)} %collective-permute-done.5.refs_1_.refs_6_, ...), custom_call_target="tpu_custom_call" | custom-call | flops 30000001024 | tf_op jit(solution)/shard_map/weigh/pallas_call | solution.py:113
  34.8 5.1 %weigh.5 = (f32[2048,768]{1,0:T(8,128)S(1)}, f32[16,128]{1,0:T(8,128)S(1)}, bf16[2048,256]{1,0:T(8,128)(2,1)S(1)}, bf16[2048,256]{1,0:T(8,128)(2,1)S(1)}, bf16[2...) custom-call(s32[5]{0:T(128)S(1)} %stack.20.place_ref.refs_0_, bf16[2048,1024]{1,0:T(8,128)(2,1)S(1)} %copy-done.1, ...), custom_call_target="tpu_custom_call" | custom-call | flops 30000001024 | tf_op jit(solution)/shard_map/weigh/pallas_call | solution.py:113
  39.9 3.3 %collective-permute-start.10 = (f32[16,128]{1,0:T(8,128)S(1)}, f32[16,128]{1,0:T(8,128)S(1)}, u32[]{:S(2)}, u32[]{:S(2)}) collective-permute-start(f32[16,128]{1,0:T(8,128)S(1)} %add_add_fusion.refs_4_), channel_id=1, source_target_pairs={{0,64},{32,96},{64,0},{96,32},{1,65},{33,97},{65,1},{97,33},{2,66}... | collective-permute-start | bytes 24584 | tf_op jit(solution)/shard_map/ppermute | solution.py:386
  43.1 0.7 collective-permute-start.11
  43.8 2.6 %collective-permute-start.12 = (f32[16,128]{1,0:T(8,128)S(1)}, f32[16,128]{1,0:T(8,128)S(1)}, u32[]{:S(2)}, u32[]{:S(2)}) collective-permute-start(f32[16,128]{1,0:T(8,128)S(1)} %add_add_fusion.refs_4_), channel_id=1, source_target_pairs={{0,96},{32,0},{64,32},{96,64},{1,97},{33,1},{65,33},{97,65},{2,98}... | collective-permute-start | bytes 24584 | tf_op jit(solution)/shard_map/ppermute | solution.py:386
  46.4 1.6 %collective-permute-done.11.refs_6_ = f32[16,128]{1,0:T(8,128)S(1)} collective-permute-done((f32[16,128]{1,0:T(8,128)S(1)}, f32[16,128]{1,0:T(8,128)S(1)}, u32[]{:S(2)}, u32[]{:S(2)}) %collective-permute-start.11) | collective-permute-done | bytes 8224 | tf_op jit(solution)/shard_map/ppermute | solution.py:386
  48.0 1.8 %row_pass.3 = (bf16[32,16,128]{2,1,0:T(8,128)(2,1)S(1)}, f32[16,128]{1,0:T(8,128)}) custom-call(s32[5]{0:T(128)S(1)} %stack.20.place_ref.refs_0_, f32[2048,512]{1,0:T(8,128)S(1)} %get-tuple-element.42.refs_1_.w0_ref, f32[2048,768]{1,0:T(8,128)S(1)} %get-tuple-element.47.refs_2_.w1_ref, f32[2048,768]{1,0:T(8,128)S(1)} %get-tuple-element.48.refs_3_.w2_ref, ...), custom_call_target="tpu_custom_call" | custom-call | tf_op jit(solution)/shard_map/row_pass/pallas_call | solution.py:155
  49.8 13.9 %all_to_all.15.sums_ref = bf16[32,16,128]{2,1,0:T(8,128)(2,1)S(1)} all-to-all(bf16[32,16,128]{2,1,0:T(8,128)(2,1)S(1)} %get-tuple-element.52), channel_id=1, replica_groups=mesh['y'=4,'x'=4,'z'=4,'core'=2] {'x','z','core'}, dimensions={0} | all-to-all | bytes 262144 | tf_op jit(solution)/shard_map/all_to_all | solution.py:430
  63.7 1.8 %col_pass.2.refs_4_ = f32[16,128]{1,0:T(8,128)S(1)} custom-call(s32[5]{0:T(128)S(1)} %stack.20.place_ref.refs_0_, f32[2048,512]{1,0:T(8,128)S(1)} %get-tuple-element.42.refs_1_.w0_ref, f32[2048,768]{1,0:T(8,128)S(1)} %get-tuple-element.47.refs_2_.w1_ref, f32[2048,768]{1,0:T(8,128)S(1)} %get-tuple-element.48.refs_3_.w2_ref, ...), custom_call_target="tpu_custom_call" | custom-call | tf_op jit(solution)/shard_map/col_pass/pallas_call | solution.py:192
  65.5 1.5 %collective-permute-start.13 = (f32[16,128]{1,0:T(8,128)S(1)}, f32[16,128]{1,0:T(8,128)S(1)}, u32[]{:S(2)}, u32[]{:S(2)}) collective-permute-start(f32[16,128]{1,0:T(8,128)S(1)} %col_pass.2.refs_4_), channel_id=1, source_target_pairs={{0,64},{32,96},{64,0},{96,32},{1,65},{33,97},{65,1},{97,33},{2,66}... | collective-permute-start | bytes 24584 | tf_op jit(solution)/shard_map/ppermute | solution.py:386
  67.1 2.6 %collective-permute-start.14 = (f32[16,128]{1,0:T(8,128)S(1)}, f32[16,128]{1,0:T(8,128)S(1)}, u32[]{:S(2)}, u32[]{:S(2)}) collective-permute-start(f32[16,128]{1,0:T(8,128)S(1)} %col_pass.2.refs_4_), channel_id=1, source_target_pairs={{0,32},{32,64},{64,96},{96,0},{1,33},{33,65},{65,97},{97,1},{2,34}... | collective-permute-start | bytes 24584 | tf_op jit(solution)/shard_map/ppermute | solution.py:386
  69.7 0.6 collective-permute-start.15
  70.3 0.5 collective-permute-done.13.refs_5_
  70.8 1.2 collective-permute-done.14.refs_6_
  71.9 1.4 collective-permute-done.15.refs_7_
  73.3 1.8 %row_pass.4 = (bf16[32,16,128]{2,1,0:T(8,128)(2,1)S(1)}, f32[16,128]{1,0:T(8,128)}) custom-call(s32[5]{0:T(128)S(1)} %stack.20.place_ref.refs_0_, f32[2048,512]{1,0:T(8,128)S(1)} %get-tuple-element.42.refs_1_.w0_ref, f32[2048,768]{1,0:T(8,128)S(1)} %get-tuple-element.47.refs_2_.w1_ref, f32[2048,768]{1,0:T(8,128)S(1)} %get-tuple-element.48.refs_3_.w2_ref, ...), custom_call_target="tpu_custom_call" | custom-call | tf_op jit(solution)/shard_map/row_pass/pallas_call | solution.py:155
  75.1 11.3 %all_to_all.16.sums_ref = bf16[32,16,128]{2,1,0:T(8,128)(2,1)S(1)} all-to-all(bf16[32,16,128]{2,1,0:T(8,128)(2,1)S(1)} %get-tuple-element.53), channel_id=1, replica_groups=mesh['y'=4,'x'=4,'z'=4,'core'=2] {'x','z','core'}, dimensions={0} | all-to-all | bytes 262144 | tf_op jit(solution)/shard_map/all_to_all | solution.py:430
  86.4 1.8 %col_pass.3.refs_4_ = f32[16,128]{1,0:T(8,128)S(1)} custom-call(s32[5]{0:T(128)S(1)} %stack.20.place_ref.refs_0_, f32[2048,512]{1,0:T(8,128)S(1)} %get-tuple-element.42.refs_1_.w0_ref, f32[2048,768]{1,0:T(8,128)S(1)} %get-tuple-element.47.refs_2_.w1_ref, f32[2048,768]{1,0:T(8,128)S(1)} %get-tuple-element.48.refs_3_.w2_ref, ...), custom_call_target="tpu_custom_call" | custom-call | tf_op jit(solution)/shard_map/col_pass/pallas_call | solution.py:192
  88.2 0.8 collective-permute-start.16
  89.0 2.0 %collective-permute-start.17 = (f32[16,128]{1,0:T(8,128)S(1)}, f32[16,128]{1,0:T(8,128)S(1)}, u32[]{:S(2)}, u32[]{:S(2)}) collective-permute-start(f32[16,128]{1,0:T(8,128)S(1)} %col_pass.3.refs_4_), channel_id=1, source_target_pairs={{0,32},{32,64},{64,96},{96,0},{1,33},{33,65},{65,97},{97,1},{2,34}... | collective-permute-start | bytes 24584 | tf_op jit(solution)/shard_map/ppermute | solution.py:386
  91.0 1.2 collective-permute-start.18
  92.2 1.2 collective-permute-done.16.refs_5_
  93.4 0.4 collective-permute-done.17.refs_6_
  93.8 0.8 collective-permute-done.18.refs_7_
  94.6 1.8 %row_pass.5 = (bf16[32,16,128]{2,1,0:T(8,128)(2,1)S(1)}, f32[16,128]{1,0:T(8,128)S(1)}) custom-call(s32[5]{0:T(128)S(1)} %stack.20.place_ref.refs_0_, f32[2048,512]{1,0:T(8,128)S(1)} %get-tuple-element.42.refs_1_.w0_ref, f32[2048,768]{1,0:T(8,128)S(1)} %get-tuple-element.47.refs_2_.w1_ref, f32[2048,768]{1,0:T(8,128)S(1)} %get-tuple-element.48.refs_3_.w2_ref, ...), custom_call_target="tpu_custom_call" | custom-call | tf_op jit(solution)/shard_map/row_pass/pallas_call | solution.py:155
  96.4 11.3 %all_to_all.17.refs_4_ = bf16[32,16,128]{2,1,0:T(8,128)(2,1)S(1)} all-to-all(bf16[32,16,128]{2,1,0:T(8,128)(2,1)S(1)} %get-tuple-element.54), channel_id=1, replica_groups=mesh['y'=4,'x'=4,'z'=4,'core'=2] {'x','z','core'}, dimensions={0} | all-to-all | bytes 262144 | tf_op jit(solution)/shard_map/all_to_all | solution.py:430
  107.7 3.4 %make_plan.2 = (bf16[1024,2048]{1,0:T(8,128)(2,1)S(1)}, f32[8,128]{1,0:T(8,128)S(1)}, bf16[1040,256]{1,0:T(8,128)(2,1)S(1)}, bf16[1040,256]{1,0:T(8,128)(2,1)S(1)}) custom-call(s32[5]{0:T(128)S(1)} %stack.20.place_ref.refs_0_, f32[2048,512]{1,0:T(8,128)S(1)} %get-tuple-element.42.refs_1_.w0_ref, f32[2048,768]{1,0:T(8,128)S(1)} %get-tuple-element.47.refs_2_.w1_ref, ...), custom_call_target="tpu_custom_call" | custom-call | flops 30000001024 | tf_op jit(solution)/shard_map/make_plan/pallas_call | solution.py:229
  111.1 0.9 collective-permute-start.23
  112.0 2.4 %collective-permute-start.24 = (bf16[1040,256]{1,0:T(8,128)(2,1)S(1)}, bf16[1040,256]{1,0:T(8,128)(2,1)S(1)}, u32[]{:S(2)}, u32[]{:S(2)}) collective-permute-start(bf16[1040,256]{1,0:T(8,128)(2,1)S(1)} %get-tuple-element.72), channel_id=1, source_target_pairs={{0,96},{32,0},{64,32},{96,64},{1,97},{33,1},{65,33},{97,65},{2,98}... | collective-permute-start | bytes 1597448 | tf_op jit(solution)/shard_map/ppermute | solution.py:386
  114.4 3.5 %make_plan.3 = (bf16[1024,2048]{1,0:T(8,128)(2,1)S(1)}, f32[8,128]{1,0:T(8,128)S(1)}, bf16[1040,256]{1,0:T(8,128)(2,1)S(1)}, bf16[1040,256]{1,0:T(8,128)(2,1)S(1)}) custom-call(s32[5]{0:T(128)S(1)} %stack.20.place_ref.refs_0_, f32[2048,512]{1,0:T(8,128)S(1)} %get-tuple-element.42.refs_1_.w0_ref, f32[2048,768]{1,0:T(8,128)S(1)} %get-tuple-element.47.refs_2_.w1_ref, ...), custom_call_target="tpu_custom_call" | custom-call | flops 30000001024 | tf_op jit(solution)/shard_map/make_plan/pallas_call | solution.py:229
  117.9 0.1 collective-permute-start.19
  118.0 3.2 %collective-permute-start.20 = (bf16[1040,256]{1,0:T(8,128)(2,1)S(1)}, bf16[1040,256]{1,0:T(8,128)(2,1)S(1)}, u32[]{:S(2)}, u32[]{:S(2)}) collective-permute-start(bf16[1040,256]{1,0:T(8,128)(2,1)S(1)} %get-tuple-element.62), channel_id=1, source_target_pairs={{0,96},{32,0},{64,32},{96,64},{1,97},{33,1},{65,33},{97,65},{2,98}... | collective-permute-start | bytes 1597448 | tf_op jit(solution)/shard_map/ppermute | solution.py:386
  121.2 6.1 %collective-permute-done.23.from_below.below = bf16[1040,256]{1,0:T(8,128)(2,1)S(1)} collective-permute-done((bf16[1040,256]{1,0:T(8,128)(2,1)S(1)}, bf16[1040,256]{1,0:T(8,128)(2,1)S(1)}, u32[]{:S(2)}, u32[]{:S(2)}) %collective-permute-start.23) | collective-permute-done | bytes 532512 | tf_op jit(solution)/shard_map/ppermute | solution.py:386
  127.3 1.2 late_sums.3
  128.6 0.7 collective-permute-start.25
  129.3 2.7 %collective-permute-start.26 = (bf16[528,256]{1,0:T(8,128)(2,1)S(1)}, bf16[528,256]{1,0:T(8,128)(2,1)S(1)}, u32[]{:S(2)}, u32[]{:S(2)}) collective-permute-start(bf16[528,256]{1,0:T(8,128)(2,1)S(1)} %get-tuple-element.76), channel_id=1, source_target_pairs={{0,96},{32,0},{64,32},{96,64},{1,97},{33,1},{65,33},{97,65},{2,98}... | collective-permute-start | bytes 811016 | tf_op jit(solution)/shard_map/ppermute | solution.py:386
  132.0 6.7 %collective-permute-done.19.from_below.refs_4_ = bf16[1040,256]{1,0:T(8,128)(2,1)S(1)} collective-permute-done((bf16[1040,256]{1,0:T(8,128)(2,1)S(1)}, bf16[1040,256]{1,0:T(8,128)(2,1)S(1)}, u32[]{:S(2)}, u32[]{:S(2)}) %collective-permute-start.19) | collective-permute-done | bytes 532512 | tf_op jit(solution)/shard_map/ppermute | solution.py:386
  138.8 1.3 late_sums.2
  140.0 0.7 collective-permute-start.21
  140.7 2.7 %collective-permute-start.22 = (bf16[528,256]{1,0:T(8,128)(2,1)S(1)}, bf16[528,256]{1,0:T(8,128)(2,1)S(1)}, u32[]{:S(2)}, u32[]{:S(2)}) collective-permute-start(bf16[528,256]{1,0:T(8,128)(2,1)S(1)} %get-tuple-element.68), channel_id=1, source_target_pairs={{0,96},{32,0},{64,32},{96,64},{1,97},{33,1},{65,33},{97,65},{2,98}... | collective-permute-start | bytes 811016 | tf_op jit(solution)/shard_map/ppermute | solution.py:386
  143.4 2.5 %own_sums.3 = (f32[1024,256]{1,0:T(8,128)S(1)}, bf16[1024,256]{1,0:T(8,128)(2,1)S(1)}) custom-call(s32[5]{0:T(128)S(1)} %stack.20.place_ref.refs_0_, bf16[1024,2048]{1,0:T(8,128)(2,1)S(1)} %get-tuple-element.70.plan_ref, bf16[1040,256]{1,0:T(8,128)(2,1)S(1)} %collective-permute-done.23.from_below.below, ...), custom_call_target="tpu_custom_call" | custom-call | flops 30000001024 | tf_op jit(solution)/shard_map/own_sums/pallas_call | solution.py:229
  145.9 1.8 %own_sums.2 = (f32[1024,256]{1,0:T(8,128)S(1)}, bf16[1024,256]{1,0:T(8,128)(2,1)S(1)}) custom-call(s32[5]{0:T(128)S(1)} %stack.20.place_ref.refs_0_, bf16[1024,2048]{1,0:T(8,128)(2,1)S(1)} %get-tuple-element.60.plan_ref, bf16[1040,256]{1,0:T(8,128)(2,1)S(1)} %collective-permute-done.19.from_below.refs_4_, ...), custom_call_target="tpu_custom_call" | custom-call | flops 30000001024 | tf_op jit(solution)/shard_map/own_sums/pallas_call | solution.py:229
  147.8 1.6 %finish.2 = (bf16[2048,256]{1,0:T(8,128)(2,1)}, f32[8,128]{1,0:T(8,128)S(1)}) custom-call(s32[5]{0:T(128)S(1)} %stack.20.place_ref.refs_0_, f32[1024,256]{1,0:T(8,128)S(1)} %get-tuple-element.74.own_ref, f32[16,128]{1,0:T(8,128)S(1)} %get-tuple-element.55.refs_5_.scale_ref.refs_2_, f32[8,128]{1,0:T(8,128)S(1)} %get-tuple-element.59.refs_6_.m_ref, ...), custom_call_target="tpu_custom_call" | custom-call | flops 30000001024 | tf_op jit(solution)/shard_map/finish/pallas_call | solution.py:365
  149.4 0.1 collective-permute-done.21.refs_6_
  149.5 1.6 %finish.3 = (bf16[2048,256]{1,0:T(8,128)(2,1)}, f32[8,128]{1,0:T(8,128)S(1)}) custom-call(s32[5]{0:T(128)S(1)} %stack.20.place_ref.refs_0_, f32[1024,256]{1,0:T(8,128)S(1)} %get-tuple-element.65.refs_1_, f32[16,128]{1,0:T(8,128)S(1)} %get-tuple-element.55.refs_5_.scale_ref.refs_2_, ...), custom_call_target="tpu_custom_call", output_to_operand_aliasing={{0}: (10, {})} | custom-call | flops 30000001024 | tf_op jit(solution)/shard_map/finish/pallas_call | solution.py:365
  151.1 0.6 maximum_bitcast_fusion
  (18 shorter events, 0.0 us)
Async XLA Ops:
  0.6 6.5 %collective-permute-start = (bf16[64,1024]{1,0:T(8,128)(2,1)}, bf16[64,1024]{1,0:T(8,128)(2,1)S(1)}, u32[]{:S(2)}, u32[]{:S(2)}) collective-permute-start(bf16[64,1024]{1,0:T(8,128)(2,1)} %refs_0_.1), channel_id=1, source_target_pairs={{0,8},{1,3},{2,10},{3,5},{4,12},{5,7},{6,14},{7,1},{8,16},{9,11},{... | collective-permute-start | bytes 393224 | tf_op jit(solution)/shard_map/ppermute | solution.py:399
  2.3 7.3 %collective-permute-start.1 = (bf16[64,1024]{1,0:T(8,128)(2,1)}, bf16[64,1024]{1,0:T(8,128)(2,1)S(1)}, u32[]{:S(2)}, u32[]{:S(2)}) collective-permute-start(bf16[64,1024]{1,0:T(8,128)(2,1)} %refs_0_.1), channel_id=1, source_target_pairs={{0,16},{1,5},{2,18},{3,7},{4,20},{5,1},{6,22},{7,3},{8,24},{9,13},... | collective-permute-start | bytes 393224 | tf_op jit(solution)/shard_map/ppermute | solution.py:399
  5.0 5.2 %collective-permute-start.2 = (bf16[64,1024]{1,0:T(8,128)(2,1)}, bf16[64,1024]{1,0:T(8,128)(2,1)S(1)}, u32[]{:S(2)}, u32[]{:S(2)}) collective-permute-start(bf16[64,1024]{1,0:T(8,128)(2,1)} %refs_0_.1), channel_id=1, source_target_pairs={{0,24},{1,7},{2,26},{3,1},{4,28},{5,3},{6,30},{7,5},{8,0},{9,15},{... | collective-permute-start | bytes 393224 | tf_op jit(solution)/shard_map/ppermute | solution.py:399
  10.2 0.9 copy-start
  11.7 6.7 %collective-permute-start.3 = (bf16[256,1024]{1,0:T(8,128)(2,1)S(1)}, bf16[256,1024]{1,0:T(8,128)(2,1)S(1)}, u32[]{:S(2)}, u32[]{:S(2)}) collective-permute-start(bf16[256,1024]{1,0:T(8,128)(2,1)S(1)} %in_order.1.refs_0_.refs_3_), channel_id=1, source_target_pairs={{0,1},{1,0},{2,3},{3,2},{4,5},{5,4},{6,7},{7,6},{8,9},{9,8},{10,11... | collective-permute-start | bytes 1572872 | tf_op jit(solution)/shard_map/ppermute | solution.py:386
  11.8 11.8 %collective-permute-start.4 = (bf16[256,1024]{1,0:T(8,128)(2,1)S(1)}, bf16[256,1024]{1,0:T(8,128)(2,1)S(1)}, u32[]{:S(2)}, u32[]{:S(2)}) collective-permute-start(bf16[256,1024]{1,0:T(8,128)(2,1)S(1)} %in_order.1.refs_0_.refs_3_), channel_id=1, source_target_pairs={{0,2},{1,9},{2,4},{3,11},{4,6},{5,13},{6,0},{7,15},{8,10},{9,17},{... | collective-permute-start | bytes 1572872 | tf_op jit(solution)/shard_map/ppermute | solution.py:399
  13.8 16.4 %collective-permute-start.5 = (bf16[256,1024]{1,0:T(8,128)(2,1)S(1)}, bf16[256,1024]{1,0:T(8,128)(2,1)S(1)}, u32[]{:S(2)}, u32[]{:S(2)}) collective-permute-start(bf16[256,1024]{1,0:T(8,128)(2,1)S(1)} %in_order.1.refs_0_.refs_3_), channel_id=1, source_target_pairs={{0,4},{1,17},{2,6},{3,19},{4,0},{5,21},{6,2},{7,23},{8,12},{9,25},... | collective-permute-start | bytes 1572872 | tf_op jit(solution)/shard_map/ppermute | solution.py:399
  17.3 12.8 %collective-permute-start.6 = (bf16[256,1024]{1,0:T(8,128)(2,1)S(1)}, bf16[256,1024]{1,0:T(8,128)(2,1)S(1)}, u32[]{:S(2)}, u32[]{:S(2)}) collective-permute-start(bf16[256,1024]{1,0:T(8,128)(2,1)S(1)} %in_order.1.refs_0_.refs_3_), channel_id=1, source_target_pairs={{0,6},{1,25},{2,0},{3,27},{4,2},{5,29},{6,4},{7,31},{8,14},{9,1},{... | collective-permute-start | bytes 1572872 | tf_op jit(solution)/shard_map/ppermute | solution.py:399
  18.4 2.2 %copy-start.1 = (bf16[2048,1024]{1,0:T(8,128)(2,1)S(1)}, bf16[2048,1024]{1,0:T(8,128)(2,1)}, u32[]{:S(2)}) copy-start(bf16[2048,1024]{1,0:T(8,128)(2,1)} %cents_ref.9) | copy-start | bytes 12582916
  30.1 4.6 %collective-permute-start.7 = (bf16[256,1024]{1,0:T(8,128)(2,1)S(1)}, bf16[256,1024]{1,0:T(8,128)(2,1)S(1)}, u32[]{:S(2)}, u32[]{:S(2)}) collective-permute-start(bf16[256,1024]{1,0:T(8,128)(2,1)S(1)} %collective-permute-done.4.refs_0_.refs_5_), channel_id=1, source_target_pairs={{0,1},{1,0},{2,3},{3,2},{4,5},{5,4},{6,7},{7,6},{8,9},{9,8},{10,11... | collective-permute-start | bytes 1572872 | tf_op jit(solution)/shard_map/ppermute | solution.py:386
  30.1 4.6 %collective-permute-start.8 = (bf16[256,1024]{1,0:T(8,128)(2,1)S(1)}, bf16[256,1024]{1,0:T(8,128)(2,1)S(1)}, u32[]{:S(2)}, u32[]{:S(2)}) collective-permute-start(bf16[256,1024]{1,0:T(8,128)(2,1)S(1)} %collective-permute-done.5.refs_1_.refs_6_), channel_id=1, source_target_pairs={{0,1},{1,0},{2,3},{3,2},{4,5},{5,4},{6,7},{7,6},{8,9},{9,8},{10,11... | collective-permute-start | bytes 1572872 | tf_op jit(solution)/shard_map/ppermute | solution.py:386
  30.6 4.1 %collective-permute-start.9 = (bf16[256,1024]{1,0:T(8,128)(2,1)S(1)}, bf16[256,1024]{1,0:T(8,128)(2,1)S(1)}, u32[]{:S(2)}, u32[]{:S(2)}) collective-permute-start(bf16[256,1024]{1,0:T(8,128)(2,1)S(1)} %collective-permute-done.6.refs_2_.refs_7_), channel_id=1, source_target_pairs={{0,1},{1,0},{2,3},{3,2},{4,5},{5,4},{6,7},{7,6},{8,9},{9,8},{10,11... | collective-permute-start | bytes 1572872 | tf_op jit(solution)/shard_map/ppermute | solution.py:386
  39.9 6.5 %collective-permute-start.10 = (f32[16,128]{1,0:T(8,128)S(1)}, f32[16,128]{1,0:T(8,128)S(1)}, u32[]{:S(2)}, u32[]{:S(2)}) collective-permute-start(f32[16,128]{1,0:T(8,128)S(1)} %add_add_fusion.refs_4_), channel_id=1, source_target_pairs={{0,64},{32,96},{64,0},{96,32},{1,65},{33,97},{65,1},{97,33},{2,66}... | collective-permute-start | bytes 24584 | tf_op jit(solution)/shard_map/ppermute | solution.py:386
  43.1 4.9 %collective-permute-start.11 = (f32[16,128]{1,0:T(8,128)S(1)}, f32[16,128]{1,0:T(8,128)S(1)}, u32[]{:S(2)}, u32[]{:S(2)}) collective-permute-start(f32[16,128]{1,0:T(8,128)S(1)} %add_add_fusion.refs_4_), channel_id=1, source_target_pairs={{0,32},{32,64},{64,96},{96,0},{1,33},{33,65},{65,97},{97,1},{2,34}... | collective-permute-start | bytes 24584 | tf_op jit(solution)/shard_map/ppermute | solution.py:386
  43.8 4.2 %collective-permute-start.12 = (f32[16,128]{1,0:T(8,128)S(1)}, f32[16,128]{1,0:T(8,128)S(1)}, u32[]{:S(2)}, u32[]{:S(2)}) collective-permute-start(f32[16,128]{1,0:T(8,128)S(1)} %add_add_fusion.refs_4_), channel_id=1, source_target_pairs={{0,96},{32,0},{64,32},{96,64},{1,97},{33,1},{65,33},{97,65},{2,98}... | collective-permute-start | bytes 24584 | tf_op jit(solution)/shard_map/ppermute | solution.py:386
  65.5 5.2 %collective-permute-start.13 = (f32[16,128]{1,0:T(8,128)S(1)}, f32[16,128]{1,0:T(8,128)S(1)}, u32[]{:S(2)}, u32[]{:S(2)}) collective-permute-start(f32[16,128]{1,0:T(8,128)S(1)} %col_pass.2.refs_4_), channel_id=1, source_target_pairs={{0,64},{32,96},{64,0},{96,32},{1,65},{33,97},{65,1},{97,33},{2,66}... | collective-permute-start | bytes 24584 | tf_op jit(solution)/shard_map/ppermute | solution.py:386
  67.1 4.9 %collective-permute-start.14 = (f32[16,128]{1,0:T(8,128)S(1)}, f32[16,128]{1,0:T(8,128)S(1)}, u32[]{:S(2)}, u32[]{:S(2)}) collective-permute-start(f32[16,128]{1,0:T(8,128)S(1)} %col_pass.2.refs_4_), channel_id=1, source_target_pairs={{0,32},{32,64},{64,96},{96,0},{1,33},{33,65},{65,97},{97,1},{2,34}... | collective-permute-start | bytes 24584 | tf_op jit(solution)/shard_map/ppermute | solution.py:386
  69.7 3.7 %collective-permute-start.15 = (f32[16,128]{1,0:T(8,128)S(1)}, f32[16,128]{1,0:T(8,128)S(1)}, u32[]{:S(2)}, u32[]{:S(2)}) collective-permute-start(f32[16,128]{1,0:T(8,128)S(1)} %col_pass.2.refs_4_), channel_id=1, source_target_pairs={{0,96},{32,0},{64,32},{96,64},{1,97},{33,1},{65,33},{97,65},{2,98}... | collective-permute-start | bytes 24584 | tf_op jit(solution)/shard_map/ppermute | solution.py:386
  88.2 5.2 %collective-permute-start.16 = (f32[16,128]{1,0:T(8,128)S(1)}, f32[16,128]{1,0:T(8,128)S(1)}, u32[]{:S(2)}, u32[]{:S(2)}) collective-permute-start(f32[16,128]{1,0:T(8,128)S(1)} %col_pass.3.refs_4_), channel_id=1, source_target_pairs={{0,64},{32,96},{64,0},{96,32},{1,65},{33,97},{65,1},{97,33},{2,66}... | collective-permute-start | bytes 24584 | tf_op jit(solution)/shard_map/ppermute | solution.py:386
  89.0 4.9 %collective-permute-start.17 = (f32[16,128]{1,0:T(8,128)S(1)}, f32[16,128]{1,0:T(8,128)S(1)}, u32[]{:S(2)}, u32[]{:S(2)}) collective-permute-start(f32[16,128]{1,0:T(8,128)S(1)} %col_pass.3.refs_4_), channel_id=1, source_target_pairs={{0,32},{32,64},{64,96},{96,0},{1,33},{33,65},{65,97},{97,1},{2,34}... | collective-permute-start | bytes 24584 | tf_op jit(solution)/shard_map/ppermute | solution.py:386
  91.0 3.7 %collective-permute-start.18 = (f32[16,128]{1,0:T(8,128)S(1)}, f32[16,128]{1,0:T(8,128)S(1)}, u32[]{:S(2)}, u32[]{:S(2)}) collective-permute-start(f32[16,128]{1,0:T(8,128)S(1)} %col_pass.3.refs_4_), channel_id=1, source_target_pairs={{0,96},{32,0},{64,32},{96,64},{1,97},{33,1},{65,33},{97,65},{2,98}... | collective-permute-start | bytes 24584 | tf_op jit(solution)/shard_map/ppermute | solution.py:386
  111.1 16.2 %collective-permute-start.23 = (bf16[1040,256]{1,0:T(8,128)(2,1)S(1)}, bf16[1040,256]{1,0:T(8,128)(2,1)S(1)}, u32[]{:S(2)}, u32[]{:S(2)}) collective-permute-start(bf16[1040,256]{1,0:T(8,128)(2,1)S(1)} %get-tuple-element.71), channel_id=1, source_target_pairs={{0,32},{32,64},{64,96},{96,0},{1,33},{33,65},{65,97},{97,1},{2,34}... | collective-permute-start | bytes 1597448 | tf_op jit(solution)/shard_map/ppermute | solution.py:386
  112.0 15.3 %collective-permute-start.24 = (bf16[1040,256]{1,0:T(8,128)(2,1)S(1)}, bf16[1040,256]{1,0:T(8,128)(2,1)S(1)}, u32[]{:S(2)}, u32[]{:S(2)}) collective-permute-start(bf16[1040,256]{1,0:T(8,128)(2,1)S(1)} %get-tuple-element.72), channel_id=1, source_target_pairs={{0,96},{32,0},{64,32},{96,64},{1,97},{33,1},{65,33},{97,65},{2,98}... | collective-permute-start | bytes 1597448 | tf_op jit(solution)/shard_map/ppermute | solution.py:386
  117.9 20.8 %collective-permute-start.19 = (bf16[1040,256]{1,0:T(8,128)(2,1)S(1)}, bf16[1040,256]{1,0:T(8,128)(2,1)S(1)}, u32[]{:S(2)}, u32[]{:S(2)}) collective-permute-start(bf16[1040,256]{1,0:T(8,128)(2,1)S(1)} %get-tuple-element.61), channel_id=1, source_target_pairs={{0,32},{32,64},{64,96},{96,0},{1,33},{33,65},{65,97},{97,1},{2,34}... | collective-permute-start | bytes 1597448 | tf_op jit(solution)/shard_map/ppermute | solution.py:386
  118.0 20.8 %collective-permute-start.20 = (bf16[1040,256]{1,0:T(8,128)(2,1)S(1)}, bf16[1040,256]{1,0:T(8,128)(2,1)S(1)}, u32[]{:S(2)}, u32[]{:S(2)}) collective-permute-start(bf16[1040,256]{1,0:T(8,128)(2,1)S(1)} %get-tuple-element.62), channel_id=1, source_target_pairs={{0,96},{32,0},{64,32},{96,64},{1,97},{33,1},{65,33},{97,65},{2,98}... | collective-permute-start | bytes 1597448 | tf_op jit(solution)/shard_map/ppermute | solution.py:386
  128.6 19.2 %collective-permute-start.25 = (bf16[528,256]{1,0:T(8,128)(2,1)S(1)}, bf16[528,256]{1,0:T(8,128)(2,1)S(1)}, u32[]{:S(2)}, u32[]{:S(2)}) collective-permute-start(bf16[528,256]{1,0:T(8,128)(2,1)S(1)} %get-tuple-element.75), channel_id=1, source_target_pairs={{0,32},{32,64},{64,96},{96,0},{1,33},{33,65},{65,97},{97,1},{2,34}... | collective-permute-start | bytes 811016 | tf_op jit(solution)/shard_map/ppermute | solution.py:386
  129.3 18.5 %collective-permute-start.26 = (bf16[528,256]{1,0:T(8,128)(2,1)S(1)}, bf16[528,256]{1,0:T(8,128)(2,1)S(1)}, u32[]{:S(2)}, u32[]{:S(2)}) collective-permute-start(bf16[528,256]{1,0:T(8,128)(2,1)S(1)} %get-tuple-element.76), channel_id=1, source_target_pairs={{0,96},{32,0},{64,32},{96,64},{1,97},{33,1},{65,33},{97,65},{2,98}... | collective-permute-start | bytes 811016 | tf_op jit(solution)/shard_map/ppermute | solution.py:386
  140.0 9.5 %collective-permute-start.21 = (bf16[528,256]{1,0:T(8,128)(2,1)S(1)}, bf16[528,256]{1,0:T(8,128)(2,1)S(1)}, u32[]{:S(2)}, u32[]{:S(2)}) collective-permute-start(bf16[528,256]{1,0:T(8,128)(2,1)S(1)} %get-tuple-element.67), channel_id=1, source_target_pairs={{0,32},{32,64},{64,96},{96,0},{1,33},{33,65},{65,97},{97,1},{2,34}... | collective-permute-start | bytes 811016 | tf_op jit(solution)/shard_map/ppermute | solution.py:386
  140.7 8.8 %collective-permute-start.22 = (bf16[528,256]{1,0:T(8,128)(2,1)S(1)}, bf16[528,256]{1,0:T(8,128)(2,1)S(1)}, u32[]{:S(2)}, u32[]{:S(2)}) collective-permute-start(bf16[528,256]{1,0:T(8,128)(2,1)S(1)} %get-tuple-element.68), channel_id=1, source_target_pairs={{0,96},{32,0},{64,32},{96,64},{1,97},{33,1},{65,33},{97,65},{2,98}... | collective-permute-start | bytes 811016 | tf_op jit(solution)/shard_map/ppermute | solution.py:386

commit v3 on v2

--- a/solution.py
+++ b/solution.py
@@ -14,8 +14,10 @@
 LANES = 128
 TAIL = 16
 PLACES = 4
+PLANES = 4
 LINES = 2
-ORDER = ((True, 0), (False, 0), (True, 1), (True, 2), (True, 3), (False, 1), (False, 2), (False, 3))
+ORDER = ((True, 0), (False, 0), (True, 1), (True, 3), (False, 1), (False, 3), (True, 2), (False, 2))
+PARTS = 3
 FLOPS = 3 * 10**10
 WEIGH_VMEM = 16 * 1024 * 1024
 SUM_VMEM = 10 * 1024 * 1024
@@ -70,71 +72,94 @@
     )(place, *blocks)
 
 
-def weigh_kernel(count, cuts, place_ref, cents_ref, *refs):
-    blocks, every = refs[:count], refs[count : count + cuts * 2]
-    w_ref, mass_ref, *outs = refs[count + cuts * 2 : count + cuts * 3 + 2]
-    acc_ref, sem = refs[-2:]
+def weigh_kernel(count, at, last, place_ref, cents_ref, *refs):
+    blocks = refs[:count]
+    olds = 0 if at == 0 else PLANES + 1
+    w_ref, *outs = refs[count + olds :]
+    cuts, acc_ref = (outs[:-2], outs[-2]) if last else (outs[:-1], outs[-1])
     n = w_ref.shape[0]
     rows = 512
-    copies = []
-    for k, out in enumerate(outs):
-        share = out.shape[1]
-        part = pl.ds(pl.multiple_of(lax.rem(place_ref[1] + k, cuts) * share, share), share)
-        for i, block in enumerate(every):
-            size = block.shape[0]
-            copies.append(
-                pltpu.make_async_copy(block.at[:, part], out.at[pl.ds(i * size, size)], sem.at[len(copies)])
-            )
-    for copy in copies:
-        copy.start()
+    full = LANES * LINES
+    groups = []
+    for block in blocks:
+        if groups and sum(x.shape[0] for x in groups[-1]) < full:
+            groups[-1].append(block)
+        else:
+            groups.append([block])
     for k in range(0, n, rows):
-        acc, at = None, 0
-        for block in blocks:
-            cols = block.shape[0]
+        acc, left = None if at == 0 else acc_ref[k : k + rows, :], 0
+        for group in groups:
+            vecs = jnp.concatenate([block[...] for block in group], axis=0)
+            cols = vecs.shape[0]
             logits = lax.dot_general(
-                cents_ref[k : k + rows, :], block[...], (((1,), (1,)), ((), ())), preferred_element_type=jnp.float32
+                cents_ref[k : k + rows, :], vecs, (((1,), (1,)), ((), ())), preferred_element_type=jnp.float32
             )
             w = jnp.exp2(logits * (SHARP * LOG2E))
-            w_ref[k : k + rows, at : at + cols] = w
-            at += cols
+            w_ref[k : k + rows, left : left + cols] = w
+            left += cols
             for j in range(0, cols, LANES):
                 acc = w[:, j : j + LANES] if acc is None else acc + w[:, j : j + LANES]
-        acc_ref[k : k + rows, :] = acc
-    for g in range(n // LANES):
-        mass_ref[g : g + 1, :] = row_of(acc_ref[g * LANES : (g + 1) * LANES, :])
-    for copy in copies:
-        copy.wait()
-
-
-def weigh(place, cents, blocks, cuts=0, every=()):
+        if not last:
+            acc_ref[k : k + rows, :] = acc
+        else:
+            for g in range(0, rows, LANES):
+                line = (k + g) // LANES
+                outs[-1][line : line + 1, :] = row_of(acc[g : g + LANES, :])
+    for k, cut in enumerate(cuts):
+        share, top = cut.shape[1], at
+        part = pl.ds(pl.multiple_of(lax.rem(place_ref[1] + k, len(cuts)) * share, share), share)
+        for block in blocks:
+            cut[top : top + block.shape[0], :] = block[:, part]
+            top += block.shape[0]
+
+
+def weigh(place, cents, blocks, planes, total, at, old=()):
     n, d = cents.shape
     m = sum(block.shape[0] for block in blocks)
-    total = sum(block.shape[0] for block in every)
-    return pl.pallas_call(
-        functools.partial(weigh_kernel, len(blocks), cuts),
-        in_specs=[SM, VM] + [VM] * len(blocks) + [pl.BlockSpec(memory_space=pl.ANY)] * len(every),
-        out_specs=[VM] * (2 + cuts),
-        out_shape=[pltpu.VMEM((n, m), jnp.float32), jax.ShapeDtypeStruct((n // LANES, LANES), jnp.float32)]
-        + [pltpu.VMEM((total, d // cuts), cents.dtype) for _ in range(cuts)],
-        scratch_shapes=[
-            pltpu.VMEM((n, LANES), jnp.float32),
-            pltpu.SemaphoreType.DMA((max(len(every) * cuts, 1),)),
-        ],
+    last = at + m == total
+    out_shape = [pltpu.VMEM((n, m), jnp.float32)]
+    out_shape += [pltpu.VMEM((total, d // planes), cents.dtype) for _ in range(planes)]
+    out_shape += [pltpu.VMEM((n, LANES), jnp.float32)]
+    if last:
+        out_shape += [jax.ShapeDtypeStruct((n // LANES, LANES), jnp.float32)]
+    return pl.pallas_call(
+        functools.partial(weigh_kernel, len(blocks), at, last),
+        in_specs=[SM] + [VM] * (1 + len(blocks) + len(old)),
+        out_specs=[VM] * len(out_shape),
+        out_shape=out_shape,
+        input_output_aliases={2 + len(blocks) + k: 1 + k for k in range(len(old))},
         compiler_params=params(WEIGH_VMEM),
         cost_estimate=pl.CostEstimate(flops=FLOPS, bytes_accessed=0, transcendentals=0),
         name="weigh",
-    )(place, held(cents), *[held(block) for block in blocks], *every)
+    )(place, held(cents), *[held(x) for x in (*blocks, *old)])
+
+
+def lift_kernel(x_ref, out_ref):
+    out_ref[...] = x_ref[...]
+
+
+def lift(x):
+    return pl.pallas_call(
+        lift_kernel,
+        in_specs=[VM],
+        out_specs=VM,
+        out_shape=pltpu.VMEM(x.shape, x.dtype),
+        compiler_params=params(8 * 1024 * 1024),
+        cost_estimate=pl.CostEstimate(flops=FLOPS, bytes_accessed=0, transcendentals=0),
+        name="lift",
+    )(outside(x))
 
 
 def tiles_of(w_refs):
     return [(ref, t) for ref in w_refs for t in range(0, ref.shape[1], LANES)]
 
 
-def row_kernel(target, place_ref, w0_ref, w1_ref, w2_ref, a_ref, b_ref, c_ref, d_ref, out_ref, scale_ref, lines_ref):
+def row_kernel(target, place_ref, *refs):
+    w_refs, (a_ref, b_ref, c_ref, d_ref, out_ref, scale_ref, lines_ref) = refs[:PARTS], refs[PARTS:]
     scale_ref[...] = target / ((a_ref[...] + b_ref[...]) + (c_ref[...] + d_ref[...]))
-    tiles = tiles_of((w0_ref, w1_ref, w2_ref))
+    tiles = tiles_of(w_refs)
     accs = [None] * len(tiles)
-    for b in range(w0_ref.shape[0] // LANES):
+    for b in range(w_refs[0].shape[0] // LANES):
         part = slice(b * LANES, (b + 1) * LANES)
         s = down(scale_ref[b : b + 1, :])
         for j, (ref, t) in enumerate(tiles):
@@ -154,7 +179,7 @@
     lines = len(ORDER) * LINES
     return pl.pallas_call(
         lambda *refs: row_kernel(target, *refs),
-        in_specs=[SM] + [VM] * 7,
+        in_specs=[SM] + [VM] * (PARTS + 4),
         out_specs=[VM, VM],
         out_shape=[
             jax.ShapeDtypeStruct((peers, lines, LANES), jnp.bfloat16),
@@ -175,10 +200,11 @@
     return [pair[i : i + 1, :] for pair in scale for i in range(LINES)]
 
 
-def col_kernel(place_ref, w0_ref, w1_ref, w2_ref, sums_ref, out_ref, lines_ref):
+def col_kernel(place_ref, *refs):
+    w_refs, (sums_ref, out_ref, lines_ref) = refs[:PARTS], refs[PARTS:]
     scale = local_scale(place_ref, sums_ref, lines_ref)
-    tiles = tiles_of((w0_ref, w1_ref, w2_ref))
-    for b in range(w0_ref.shape[0] // LANES):
+    tiles = tiles_of(w_refs)
+    for b in range(w_refs[0].shape[0] // LANES):
         part = slice(b * LANES, (b + 1) * LANES)
         acc = None
         for j, (ref, t) in enumerate(tiles):
@@ -191,7 +217,7 @@
     n = w[0].shape[0]
     return pl.pallas_call(
         col_kernel,
-        in_specs=[SM] + [VM] * 4,
+        in_specs=[SM] + [VM] * (PARTS + 1),
         out_specs=VM,
         out_shape=jax.ShapeDtypeStruct((n // LANES, LANES), jnp.float32),
         scratch_shapes=[pltpu.VMEM(sums.shape[1:], jnp.float32)],
@@ -238,12 +264,11 @@
     )(*args)
 
 
-def plan_kernel(
-    first, place_ref, w0_ref, w1_ref, w2_ref, sums_ref, scale_ref, mark_ref, u_ref, f_ref, d_ref, *refs
-):
+def plan_kernel(first, place_ref, *refs):
+    w_refs, (sums_ref, scale_ref, mark_ref, u_ref, f_ref, d_ref, *refs) = refs[:PARTS], refs[PARTS:]
     plan_ref, mass_ref, up_ref, down_ref, lines_ref = refs
     scale = local_scale(place_ref, sums_ref, lines_ref)
-    tiles = tiles_of((w0_ref, w1_ref, w2_ref))
+    tiles = tiles_of(w_refs)
     rows = 2 * LANES
     n = plan_ref.shape[0]
     half = n // 2
@@ -273,7 +298,7 @@
     return call(
         lambda *refs: plan_kernel(first, *refs),
         "make_plan",
-        [SM] + [VM] * 9,
+        [SM] + [VM] * (PARTS + 6),
         [pltpu.VMEM((n // 2, m), jnp.bfloat16), jax.ShapeDtypeStruct((n // 2 // LANES, LANES), jnp.float32), part, part],
         (place, *[held(x) for x in w], sums, scale, mark, *[held(v) for v in cuts[1:]]),
         [pltpu.VMEM(sums.shape[1:], jnp.float32)],
@@ -413,18 +438,20 @@
     n, d = centroids.shape
     target = vectors.shape[0] * planes * peers / (n * peers)
 
-    near = in_order(place, [spread(vectors, turn, True) for turn in range(PLACES)])
-    mine = [spread(near, turn, False) for turn in range(PLACES)]
-    other = [move(mine[0], "core", 1)]
-    w0, mass0 = weigh(place, centroids, (mine[0], other[0]))
-    mass0, *mine[1:] = lax.optimization_barrier((mass0, *mine[1:]))
-    other += [move(block, "core", 1) for block in mine[1:]]
-    every = (mine[0], other[0], *mine[1:], *other[1:])
-    w1, mass1 = weigh(place, centroids, mine[1:])
-    w2, mass2, *cuts = weigh(place, centroids, other[1:], planes, every)
+    near = in_order(place, [lift(vectors)] + [spread(vectors, turn, True) for turn in range(1, PLACES)])
+    size = near.shape[0]
+    one, three = spread(near, 1, False), spread(near, 3, False)
+    total = size * len(ORDER)
+    w0, *old = weigh(place, centroids, (near, move(near, "core", 1)), planes, total, 0)
+    mark, one, three = lax.optimization_barrier((old[-1], one, three))
+    other = move(one, "core", 1), move(three, "core", 1)
+    two = spread(one[: size // 2], 1, False), spread(three[size // 2 :], 3, False)
+    w1, *old = weigh(place, centroids, (one, three, *other), planes, total, 2 * size, (*old[:-1], mark))
+    mark, *two = lax.optimization_barrier((old[-1], *two))
+    other = [move(block, "core", 1) for block in two]
+    w2, *cuts, _, colmass = weigh(place, centroids, (*two, *other), planes, total, 6 * size, (*old[:-1], mark))
     w = (w0, w1, w2)
 
-    colmass = mass0 + mass1 + mass2
     for step in range(ROUNDS):
         sums, scale = row_pass(target, place, w, row_peers(colmass), peers)
         sums = lax.all_to_all(sums, CENTS, 0, 0, tiled=True)

time: 152 us -> 149 us (0.980)
  waiting for transfers between devices: 30.2 us -> 25.8 us
  starting transfers between devices: 41.7 us -> 43.6 us
    ppermute x6 -> x7, waiting for transfers between devices: 10.2 us -> 4.61 us  [spread(): return lax.ppermute(x, CENTS, pairs)]
    ppermute x21 -> x22, waiting for transfers between devices: 20 us -> 21.2 us  [move(): return lax.ppermute(x, axis, [(i, (i + by) % n) for i in range(n)])]
    ppermute x6 -> x7, starting transfers between devices: 12.4 us -> 13.5 us  [spread(): return lax.ppermute(x, CENTS, pairs)]
    unnamed x4 -> x2, local copies, waits for them, and re-layouts: 3.09 us -> 2.19 us
    ppermute x21 -> x22, starting transfers between devices: 29.3 us -> 30.1 us  [move(): return lax.ppermute(x, axis, [(i, (i + by) % n) for i in range(n)])]
    pallas_call x5 -> x6, Pallas kernels: 15.7 us -> 15.9 us  [the longest x3 11.3 us: weigh(): pl.pallas_call(functools.partial(weigh_kernel, len(blocks), at, last), in...]
  transfers between devices with their start and end apart: 27 -> 29, of which waited for: 14 -> 15; matrix products, arithmetic and copies ran while one was open for 0% -> 0% of each run, Pallas kernels for 13% -> 14%
where the time goes in v3:
time: 149 us
  starting transfers between devices  43.6 us (29%)
  Pallas kernels  39.2 us (26%)
  blocking collectives  36.3 us (24%)
  waiting for transfers between devices  25.8 us (17%)
  local copies, waits for them, and re-layouts  2.31 us (2%)
    all_to_all x3, blocking collectives, body(): sums = lax.all_to_all(sums, CENTS, 0, 0, tiled=True)  36.3 us
    ppermute x22, starting transfers between devices, move(): return lax.ppermute(x, axis, [(i, (i + by) % n) for i in range(n)])  30.1 us
    ppermute x22, waiting for transfers between devices, move(): return lax.ppermute(x, axis, [(i, (i + by) % n) for i in range(n)])  21.2 us
    pallas_call x6, Pallas kernels, call(): pl.pallas_call(kernel, in_specs=specs, out_specs=[VM] * len(out_shape), o...  14.1 us
    ppermute x7, starting transfers between devices, spread(): return lax.ppermute(x, CENTS, pairs)  13.5 us
    pallas_call x3, Pallas kernels, weigh(): pl.pallas_call(functools.partial(weigh_kernel, len(blocks), at, last), in...  11.3 us
    pallas_call x3, Pallas kernels, row_pass(): pl.pallas_call(lambda *refs: row_kernel(target, *refs), in_specs=[SM] + [...  5.37 us
    ppermute x7, waiting for transfers between devices, spread(): return lax.ppermute(x, CENTS, pairs)  4.61 us
  transfers between devices with their start and end apart: 29, of which 15 were waited for; matrix products, arithmetic and copies ran while one was open for 0% of the time, Pallas kernels for 14%

profile of v3, /device:TPU:0, one launch (start us, length us, event | category | flops | bytes accessed | tf_op | source)
XLA Modules:
  0.0 148.7 jit_solution(6678004872173802654)
XLA Ops:
  0.6 1.6 %collective-permute-start = (bf16[64,1024]{1,0:T(8,128)(2,1)}, bf16[64,1024]{1,0:T(8,128)(2,1)S(1)}, u32[]{:S(2)}, u32[]{:S(2)}) collective-permute-start(bf16[64,1024]{1,0:T(8,128)(2,1)} %x_ref.1), channel_id=1, source_target_pairs={{0,8},{1,3},{2,10},{3,5},{4,12},{5,7},{6,14},{7,1},{8,16},{9,11},{... | collective-permute-start | bytes 393224 | tf_op jit(solution)/shard_map/ppermute | solution.py:424
  2.3 2.7 %collective-permute-start.1 = (bf16[64,1024]{1,0:T(8,128)(2,1)}, bf16[64,1024]{1,0:T(8,128)(2,1)S(1)}, u32[]{:S(2)}, u32[]{:S(2)}) collective-permute-start(bf16[64,1024]{1,0:T(8,128)(2,1)} %x_ref.1), channel_id=1, source_target_pairs={{0,16},{1,5},{2,18},{3,7},{4,20},{5,1},{6,22},{7,3},{8,24},{9,13},... | collective-permute-start | bytes 393224 | tf_op jit(solution)/shard_map/ppermute | solution.py:424
  5.0 1.4 collective-permute-start.2
  6.4 0.9 lift.1.refs_0_
  7.4 0.1 stack.20.place_ref.refs_0_
  7.5 2.1 %collective-permute-done.1.refs_2_ = bf16[64,1024]{1,0:T(8,128)(2,1)S(1)} collective-permute-done((bf16[64,1024]{1,0:T(8,128)(2,1)}, bf16[64,1024]{1,0:T(8,128)(2,1)S(1)}, u32[]{:S(2)}, u32[]{:S(2)}) %collective-permute-start.1) | collective-permute-done | bytes 131104 | tf_op jit(solution)/shard_map/ppermute | solution.py:424
  9.6 0.6 collective-permute-done.2.refs_3_
  10.2 0.6 in_order.1.refs_0_
  10.8 0.1 collective-permute-start.3
  10.9 2.0 %collective-permute-start.4 = (bf16[256,1024]{1,0:T(8,128)(2,1)S(1)}, bf16[256,1024]{1,0:T(8,128)(2,1)S(1)}, u32[]{:S(2)}, u32[]{:S(2)}) collective-permute-start(bf16[256,1024]{1,0:T(8,128)(2,1)S(1)} %in_order.1.refs_0_), channel_id=1, source_target_pairs={{0,2},{1,9},{2,4},{3,11},{4,6},{5,13},{6,0},{7,15},{8,10},{9,17},{... | collective-permute-start | bytes 1572872 | tf_op jit(solution)/shard_map/ppermute | solution.py:424
  12.9 2.2 %collective-permute-start.5 = (bf16[256,1024]{1,0:T(8,128)(2,1)S(1)}, bf16[256,1024]{1,0:T(8,128)(2,1)S(1)}, u32[]{:S(2)}, u32[]{:S(2)}) collective-permute-start(bf16[256,1024]{1,0:T(8,128)(2,1)S(1)} %in_order.1.refs_0_), channel_id=1, source_target_pairs={{0,6},{1,25},{2,0},{3,27},{4,2},{5,29},{6,4},{7,31},{8,14},{9,1},{... | collective-permute-start | bytes 1572872 | tf_op jit(solution)/shard_map/ppermute | solution.py:424
  15.1 2.2 %copy-done = bf16[2048,1024]{1,0:T(8,128)(2,1)S(1)} copy-done((bf16[2048,1024]{1,0:T(8,128)(2,1)S(1)}, bf16[2048,1024]{1,0:T(8,128)(2,1)}, u32[]{:S(2)}) %copy-start) | copy-done | bytes 4194328
  17.2 3.0 %weigh.3 = (f32[2048,512]{1,0:T(8,128)S(1)}, bf16[2048,256]{1,0:T(8,128)(2,1)S(1)}, bf16[2048,256]{1,0:T(8,128)(2,1)S(1)}, bf16[2048,256]{1,0:T(8,128)(2,1)S(1)}...) custom-call(s32[5]{0:T(128)S(1)} %stack.20.place_ref.refs_0_, bf16[2048,1024]{1,0:T(8,128)(2,1)S(1)} %copy-done, ...), custom_call_target="tpu_custom_call" | custom-call | flops 30000001024 | tf_op jit(solution)/shard_map/weigh/pallas_call | solution.py:125
  20.2 1.9 %collective-permute-done.4.refs_0_ = bf16[256,1024]{1,0:T(8,128)(2,1)S(1)} collective-permute-done((bf16[256,1024]{1,0:T(8,128)(2,1)S(1)}, bf16[256,1024]{1,0:T(8,128)(2,1)S(1)}, u32[]{:S(2)}, u32[]{:S(2)}) %collective-permute-start.4) | collective-permute-done | bytes 524320 | tf_op jit(solution)/shard_map/ppermute | solution.py:424
  22.1 0.5 collective-permute-start.7
  22.7 1.9 %collective-permute-start.8 = (bf16[128,1024]{1,0:T(8,128)(2,1)S(1)}, bf16[128,1024]{1,0:T(8,128)(2,1)S(1)}, u32[]{:S(2)}, u32[]{:S(2)}) collective-permute-start(bf16[128,1024]{1,0:T(8,128)(2,1)S(1)} %slice.6), channel_id=1, source_target_pairs={{0,2},{1,9},{2,4},{3,11},{4,6},{5,13},{6,0},{7,15},{8,10},{9,17},{... | collective-permute-start | bytes 786440 | tf_op jit(solution)/shard_map/ppermute | solution.py:424
  24.6 1.6 %collective-permute-start.9 = (bf16[128,1024]{1,0:T(8,128)(2,1)S(1)}, bf16[128,1024]{1,0:T(8,128)(2,1)S(1)}, u32[]{:S(2)}, u32[]{:S(2)}) collective-permute-start(bf16[128,1024]{1,0:T(8,128)(2,1)S(1)} %slice.7), channel_id=1, source_target_pairs={{0,6},{1,25},{2,0},{3,27},{4,2},{5,29},{6,4},{7,31},{8,14},{9,1},{... | collective-permute-start | bytes 786440 | tf_op jit(solution)/shard_map/ppermute | solution.py:424
  26.2 5.3 %weigh.4 = (f32[2048,1024]{1,0:T(8,128)S(1)}, bf16[2048,256]{1,0:T(8,128)(2,1)S(1)}, bf16[2048,256]{1,0:T(8,128)(2,1)S(1)}, bf16[2048,256]{1,0:T(8,128)(2,1)S(1)...) custom-call(s32[5]{0:T(128)S(1)} %stack.20.place_ref.refs_0_, ...), custom_call_target="tpu_custom_call", output_to_operand_aliasing={{1}: (6, {}), {2}: (7, {}), {3}: (8, {}), {4}: (9, {}), {5}... | custom-call | flops 30000001024 | tf_op jit(solution)/shard_map/weigh/pallas_call | solution.py:125
  31.6 0.5 collective-permute-start.11
  32.1 1.0 collective-permute-done.10.refs_2_
  33.1 0.4 collective-permute-done.11.refs_3_
  33.5 3.1 %weigh.5 = (f32[2048,512]{1,0:T(8,128)S(1)}, bf16[2048,256]{1,0:T(8,128)(2,1)S(1)}, bf16[2048,256]{1,0:T(8,128)(2,1)S(1)}, bf16[2048,256]{1,0:T(8,128)(2,1)S(1)}...) custom-call(s32[5]{0:T(128)S(1)} %stack.20.place_ref.refs_0_, ...), custom_call_target="tpu_custom_call", output_to_operand_aliasing={{1}: (6, {}), {2}: (7, {}), {3}: (8, {}), {4}: (9, {}), {5}... | custom-call | flops 30000001024 | tf_op jit(solution)/shard_map/weigh/pallas_call | solution.py:125
  36.6 3.4 %collective-permute-start.12 = (f32[16,128]{1,0:T(8,128)S(1)}, f32[16,128]{1,0:T(8,128)S(1)}, u32[]{:S(2)}, u32[]{:S(2)}) collective-permute-start(f32[16,128]{1,0:T(8,128)S(1)} %get-tuple-element.71.refs_4_), channel_id=1, source_target_pairs={{0,64},{32,96},{64,0},{96,32},{1,65},{33,97},{65,1},{97,33},{2,66}... | collective-permute-start | bytes 24584 | tf_op jit(solution)/shard_map/ppermute | solution.py:411
  40.0 0.7 collective-permute-start.13
  40.7 2.6 %collective-permute-start.14 = (f32[16,128]{1,0:T(8,128)S(1)}, f32[16,128]{1,0:T(8,128)S(1)}, u32[]{:S(2)}, u32[]{:S(2)}) collective-permute-start(f32[16,128]{1,0:T(8,128)S(1)} %get-tuple-element.71.refs_4_), channel_id=1, source_target_pairs={{0,96},{32,0},{64,32},{96,64},{1,97},{33,1},{65,33},{97,65},{2,98}... | collective-permute-start | bytes 24584 | tf_op jit(solution)/shard_map/ppermute | solution.py:411
  43.3 1.6 %collective-permute-done.13.refs_6_ = f32[16,128]{1,0:T(8,128)S(1)} collective-permute-done((f32[16,128]{1,0:T(8,128)S(1)}, f32[16,128]{1,0:T(8,128)S(1)}, u32[]{:S(2)}, u32[]{:S(2)}) %collective-permute-start.13) | collective-permute-done | bytes 8224 | tf_op jit(solution)/shard_map/ppermute | solution.py:411
  44.9 1.8 %row_pass.3 = (bf16[32,16,128]{2,1,0:T(8,128)(2,1)S(1)}, f32[16,128]{1,0:T(8,128)}) custom-call(s32[5]{0:T(128)S(1)} %stack.20.place_ref.refs_0_, f32[2048,512]{1,0:T(8,128)S(1)} %get-tuple-element.52.refs_1_.refs_0_, f32[2048,1024]{1,0:T(8,128)S(1)} %get-tuple-element.61.refs_2_.refs_1_, f32[2048,512]{1,0:T(8,128)S(1)} %get-tuple-element.70.refs_3_.refs_2_, ...), custom_call_target="tpu_custom_call" | custom-call | tf_op jit(solution)/shard_map/row_pass/pallas_call | solution.py:180
  46.7 13.8 %all_to_all.15.refs_3_ = bf16[32,16,128]{2,1,0:T(8,128)(2,1)S(1)} all-to-all(bf16[32,16,128]{2,1,0:T(8,128)(2,1)S(1)} %get-tuple-element.72), channel_id=1, replica_groups=mesh['y'=4,'x'=4,'z'=4,'core'=2] {'x','z','core'}, dimensions={0} | all-to-all | bytes 262144 | tf_op jit(solution)/shard_map/all_to_all | solution.py:457
  60.4 1.8 %col_pass.2.refs_4_ = f32[16,128]{1,0:T(8,128)S(1)} custom-call(s32[5]{0:T(128)S(1)} %stack.20.place_ref.refs_0_, f32[2048,512]{1,0:T(8,128)S(1)} %get-tuple-element.52.refs_1_.refs_0_, f32[2048,1024]{1,0:T(8,128)S(1)} %get-tuple-element.61.refs_2_.refs_1_, f32[2048,512]{1,0:T(8,128)S(1)} %get-tuple-element.70.refs_3_.refs_2_, ...), custom_call_target="tpu_custom_call" | custom-call | tf_op jit(solution)/shard_map/col_pass/pallas_call | solution.py:218
  62.2 1.5 %collective-permute-start.15 = (f32[16,128]{1,0:T(8,128)S(1)}, f32[16,128]{1,0:T(8,128)S(1)}, u32[]{:S(2)}, u32[]{:S(2)}) collective-permute-start(f32[16,128]{1,0:T(8,128)S(1)} %col_pass.2.refs_4_), channel_id=1, source_target_pairs={{0,64},{32,96},{64,0},{96,32},{1,65},{33,97},{65,1},{97,33},{2,66}... | collective-permute-start | bytes 24584 | tf_op jit(solution)/shard_map/ppermute | solution.py:411
  63.8 2.6 %collective-permute-start.16 = (f32[16,128]{1,0:T(8,128)S(1)}, f32[16,128]{1,0:T(8,128)S(1)}, u32[]{:S(2)}, u32[]{:S(2)}) collective-permute-start(f32[16,128]{1,0:T(8,128)S(1)} %col_pass.2.refs_4_), channel_id=1, source_target_pairs={{0,32},{32,64},{64,96},{96,0},{1,33},{33,65},{65,97},{97,1},{2,34}... | collective-permute-start | bytes 24584 | tf_op jit(solution)/shard_map/ppermute | solution.py:411
  66.4 0.6 collective-permute-start.17
  67.0 0.5 collective-permute-done.15.refs_5_
  67.5 1.2 collective-permute-done.16.refs_6_
  68.6 1.4 collective-permute-done.17.refs_7_
  70.0 1.8 %row_pass.4 = (bf16[32,16,128]{2,1,0:T(8,128)(2,1)S(1)}, f32[16,128]{1,0:T(8,128)}) custom-call(s32[5]{0:T(128)S(1)} %stack.20.place_ref.refs_0_, f32[2048,512]{1,0:T(8,128)S(1)} %get-tuple-element.52.refs_1_.refs_0_, f32[2048,1024]{1,0:T(8,128)S(1)} %get-tuple-element.61.refs_2_.refs_1_, f32[2048,512]{1,0:T(8,128)S(1)} %get-tuple-element.70.refs_3_.refs_2_, ...), custom_call_target="tpu_custom_call" | custom-call | tf_op jit(solution)/shard_map/row_pass/pallas_call | solution.py:180
  71.8 11.3 %all_to_all.16.refs_3_ = bf16[32,16,128]{2,1,0:T(8,128)(2,1)S(1)} all-to-all(bf16[32,16,128]{2,1,0:T(8,128)(2,1)S(1)} %get-tuple-element.73), channel_id=1, replica_groups=mesh['y'=4,'x'=4,'z'=4,'core'=2] {'x','z','core'}, dimensions={0} | all-to-all | bytes 262144 | tf_op jit(solution)/shard_map/all_to_all | solution.py:457
  83.1 1.8 %col_pass.3.refs_4_ = f32[16,128]{1,0:T(8,128)S(1)} custom-call(s32[5]{0:T(128)S(1)} %stack.20.place_ref.refs_0_, f32[2048,512]{1,0:T(8,128)S(1)} %get-tuple-element.52.refs_1_.refs_0_, f32[2048,1024]{1,0:T(8,128)S(1)} %get-tuple-element.61.refs_2_.refs_1_, f32[2048,512]{1,0:T(8,128)S(1)} %get-tuple-element.70.refs_3_.refs_2_, ...), custom_call_target="tpu_custom_call" | custom-call | tf_op jit(solution)/shard_map/col_pass/pallas_call | solution.py:218
  84.9 0.8 collective-permute-start.18
  85.7 2.0 %collective-permute-start.19 = (f32[16,128]{1,0:T(8,128)S(1)}, f32[16,128]{1,0:T(8,128)S(1)}, u32[]{:S(2)}, u32[]{:S(2)}) collective-permute-start(f32[16,128]{1,0:T(8,128)S(1)} %col_pass.3.refs_4_), channel_id=1, source_target_pairs={{0,32},{32,64},{64,96},{96,0},{1,33},{33,65},{65,97},{97,1},{2,34}... | collective-permute-start | bytes 24584 | tf_op jit(solution)/shard_map/ppermute | solution.py:411
  87.7 1.2 collective-permute-start.20
  88.9 1.2 collective-permute-done.18.refs_5_
  90.1 0.4 collective-permute-done.19.refs_6_
  90.5 0.8 collective-permute-done.20.refs_7_
  91.3 1.8 %row_pass.5 = (bf16[32,16,128]{2,1,0:T(8,128)(2,1)S(1)}, f32[16,128]{1,0:T(8,128)S(1)}) custom-call(s32[5]{0:T(128)S(1)} %stack.20.place_ref.refs_0_, f32[2048,512]{1,0:T(8,128)S(1)} %get-tuple-element.52.refs_1_.refs_0_, f32[2048,1024]{1,0:T(8,128)S(1)} %get-tuple-element.61.refs_2_.refs_1_, f32[2048,512]{1,0:T(8,128)S(1)} %get-tuple-element.70.refs_3_.refs_2_, ...), custom_call_target="tpu_custom_call" | custom-call | tf_op jit(solution)/shard_map/row_pass/pallas_call | solution.py:180
  93.1 11.3 %all_to_all.17.refs_4_ = bf16[32,16,128]{2,1,0:T(8,128)(2,1)S(1)} all-to-all(bf16[32,16,128]{2,1,0:T(8,128)(2,1)S(1)} %get-tuple-element.74), channel_id=1, replica_groups=mesh['y'=4,'x'=4,'z'=4,'core'=2] {'x','z','core'}, dimensions={0} | all-to-all | bytes 262144 | tf_op jit(solution)/shard_map/all_to_all | solution.py:457
  104.4 3.6 %make_plan.2 = (bf16[1024,2048]{1,0:T(8,128)(2,1)S(1)}, f32[8,128]{1,0:T(8,128)S(1)}, bf16[1040,256]{1,0:T(8,128)(2,1)S(1)}, bf16[1040,256]{1,0:T(8,128)(2,1)S(1)}) custom-call(s32[5]{0:T(128)S(1)} %stack.20.place_ref.refs_0_, f32[2048,512]{1,0:T(8,128)S(1)} %get-tuple-element.52.refs_1_.refs_0_, f32[2048,1024]{1,0:T(8,128)S(1)} %get-tuple-element.61.refs_2_.refs_1_, ...), custom_call_target="tpu_custom_call" | custom-call | flops 30000001024 | tf_op jit(solution)/shard_map/make_plan/pallas_call | solution.py:255
  108.0 0.9 collective-permute-start.25
  108.9 2.4 %collective-permute-start.26 = (bf16[1040,256]{1,0:T(8,128)(2,1)S(1)}, bf16[1040,256]{1,0:T(8,128)(2,1)S(1)}, u32[]{:S(2)}, u32[]{:S(2)}) collective-permute-start(bf16[1040,256]{1,0:T(8,128)(2,1)S(1)} %get-tuple-element.92), channel_id=1, source_target_pairs={{0,96},{32,0},{64,32},{96,64},{1,97},{33,1},{65,33},{97,65},{2,98}... | collective-permute-start | bytes 1597448 | tf_op jit(solution)/shard_map/ppermute | solution.py:411
  111.3 3.7 %make_plan.3 = (bf16[1024,2048]{1,0:T(8,128)(2,1)S(1)}, f32[8,128]{1,0:T(8,128)S(1)}, bf16[1040,256]{1,0:T(8,128)(2,1)S(1)}, bf16[1040,256]{1,0:T(8,128)(2,1)S(1)}) custom-call(s32[5]{0:T(128)S(1)} %stack.20.place_ref.refs_0_, f32[2048,512]{1,0:T(8,128)S(1)} %get-tuple-element.52.refs_1_.refs_0_, f32[2048,1024]{1,0:T(8,128)S(1)} %get-tuple-element.61.refs_2_.refs_1_, ...), custom_call_target="tpu_custom_call" | custom-call | flops 30000001024 | tf_op jit(solution)/shard_map/make_plan/pallas_call | solution.py:255
  115.1 3.2 %collective-permute-start.22 = (bf16[1040,256]{1,0:T(8,128)(2,1)S(1)}, bf16[1040,256]{1,0:T(8,128)(2,1)S(1)}, u32[]{:S(2)}, u32[]{:S(2)}) collective-permute-start(bf16[1040,256]{1,0:T(8,128)(2,1)S(1)} %get-tuple-element.82), channel_id=1, source_target_pairs={{0,96},{32,0},{64,32},{96,64},{1,97},{33,1},{65,33},{97,65},{2,98}... | collective-permute-start | bytes 1597448 | tf_op jit(solution)/shard_map/ppermute | solution.py:411
  118.3 6.0 %collective-permute-done.25.from_below.below = bf16[1040,256]{1,0:T(8,128)(2,1)S(1)} collective-permute-done((bf16[1040,256]{1,0:T(8,128)(2,1)S(1)}, bf16[1040,256]{1,0:T(8,128)(2,1)S(1)}, u32[]{:S(2)}, u32[]{:S(2)}) %collective-permute-start.25) | collective-permute-done | bytes 532512 | tf_op jit(solution)/shard_map/ppermute | solution.py:411
  124.3 1.3 late_sums.3
  125.5 0.7 collective-permute-start.27
  126.2 2.7 %collective-permute-start.28 = (bf16[528,256]{1,0:T(8,128)(2,1)S(1)}, bf16[528,256]{1,0:T(8,128)(2,1)S(1)}, u32[]{:S(2)}, u32[]{:S(2)}) collective-permute-start(bf16[528,256]{1,0:T(8,128)(2,1)S(1)} %get-tuple-element.96), channel_id=1, source_target_pairs={{0,96},{32,0},{64,32},{96,64},{1,97},{33,1},{65,33},{97,65},{2,98}... | collective-permute-start | bytes 811016 | tf_op jit(solution)/shard_map/ppermute | solution.py:411
  129.0 6.7 %collective-permute-done.21.from_below.refs_4_ = bf16[1040,256]{1,0:T(8,128)(2,1)S(1)} collective-permute-done((bf16[1040,256]{1,0:T(8,128)(2,1)S(1)}, bf16[1040,256]{1,0:T(8,128)(2,1)S(1)}, u32[]{:S(2)}, u32[]{:S(2)}) %collective-permute-start.21) | collective-permute-done | bytes 532512 | tf_op jit(solution)/shard_map/ppermute | solution.py:411
  135.7 1.3 late_sums.2
  136.9 0.7 collective-permute-start.23
  137.7 2.7 %collective-permute-start.24 = (bf16[528,256]{1,0:T(8,128)(2,1)S(1)}, bf16[528,256]{1,0:T(8,128)(2,1)S(1)}, u32[]{:S(2)}, u32[]{:S(2)}) collective-permute-start(bf16[528,256]{1,0:T(8,128)(2,1)S(1)} %get-tuple-element.88), channel_id=1, source_target_pairs={{0,96},{32,0},{64,32},{96,64},{1,97},{33,1},{65,33},{97,65},{2,98}... | collective-permute-start | bytes 811016 | tf_op jit(solution)/shard_map/ppermute | solution.py:411
  140.4 2.5 %own_sums.3 = (f32[1024,256]{1,0:T(8,128)S(1)}, bf16[1024,256]{1,0:T(8,128)(2,1)S(1)}) custom-call(s32[5]{0:T(128)S(1)} %stack.20.place_ref.refs_0_, bf16[1024,2048]{1,0:T(8,128)(2,1)S(1)} %get-tuple-element.90.plan_ref, bf16[1040,256]{1,0:T(8,128)(2,1)S(1)} %collective-permute-done.25.from_below.below, ...), custom_call_target="tpu_custom_call" | custom-call | flops 30000001024 | tf_op jit(solution)/shard_map/own_sums/pallas_call | solution.py:255
  142.9 1.8 %own_sums.2 = (f32[1024,256]{1,0:T(8,128)S(1)}, bf16[1024,256]{1,0:T(8,128)(2,1)S(1)}) custom-call(s32[5]{0:T(128)S(1)} %stack.20.place_ref.refs_0_, bf16[1024,2048]{1,0:T(8,128)(2,1)S(1)} %get-tuple-element.80.plan_ref, bf16[1040,256]{1,0:T(8,128)(2,1)S(1)} %collective-permute-done.21.from_below.refs_4_, ...), custom_call_target="tpu_custom_call" | custom-call | flops 30000001024 | tf_op jit(solution)/shard_map/own_sums/pallas_call | solution.py:255
  144.7 1.6 %finish.2 = (bf16[2048,256]{1,0:T(8,128)(2,1)}, f32[8,128]{1,0:T(8,128)S(1)}) custom-call(s32[5]{0:T(128)S(1)} %stack.20.place_ref.refs_0_, f32[1024,256]{1,0:T(8,128)S(1)} %get-tuple-element.94.own_ref, f32[16,128]{1,0:T(8,128)S(1)} %get-tuple-element.75.refs_5_.scale_ref.refs_2_, f32[8,128]{1,0:T(8,128)S(1)} %get-tuple-element.79.refs_6_.m_ref, ...), custom_call_target="tpu_custom_call" | custom-call | flops 30000001024 | tf_op jit(solution)/shard_map/finish/pallas_call | solution.py:390
  146.4 1.6 %finish.3 = (bf16[2048,256]{1,0:T(8,128)(2,1)}, f32[8,128]{1,0:T(8,128)S(1)}) custom-call(s32[5]{0:T(128)S(1)} %stack.20.place_ref.refs_0_, f32[1024,256]{1,0:T(8,128)S(1)} %get-tuple-element.85.refs_1_, f32[16,128]{1,0:T(8,128)S(1)} %get-tuple-element.75.refs_5_.scale_ref.refs_2_, ...), custom_call_target="tpu_custom_call", output_to_operand_aliasing={{0}: (10, {})} | custom-call | flops 30000001024 | tf_op jit(solution)/shard_map/finish/pallas_call | solution.py:390
  148.1 0.6 maximum_bitcast_fusion
  (22 shorter events, 0.3 us)
Async XLA Ops:
  0.6 6.9 %collective-permute-start = (bf16[64,1024]{1,0:T(8,128)(2,1)}, bf16[64,1024]{1,0:T(8,128)(2,1)S(1)}, u32[]{:S(2)}, u32[]{:S(2)}) collective-permute-start(bf16[64,1024]{1,0:T(8,128)(2,1)} %x_ref.1), channel_id=1, source_target_pairs={{0,8},{1,3},{2,10},{3,5},{4,12},{5,7},{6,14},{7,1},{8,16},{9,11},{... | collective-permute-start | bytes 393224 | tf_op jit(solution)/shard_map/ppermute | solution.py:424
  2.3 7.3 %collective-permute-start.1 = (bf16[64,1024]{1,0:T(8,128)(2,1)}, bf16[64,1024]{1,0:T(8,128)(2,1)S(1)}, u32[]{:S(2)}, u32[]{:S(2)}) collective-permute-start(bf16[64,1024]{1,0:T(8,128)(2,1)} %x_ref.1), channel_id=1, source_target_pairs={{0,16},{1,5},{2,18},{3,7},{4,20},{5,1},{6,22},{7,3},{8,24},{9,13},... | collective-permute-start | bytes 393224 | tf_op jit(solution)/shard_map/ppermute | solution.py:424
  5.0 5.2 %collective-permute-start.2 = (bf16[64,1024]{1,0:T(8,128)(2,1)}, bf16[64,1024]{1,0:T(8,128)(2,1)S(1)}, u32[]{:S(2)}, u32[]{:S(2)}) collective-permute-start(bf16[64,1024]{1,0:T(8,128)(2,1)} %x_ref.1), channel_id=1, source_target_pairs={{0,24},{1,7},{2,26},{3,1},{4,28},{5,3},{6,30},{7,5},{8,0},{9,15},{... | collective-permute-start | bytes 393224 | tf_op jit(solution)/shard_map/ppermute | solution.py:424
  10.8 4.3 %collective-permute-start.3 = (bf16[256,1024]{1,0:T(8,128)(2,1)S(1)}, bf16[256,1024]{1,0:T(8,128)(2,1)S(1)}, u32[]{:S(2)}, u32[]{:S(2)}) collective-permute-start(bf16[256,1024]{1,0:T(8,128)(2,1)S(1)} %in_order.1.refs_0_), channel_id=1, source_target_pairs={{0,1},{1,0},{2,3},{3,2},{4,5},{5,4},{6,7},{7,6},{8,9},{9,8},{10,11... | collective-permute-start | bytes 1572872 | tf_op jit(solution)/shard_map/ppermute | solution.py:411
  10.9 11.3 %collective-permute-start.4 = (bf16[256,1024]{1,0:T(8,128)(2,1)S(1)}, bf16[256,1024]{1,0:T(8,128)(2,1)S(1)}, u32[]{:S(2)}, u32[]{:S(2)}) collective-permute-start(bf16[256,1024]{1,0:T(8,128)(2,1)S(1)} %in_order.1.refs_0_), channel_id=1, source_target_pairs={{0,2},{1,9},{2,4},{3,11},{4,6},{5,13},{6,0},{7,15},{8,10},{9,17},{... | collective-permute-start | bytes 1572872 | tf_op jit(solution)/shard_map/ppermute | solution.py:424
  12.9 9.3 %collective-permute-start.5 = (bf16[256,1024]{1,0:T(8,128)(2,1)S(1)}, bf16[256,1024]{1,0:T(8,128)(2,1)S(1)}, u32[]{:S(2)}, u32[]{:S(2)}) collective-permute-start(bf16[256,1024]{1,0:T(8,128)(2,1)S(1)} %in_order.1.refs_0_), channel_id=1, source_target_pairs={{0,6},{1,25},{2,0},{3,27},{4,2},{5,29},{6,4},{7,31},{8,14},{9,1},{... | collective-permute-start | bytes 1572872 | tf_op jit(solution)/shard_map/ppermute | solution.py:424
  15.1 2.2 %copy-start = (bf16[2048,1024]{1,0:T(8,128)(2,1)S(1)}, bf16[2048,1024]{1,0:T(8,128)(2,1)}, u32[]{:S(2)}) copy-start(bf16[2048,1024]{1,0:T(8,128)(2,1)} %cents_ref.9) | copy-start | bytes 12582916
  22.1 4.0 %collective-permute-start.6 = (bf16[256,1024]{1,0:T(8,128)(2,1)S(1)}, bf16[256,1024]{1,0:T(8,128)(2,1)S(1)}, u32[]{:S(2)}, u32[]{:S(2)}) collective-permute-start(bf16[256,1024]{1,0:T(8,128)(2,1)S(1)} %collective-permute-done.4.refs_0_), channel_id=1, source_target_pairs={{0,1},{1,0},{2,3},{3,2},{4,5},{5,4},{6,7},{7,6},{8,9},{9,8},{10,11... | collective-permute-start | bytes 1572872 | tf_op jit(solution)/shard_map/ppermute | solution.py:411
  22.1 4.0 %collective-permute-start.7 = (bf16[256,1024]{1,0:T(8,128)(2,1)S(1)}, bf16[256,1024]{1,0:T(8,128)(2,1)S(1)}, u32[]{:S(2)}, u32[]{:S(2)}) collective-permute-start(bf16[256,1024]{1,0:T(8,128)(2,1)S(1)} %collective-permute-done.5.refs_1_), channel_id=1, source_target_pairs={{0,1},{1,0},{2,3},{3,2},{4,5},{5,4},{6,7},{7,6},{8,9},{9,8},{10,11... | collective-permute-start | bytes 1572872 | tf_op jit(solution)/shard_map/ppermute | solution.py:411
  22.7 8.8 %collective-permute-start.8 = (bf16[128,1024]{1,0:T(8,128)(2,1)S(1)}, bf16[128,1024]{1,0:T(8,128)(2,1)S(1)}, u32[]{:S(2)}, u32[]{:S(2)}) collective-permute-start(bf16[128,1024]{1,0:T(8,128)(2,1)S(1)} %slice.6), channel_id=1, source_target_pairs={{0,2},{1,9},{2,4},{3,11},{4,6},{5,13},{6,0},{7,15},{8,10},{9,17},{... | collective-permute-start | bytes 786440 | tf_op jit(solution)/shard_map/ppermute | solution.py:424
  24.6 6.9 %collective-permute-start.9 = (bf16[128,1024]{1,0:T(8,128)(2,1)S(1)}, bf16[128,1024]{1,0:T(8,128)(2,1)S(1)}, u32[]{:S(2)}, u32[]{:S(2)}) collective-permute-start(bf16[128,1024]{1,0:T(8,128)(2,1)S(1)} %slice.7), channel_id=1, source_target_pairs={{0,6},{1,25},{2,0},{3,27},{4,2},{5,29},{6,4},{7,31},{8,14},{9,1},{... | collective-permute-start | bytes 786440 | tf_op jit(solution)/shard_map/ppermute | solution.py:424
  31.5 1.6 %collective-permute-start.10 = (bf16[128,1024]{1,0:T(8,128)(2,1)S(1)}, bf16[128,1024]{1,0:T(8,128)(2,1)S(1)}, u32[]{:S(2)}, u32[]{:S(2)}) collective-permute-start(bf16[128,1024]{1,0:T(8,128)(2,1)S(1)} %collective-permute-done.8.refs_0_), channel_id=1, source_target_pairs={{0,1},{1,0},{2,3},{3,2},{4,5},{5,4},{6,7},{7,6},{8,9},{9,8},{10,11... | collective-permute-start | bytes 786440 | tf_op jit(solution)/shard_map/ppermute | solution.py:411
  31.6 1.9 %collective-permute-start.11 = (bf16[128,1024]{1,0:T(8,128)(2,1)S(1)}, bf16[128,1024]{1,0:T(8,128)(2,1)S(1)}, u32[]{:S(2)}, u32[]{:S(2)}) collective-permute-start(bf16[128,1024]{1,0:T(8,128)(2,1)S(1)} %collective-permute-done.9.refs_1_), channel_id=1, source_target_pairs={{0,1},{1,0},{2,3},{3,2},{4,5},{5,4},{6,7},{7,6},{8,9},{9,8},{10,11... | collective-permute-start | bytes 786440 | tf_op jit(solution)/shard_map/ppermute | solution.py:411
  36.6 6.7 %collective-permute-start.12 = (f32[16,128]{1,0:T(8,128)S(1)}, f32[16,128]{1,0:T(8,128)S(1)}, u32[]{:S(2)}, u32[]{:S(2)}) collective-permute-start(f32[16,128]{1,0:T(8,128)S(1)} %get-tuple-element.71.refs_4_), channel_id=1, source_target_pairs={{0,64},{32,96},{64,0},{96,32},{1,65},{33,97},{65,1},{97,33},{2,66}... | collective-permute-start | bytes 24584 | tf_op jit(solution)/shard_map/ppermute | solution.py:411
  40.0 4.9 %collective-permute-start.13 = (f32[16,128]{1,0:T(8,128)S(1)}, f32[16,128]{1,0:T(8,128)S(1)}, u32[]{:S(2)}, u32[]{:S(2)}) collective-permute-start(f32[16,128]{1,0:T(8,128)S(1)} %get-tuple-element.71.refs_4_), channel_id=1, source_target_pairs={{0,32},{32,64},{64,96},{96,0},{1,33},{33,65},{65,97},{97,1},{2,34}... | collective-permute-start | bytes 24584 | tf_op jit(solution)/shard_map/ppermute | solution.py:411
  40.7 4.2 %collective-permute-start.14 = (f32[16,128]{1,0:T(8,128)S(1)}, f32[16,128]{1,0:T(8,128)S(1)}, u32[]{:S(2)}, u32[]{:S(2)}) collective-permute-start(f32[16,128]{1,0:T(8,128)S(1)} %get-tuple-element.71.refs_4_), channel_id=1, source_target_pairs={{0,96},{32,0},{64,32},{96,64},{1,97},{33,1},{65,33},{97,65},{2,98}... | collective-permute-start | bytes 24584 | tf_op jit(solution)/shard_map/ppermute | solution.py:411
  62.2 5.2 %collective-permute-start.15 = (f32[16,128]{1,0:T(8,128)S(1)}, f32[16,128]{1,0:T(8,128)S(1)}, u32[]{:S(2)}, u32[]{:S(2)}) collective-permute-start(f32[16,128]{1,0:T(8,128)S(1)} %col_pass.2.refs_4_), channel_id=1, source_target_pairs={{0,64},{32,96},{64,0},{96,32},{1,65},{33,97},{65,1},{97,33},{2,66}... | collective-permute-start | bytes 24584 | tf_op jit(solution)/shard_map/ppermute | solution.py:411
  63.8 4.9 %collective-permute-start.16 = (f32[16,128]{1,0:T(8,128)S(1)}, f32[16,128]{1,0:T(8,128)S(1)}, u32[]{:S(2)}, u32[]{:S(2)}) collective-permute-start(f32[16,128]{1,0:T(8,128)S(1)} %col_pass.2.refs_4_), channel_id=1, source_target_pairs={{0,32},{32,64},{64,96},{96,0},{1,33},{33,65},{65,97},{97,1},{2,34}... | collective-permute-start | bytes 24584 | tf_op jit(solution)/shard_map/ppermute | solution.py:411
  66.4 3.7 %collective-permute-start.17 = (f32[16,128]{1,0:T(8,128)S(1)}, f32[16,128]{1,0:T(8,128)S(1)}, u32[]{:S(2)}, u32[]{:S(2)}) collective-permute-start(f32[16,128]{1,0:T(8,128)S(1)} %col_pass.2.refs_4_), channel_id=1, source_target_pairs={{0,96},{32,0},{64,32},{96,64},{1,97},{33,1},{65,33},{97,65},{2,98}... | collective-permute-start | bytes 24584 | tf_op jit(solution)/shard_map/ppermute | solution.py:411
  84.9 5.2 %collective-permute-start.18 = (f32[16,128]{1,0:T(8,128)S(1)}, f32[16,128]{1,0:T(8,128)S(1)}, u32[]{:S(2)}, u32[]{:S(2)}) collective-permute-start(f32[16,128]{1,0:T(8,128)S(1)} %col_pass.3.refs_4_), channel_id=1, source_target_pairs={{0,64},{32,96},{64,0},{96,32},{1,65},{33,97},{65,1},{97,33},{2,66}... | collective-permute-start | bytes 24584 | tf_op jit(solution)/shard_map/ppermute | solution.py:411
  85.7 4.9 %collective-permute-start.19 = (f32[16,128]{1,0:T(8,128)S(1)}, f32[16,128]{1,0:T(8,128)S(1)}, u32[]{:S(2)}, u32[]{:S(2)}) collective-permute-start(f32[16,128]{1,0:T(8,128)S(1)} %col_pass.3.refs_4_), channel_id=1, source_target_pairs={{0,32},{32,64},{64,96},{96,0},{1,33},{33,65},{65,97},{97,1},{2,34}... | collective-permute-start | bytes 24584 | tf_op jit(solution)/shard_map/ppermute | solution.py:411
  87.7 3.7 %collective-permute-start.20 = (f32[16,128]{1,0:T(8,128)S(1)}, f32[16,128]{1,0:T(8,128)S(1)}, u32[]{:S(2)}, u32[]{:S(2)}) collective-permute-start(f32[16,128]{1,0:T(8,128)S(1)} %col_pass.3.refs_4_), channel_id=1, source_target_pairs={{0,96},{32,0},{64,32},{96,64},{1,97},{33,1},{65,33},{97,65},{2,98}... | collective-permute-start | bytes 24584 | tf_op jit(solution)/shard_map/ppermute | solution.py:411
  108.0 16.2 %collective-permute-start.25 = (bf16[1040,256]{1,0:T(8,128)(2,1)S(1)}, bf16[1040,256]{1,0:T(8,128)(2,1)S(1)}, u32[]{:S(2)}, u32[]{:S(2)}) collective-permute-start(bf16[1040,256]{1,0:T(8,128)(2,1)S(1)} %get-tuple-element.91), channel_id=1, source_target_pairs={{0,32},{32,64},{64,96},{96,0},{1,33},{33,65},{65,97},{97,1},{2,34}... | collective-permute-start | bytes 1597448 | tf_op jit(solution)/shard_map/ppermute | solution.py:411
  108.9 15.3 %collective-permute-start.26 = (bf16[1040,256]{1,0:T(8,128)(2,1)S(1)}, bf16[1040,256]{1,0:T(8,128)(2,1)S(1)}, u32[]{:S(2)}, u32[]{:S(2)}) collective-permute-start(bf16[1040,256]{1,0:T(8,128)(2,1)S(1)} %get-tuple-element.92), channel_id=1, source_target_pairs={{0,96},{32,0},{64,32},{96,64},{1,97},{33,1},{65,33},{97,65},{2,98}... | collective-permute-start | bytes 1597448 | tf_op jit(solution)/shard_map/ppermute | solution.py:411
  115.0 20.7 %collective-permute-start.21 = (bf16[1040,256]{1,0:T(8,128)(2,1)S(1)}, bf16[1040,256]{1,0:T(8,128)(2,1)S(1)}, u32[]{:S(2)}, u32[]{:S(2)}) collective-permute-start(bf16[1040,256]{1,0:T(8,128)(2,1)S(1)} %get-tuple-element.81), channel_id=1, source_target_pairs={{0,32},{32,64},{64,96},{96,0},{1,33},{33,65},{65,97},{97,1},{2,34}... | collective-permute-start | bytes 1597448 | tf_op jit(solution)/shard_map/ppermute | solution.py:411
  115.1 20.6 %collective-permute-start.22 = (bf16[1040,256]{1,0:T(8,128)(2,1)S(1)}, bf16[1040,256]{1,0:T(8,128)(2,1)S(1)}, u32[]{:S(2)}, u32[]{:S(2)}) collective-permute-start(bf16[1040,256]{1,0:T(8,128)(2,1)S(1)} %get-tuple-element.82), channel_id=1, source_target_pairs={{0,96},{32,0},{64,32},{96,64},{1,97},{33,1},{65,33},{97,65},{2,98}... | collective-permute-start | bytes 1597448 | tf_op jit(solution)/shard_map/ppermute | solution.py:411
  125.5 19.2 %collective-permute-start.27 = (bf16[528,256]{1,0:T(8,128)(2,1)S(1)}, bf16[528,256]{1,0:T(8,128)(2,1)S(1)}, u32[]{:S(2)}, u32[]{:S(2)}) collective-permute-start(bf16[528,256]{1,0:T(8,128)(2,1)S(1)} %get-tuple-element.95), channel_id=1, source_target_pairs={{0,32},{32,64},{64,96},{96,0},{1,33},{33,65},{65,97},{97,1},{2,34}... | collective-permute-start | bytes 811016 | tf_op jit(solution)/shard_map/ppermute | solution.py:411
  126.2 18.5 %collective-permute-start.28 = (bf16[528,256]{1,0:T(8,128)(2,1)S(1)}, bf16[528,256]{1,0:T(8,128)(2,1)S(1)}, u32[]{:S(2)}, u32[]{:S(2)}) collective-permute-start(bf16[528,256]{1,0:T(8,128)(2,1)S(1)} %get-tuple-element.96), channel_id=1, source_target_pairs={{0,96},{32,0},{64,32},{96,64},{1,97},{33,1},{65,33},{97,65},{2,98}... | collective-permute-start | bytes 811016 | tf_op jit(solution)/shard_map/ppermute | solution.py:411
  136.9 9.5 %collective-permute-start.23 = (bf16[528,256]{1,0:T(8,128)(2,1)S(1)}, bf16[528,256]{1,0:T(8,128)(2,1)S(1)}, u32[]{:S(2)}, u32[]{:S(2)}) collective-permute-start(bf16[528,256]{1,0:T(8,128)(2,1)S(1)} %get-tuple-element.87), channel_id=1, source_target_pairs={{0,32},{32,64},{64,96},{96,0},{1,33},{33,65},{65,97},{97,1},{2,34}... | collective-permute-start | bytes 811016 | tf_op jit(solution)/shard_map/ppermute | solution.py:411
  137.7 8.8 %collective-permute-start.24 = (bf16[528,256]{1,0:T(8,128)(2,1)S(1)}, bf16[528,256]{1,0:T(8,128)(2,1)S(1)}, u32[]{:S(2)}, u32[]{:S(2)}) collective-permute-start(bf16[528,256]{1,0:T(8,128)(2,1)S(1)} %get-tuple-element.88), channel_id=1, source_target_pairs={{0,96},{32,0},{64,32},{96,64},{1,97},{33,1},{65,33},{97,65},{2,98}... | collective-permute-start | bytes 811016 | tf_op jit(solution)/shard_map/ppermute | solution.py:411

commit v4 on v3

--- a/solution.py
+++ b/solution.py
@@ -16,6 +16,7 @@
 PLACES = 4
 PLANES = 4
 LINES = 2
+SPARE = 8
 ORDER = ((True, 0), (False, 0), (True, 1), (True, 3), (False, 1), (False, 3), (True, 2), (False, 2))
 PARTS = 3
 FLOPS = 3 * 10**10
@@ -169,7 +170,7 @@
     for block, (mine, turn) in enumerate(ORDER):
         pair = [jnp.sum(a, axis=0, keepdims=True) for a in accs[block * LINES : (block + 1) * LINES]]
         lines_ref[pl.ds(line_of(place_ref, mine, turn), LINES), :] = jnp.concatenate(pair, axis=0)
-    value = lines_ref[...].astype(out_ref.dtype)
+    value = lines_ref[: out_ref.shape[1], :].astype(out_ref.dtype)
     for q in range(out_ref.shape[0]):
         out_ref[q] = value
 
@@ -185,7 +186,7 @@
             jax.ShapeDtypeStruct((peers, lines, LANES), jnp.bfloat16),
             jax.ShapeDtypeStruct((n // LANES, LANES), jnp.float32),
         ],
-        scratch_shapes=[pltpu.VMEM((lines, LANES), jnp.float32)],
+        scratch_shapes=[pltpu.VMEM((lines + SPARE, LANES), jnp.float32)],
         compiler_params=params(8 * 1024 * 1024),
         name="row_pass",
     )(place, *[held(x) for x in w], *masses)
@@ -195,7 +196,7 @@
     total = sums_ref[0].astype(jnp.float32)
     for q in range(1, sums_ref.shape[0]):
         total = total + sums_ref[q].astype(jnp.float32)
-    lines_ref[...] = 1.0 / total
+    lines_ref[: total.shape[0], :] = 1.0 / total
     scale = [lines_ref[pl.ds(line_of(place_ref, mine, turn), LINES), :] for mine, turn in ORDER]
     return [pair[i : i + 1, :] for pair in scale for i in range(LINES)]
 
@@ -220,7 +221,7 @@
         in_specs=[SM] + [VM] * (PARTS + 1),
         out_specs=VM,
         out_shape=jax.ShapeDtypeStruct((n // LANES, LANES), jnp.float32),
-        scratch_shapes=[pltpu.VMEM(sums.shape[1:], jnp.float32)],
+        scratch_shapes=[pltpu.VMEM((sums.shape[1] + SPARE, LANES), jnp.float32)],
         compiler_params=params(8 * 1024 * 1024),
         name="col_pass",
     )(place, *[held(x) for x in w], sums)
@@ -301,7 +302,7 @@
         [SM] + [VM] * (PARTS + 6),
         [pltpu.VMEM((n // 2, m), jnp.bfloat16), jax.ShapeDtypeStruct((n // 2 // LANES, LANES), jnp.float32), part, part],
         (place, *[held(x) for x in w], sums, scale, mark, *[held(v) for v in cuts[1:]]),
-        [pltpu.VMEM(sums.shape[1:], jnp.float32)],
+        [pltpu.VMEM((sums.shape[1] + SPARE, LANES), jnp.float32)],
     )
 
 

time: 149 us -> 149 us (level)
  no operation moved by 1% of the time
where the time goes in v4:
time: 149 us
  starting transfers between devices  43.5 us (29%)
  Pallas kernels  39.2 us (26%)
  blocking collectives  36.3 us (24%)
  waiting for transfers between devices  25.8 us (17%)
  local copies, waits for them, and re-layouts  2.31 us (2%)
    all_to_all x3, blocking collectives, body(): sums = lax.all_to_all(sums, CENTS, 0, 0, tiled=True)  36.3 us
    ppermute x22, starting transfers between devices, move(): return lax.ppermute(x, axis, [(i, (i + by) % n) for i in range(n)])  30.1 us
    ppermute x22, waiting for transfers between devices, move(): return lax.ppermute(x, axis, [(i, (i + by) % n) for i in range(n)])  21.2 us
    pallas_call x6, Pallas kernels, call(): pl.pallas_call(kernel, in_specs=specs, out_specs=[VM] * len(out_shape), o...  14.1 us
    ppermute x7, starting transfers between devices, spread(): return lax.ppermute(x, CENTS, pairs)  13.5 us
    pallas_call x3, Pallas kernels, weigh(): pl.pallas_call(functools.partial(weigh_kernel, len(blocks), at, last), in...  11.3 us
    pallas_call x3, Pallas kernels, row_pass(): pl.pallas_call(lambda *refs: row_kernel(target, *refs), in_specs=[SM] + [...  5.37 us
    ppermute x7, waiting for transfers between devices, spread(): return lax.ppermute(x, CENTS, pairs)  4.61 us
  transfers between devices with their start and end apart: 29, of which 15 were waited for; matrix products, arithmetic and copies ran while one was open for 0% of the time, Pallas kernels for 14%

profile of v4, /device:TPU:0, one launch (start us, length us, event | category | flops | bytes accessed | tf_op | source)
XLA Modules:
  0.0 148.7 jit_solution(17310397231781193420)
XLA Ops:
  0.6 1.6 %collective-permute-start = (bf16[64,1024]{1,0:T(8,128)(2,1)}, bf16[64,1024]{1,0:T(8,128)(2,1)S(1)}, u32[]{:S(2)}, u32[]{:S(2)}) collective-permute-start(bf16[64,1024]{1,0:T(8,128)(2,1)} %x_ref.1), channel_id=1, source_target_pairs={{0,8},{1,3},{2,10},{3,5},{4,12},{5,7},{6,14},{7,1},{8,16},{9,11},{... | collective-permute-start | bytes 393224 | tf_op jit(solution)/shard_map/ppermute | solution.py:425
  2.3 2.7 %collective-permute-start.1 = (bf16[64,1024]{1,0:T(8,128)(2,1)}, bf16[64,1024]{1,0:T(8,128)(2,1)S(1)}, u32[]{:S(2)}, u32[]{:S(2)}) collective-permute-start(bf16[64,1024]{1,0:T(8,128)(2,1)} %x_ref.1), channel_id=1, source_target_pairs={{0,16},{1,5},{2,18},{3,7},{4,20},{5,1},{6,22},{7,3},{8,24},{9,13},... | collective-permute-start | bytes 393224 | tf_op jit(solution)/shard_map/ppermute | solution.py:425
  5.0 1.4 collective-permute-start.2
  6.4 0.9 lift.1.refs_0_
  7.4 0.1 stack.20.place_ref.refs_0_
  7.5 2.1 %collective-permute-done.1.refs_2_ = bf16[64,1024]{1,0:T(8,128)(2,1)S(1)} collective-permute-done((bf16[64,1024]{1,0:T(8,128)(2,1)}, bf16[64,1024]{1,0:T(8,128)(2,1)S(1)}, u32[]{:S(2)}, u32[]{:S(2)}) %collective-permute-start.1) | collective-permute-done | bytes 131104 | tf_op jit(solution)/shard_map/ppermute | solution.py:425
  9.6 0.6 collective-permute-done.2.refs_3_
  10.2 0.6 in_order.1.refs_0_
  10.8 0.1 collective-permute-start.3
  10.9 2.0 %collective-permute-start.4 = (bf16[256,1024]{1,0:T(8,128)(2,1)S(1)}, bf16[256,1024]{1,0:T(8,128)(2,1)S(1)}, u32[]{:S(2)}, u32[]{:S(2)}) collective-permute-start(bf16[256,1024]{1,0:T(8,128)(2,1)S(1)} %in_order.1.refs_0_), channel_id=1, source_target_pairs={{0,2},{1,9},{2,4},{3,11},{4,6},{5,13},{6,0},{7,15},{8,10},{9,17},{... | collective-permute-start | bytes 1572872 | tf_op jit(solution)/shard_map/ppermute | solution.py:425
  12.9 2.2 %collective-permute-start.5 = (bf16[256,1024]{1,0:T(8,128)(2,1)S(1)}, bf16[256,1024]{1,0:T(8,128)(2,1)S(1)}, u32[]{:S(2)}, u32[]{:S(2)}) collective-permute-start(bf16[256,1024]{1,0:T(8,128)(2,1)S(1)} %in_order.1.refs_0_), channel_id=1, source_target_pairs={{0,6},{1,25},{2,0},{3,27},{4,2},{5,29},{6,4},{7,31},{8,14},{9,1},{... | collective-permute-start | bytes 1572872 | tf_op jit(solution)/shard_map/ppermute | solution.py:425
  15.1 2.2 %copy-done = bf16[2048,1024]{1,0:T(8,128)(2,1)S(1)} copy-done((bf16[2048,1024]{1,0:T(8,128)(2,1)S(1)}, bf16[2048,1024]{1,0:T(8,128)(2,1)}, u32[]{:S(2)}) %copy-start) | copy-done | bytes 4194328
  17.2 3.0 %weigh.3 = (f32[2048,512]{1,0:T(8,128)S(1)}, bf16[2048,256]{1,0:T(8,128)(2,1)S(1)}, bf16[2048,256]{1,0:T(8,128)(2,1)S(1)}, bf16[2048,256]{1,0:T(8,128)(2,1)S(1)}...) custom-call(s32[5]{0:T(128)S(1)} %stack.20.place_ref.refs_0_, bf16[2048,1024]{1,0:T(8,128)(2,1)S(1)} %copy-done, ...), custom_call_target="tpu_custom_call" | custom-call | flops 30000001024 | tf_op jit(solution)/shard_map/weigh/pallas_call | solution.py:126
  20.2 1.9 %collective-permute-done.4.refs_0_ = bf16[256,1024]{1,0:T(8,128)(2,1)S(1)} collective-permute-done((bf16[256,1024]{1,0:T(8,128)(2,1)S(1)}, bf16[256,1024]{1,0:T(8,128)(2,1)S(1)}, u32[]{:S(2)}, u32[]{:S(2)}) %collective-permute-start.4) | collective-permute-done | bytes 524320 | tf_op jit(solution)/shard_map/ppermute | solution.py:425
  22.1 0.5 collective-permute-start.7
  22.7 1.9 %collective-permute-start.8 = (bf16[128,1024]{1,0:T(8,128)(2,1)S(1)}, bf16[128,1024]{1,0:T(8,128)(2,1)S(1)}, u32[]{:S(2)}, u32[]{:S(2)}) collective-permute-start(bf16[128,1024]{1,0:T(8,128)(2,1)S(1)} %slice.6), channel_id=1, source_target_pairs={{0,2},{1,9},{2,4},{3,11},{4,6},{5,13},{6,0},{7,15},{8,10},{9,17},{... | collective-permute-start | bytes 786440 | tf_op jit(solution)/shard_map/ppermute | solution.py:425
  24.6 1.6 %collective-permute-start.9 = (bf16[128,1024]{1,0:T(8,128)(2,1)S(1)}, bf16[128,1024]{1,0:T(8,128)(2,1)S(1)}, u32[]{:S(2)}, u32[]{:S(2)}) collective-permute-start(bf16[128,1024]{1,0:T(8,128)(2,1)S(1)} %slice.7), channel_id=1, source_target_pairs={{0,6},{1,25},{2,0},{3,27},{4,2},{5,29},{6,4},{7,31},{8,14},{9,1},{... | collective-permute-start | bytes 786440 | tf_op jit(solution)/shard_map/ppermute | solution.py:425
  26.2 5.3 %weigh.4 = (f32[2048,1024]{1,0:T(8,128)S(1)}, bf16[2048,256]{1,0:T(8,128)(2,1)S(1)}, bf16[2048,256]{1,0:T(8,128)(2,1)S(1)}, bf16[2048,256]{1,0:T(8,128)(2,1)S(1)...) custom-call(s32[5]{0:T(128)S(1)} %stack.20.place_ref.refs_0_, ...), custom_call_target="tpu_custom_call", output_to_operand_aliasing={{1}: (6, {}), {2}: (7, {}), {3}: (8, {}), {4}: (9, {}), {5}... | custom-call | flops 30000001024 | tf_op jit(solution)/shard_map/weigh/pallas_call | solution.py:126
  31.6 0.5 collective-permute-start.11
  32.1 1.0 collective-permute-done.10.refs_2_
  33.1 0.4 collective-permute-done.11.refs_3_
  33.5 3.1 %weigh.5 = (f32[2048,512]{1,0:T(8,128)S(1)}, bf16[2048,256]{1,0:T(8,128)(2,1)S(1)}, bf16[2048,256]{1,0:T(8,128)(2,1)S(1)}, bf16[2048,256]{1,0:T(8,128)(2,1)S(1)}...) custom-call(s32[5]{0:T(128)S(1)} %stack.20.place_ref.refs_0_, ...), custom_call_target="tpu_custom_call", output_to_operand_aliasing={{1}: (6, {}), {2}: (7, {}), {3}: (8, {}), {4}: (9, {}), {5}... | custom-call | flops 30000001024 | tf_op jit(solution)/shard_map/weigh/pallas_call | solution.py:126
  36.6 3.4 %collective-permute-start.12 = (f32[16,128]{1,0:T(8,128)S(1)}, f32[16,128]{1,0:T(8,128)S(1)}, u32[]{:S(2)}, u32[]{:S(2)}) collective-permute-start(f32[16,128]{1,0:T(8,128)S(1)} %get-tuple-element.71.refs_4_), channel_id=1, source_target_pairs={{0,64},{32,96},{64,0},{96,32},{1,65},{33,97},{65,1},{97,33},{2,66}... | collective-permute-start | bytes 24584 | tf_op jit(solution)/shard_map/ppermute | solution.py:412
  40.0 0.7 collective-permute-start.13
  40.7 2.6 %collective-permute-start.14 = (f32[16,128]{1,0:T(8,128)S(1)}, f32[16,128]{1,0:T(8,128)S(1)}, u32[]{:S(2)}, u32[]{:S(2)}) collective-permute-start(f32[16,128]{1,0:T(8,128)S(1)} %get-tuple-element.71.refs_4_), channel_id=1, source_target_pairs={{0,96},{32,0},{64,32},{96,64},{1,97},{33,1},{65,33},{97,65},{2,98}... | collective-permute-start | bytes 24584 | tf_op jit(solution)/shard_map/ppermute | solution.py:412
  43.3 1.6 %collective-permute-done.13.refs_6_ = f32[16,128]{1,0:T(8,128)S(1)} collective-permute-done((f32[16,128]{1,0:T(8,128)S(1)}, f32[16,128]{1,0:T(8,128)S(1)}, u32[]{:S(2)}, u32[]{:S(2)}) %collective-permute-start.13) | collective-permute-done | bytes 8224 | tf_op jit(solution)/shard_map/ppermute | solution.py:412
  44.9 1.8 %row_pass.3 = (bf16[32,16,128]{2,1,0:T(8,128)(2,1)S(1)}, f32[16,128]{1,0:T(8,128)}) custom-call(s32[5]{0:T(128)S(1)} %stack.20.place_ref.refs_0_, f32[2048,512]{1,0:T(8,128)S(1)} %get-tuple-element.52.refs_1_.refs_0_, f32[2048,1024]{1,0:T(8,128)S(1)} %get-tuple-element.61.refs_2_.refs_1_, f32[2048,512]{1,0:T(8,128)S(1)} %get-tuple-element.70.refs_3_.refs_2_, ...), custom_call_target="tpu_custom_call" | custom-call | tf_op jit(solution)/shard_map/row_pass/pallas_call | solution.py:181
  46.7 13.8 %all_to_all.15.refs_3_ = bf16[32,16,128]{2,1,0:T(8,128)(2,1)S(1)} all-to-all(bf16[32,16,128]{2,1,0:T(8,128)(2,1)S(1)} %get-tuple-element.72), channel_id=1, replica_groups=mesh['y'=4,'x'=4,'z'=4,'core'=2] {'x','z','core'}, dimensions={0} | all-to-all | bytes 262144 | tf_op jit(solution)/shard_map/all_to_all | solution.py:458
  60.4 1.8 %col_pass.2.refs_4_ = f32[16,128]{1,0:T(8,128)S(1)} custom-call(s32[5]{0:T(128)S(1)} %stack.20.place_ref.refs_0_, f32[2048,512]{1,0:T(8,128)S(1)} %get-tuple-element.52.refs_1_.refs_0_, f32[2048,1024]{1,0:T(8,128)S(1)} %get-tuple-element.61.refs_2_.refs_1_, f32[2048,512]{1,0:T(8,128)S(1)} %get-tuple-element.70.refs_3_.refs_2_, ...), custom_call_target="tpu_custom_call" | custom-call | tf_op jit(solution)/shard_map/col_pass/pallas_call | solution.py:219
  62.2 1.5 %collective-permute-start.15 = (f32[16,128]{1,0:T(8,128)S(1)}, f32[16,128]{1,0:T(8,128)S(1)}, u32[]{:S(2)}, u32[]{:S(2)}) collective-permute-start(f32[16,128]{1,0:T(8,128)S(1)} %col_pass.2.refs_4_), channel_id=1, source_target_pairs={{0,64},{32,96},{64,0},{96,32},{1,65},{33,97},{65,1},{97,33},{2,66}... | collective-permute-start | bytes 24584 | tf_op jit(solution)/shard_map/ppermute | solution.py:412
  63.8 2.6 %collective-permute-start.16 = (f32[16,128]{1,0:T(8,128)S(1)}, f32[16,128]{1,0:T(8,128)S(1)}, u32[]{:S(2)}, u32[]{:S(2)}) collective-permute-start(f32[16,128]{1,0:T(8,128)S(1)} %col_pass.2.refs_4_), channel_id=1, source_target_pairs={{0,32},{32,64},{64,96},{96,0},{1,33},{33,65},{65,97},{97,1},{2,34}... | collective-permute-start | bytes 24584 | tf_op jit(solution)/shard_map/ppermute | solution.py:412
  66.4 0.6 collective-permute-start.17
  67.0 0.5 collective-permute-done.15.refs_5_
  67.5 1.2 collective-permute-done.16.refs_6_
  68.6 1.4 collective-permute-done.17.refs_7_
  70.0 1.8 %row_pass.4 = (bf16[32,16,128]{2,1,0:T(8,128)(2,1)S(1)}, f32[16,128]{1,0:T(8,128)}) custom-call(s32[5]{0:T(128)S(1)} %stack.20.place_ref.refs_0_, f32[2048,512]{1,0:T(8,128)S(1)} %get-tuple-element.52.refs_1_.refs_0_, f32[2048,1024]{1,0:T(8,128)S(1)} %get-tuple-element.61.refs_2_.refs_1_, f32[2048,512]{1,0:T(8,128)S(1)} %get-tuple-element.70.refs_3_.refs_2_, ...), custom_call_target="tpu_custom_call" | custom-call | tf_op jit(solution)/shard_map/row_pass/pallas_call | solution.py:181
  71.8 11.3 %all_to_all.16.refs_3_ = bf16[32,16,128]{2,1,0:T(8,128)(2,1)S(1)} all-to-all(bf16[32,16,128]{2,1,0:T(8,128)(2,1)S(1)} %get-tuple-element.73), channel_id=1, replica_groups=mesh['y'=4,'x'=4,'z'=4,'core'=2] {'x','z','core'}, dimensions={0} | all-to-all | bytes 262144 | tf_op jit(solution)/shard_map/all_to_all | solution.py:458
  83.1 1.8 %col_pass.3.refs_4_ = f32[16,128]{1,0:T(8,128)S(1)} custom-call(s32[5]{0:T(128)S(1)} %stack.20.place_ref.refs_0_, f32[2048,512]{1,0:T(8,128)S(1)} %get-tuple-element.52.refs_1_.refs_0_, f32[2048,1024]{1,0:T(8,128)S(1)} %get-tuple-element.61.refs_2_.refs_1_, f32[2048,512]{1,0:T(8,128)S(1)} %get-tuple-element.70.refs_3_.refs_2_, ...), custom_call_target="tpu_custom_call" | custom-call | tf_op jit(solution)/shard_map/col_pass/pallas_call | solution.py:219
  84.9 0.8 collective-permute-start.18
  85.7 2.0 %collective-permute-start.19 = (f32[16,128]{1,0:T(8,128)S(1)}, f32[16,128]{1,0:T(8,128)S(1)}, u32[]{:S(2)}, u32[]{:S(2)}) collective-permute-start(f32[16,128]{1,0:T(8,128)S(1)} %col_pass.3.refs_4_), channel_id=1, source_target_pairs={{0,32},{32,64},{64,96},{96,0},{1,33},{33,65},{65,97},{97,1},{2,34}... | collective-permute-start | bytes 24584 | tf_op jit(solution)/shard_map/ppermute | solution.py:412
  87.7 1.2 collective-permute-start.20
  88.9 1.2 collective-permute-done.18.refs_5_
  90.1 0.4 collective-permute-done.19.refs_6_
  90.5 0.8 collective-permute-done.20.refs_7_
  91.3 1.8 %row_pass.5 = (bf16[32,16,128]{2,1,0:T(8,128)(2,1)S(1)}, f32[16,128]{1,0:T(8,128)S(1)}) custom-call(s32[5]{0:T(128)S(1)} %stack.20.place_ref.refs_0_, f32[2048,512]{1,0:T(8,128)S(1)} %get-tuple-element.52.refs_1_.refs_0_, f32[2048,1024]{1,0:T(8,128)S(1)} %get-tuple-element.61.refs_2_.refs_1_, f32[2048,512]{1,0:T(8,128)S(1)} %get-tuple-element.70.refs_3_.refs_2_, ...), custom_call_target="tpu_custom_call" | custom-call | tf_op jit(solution)/shard_map/row_pass/pallas_call | solution.py:181
  93.1 11.3 %all_to_all.17.refs_4_ = bf16[32,16,128]{2,1,0:T(8,128)(2,1)S(1)} all-to-all(bf16[32,16,128]{2,1,0:T(8,128)(2,1)S(1)} %get-tuple-element.74), channel_id=1, replica_groups=mesh['y'=4,'x'=4,'z'=4,'core'=2] {'x','z','core'}, dimensions={0} | all-to-all | bytes 262144 | tf_op jit(solution)/shard_map/all_to_all | solution.py:458
  104.4 3.7 %make_plan.2 = (bf16[1024,2048]{1,0:T(8,128)(2,1)S(1)}, f32[8,128]{1,0:T(8,128)S(1)}, bf16[1040,256]{1,0:T(8,128)(2,1)S(1)}, bf16[1040,256]{1,0:T(8,128)(2,1)S(1)}) custom-call(s32[5]{0:T(128)S(1)} %stack.20.place_ref.refs_0_, f32[2048,512]{1,0:T(8,128)S(1)} %get-tuple-element.52.refs_1_.refs_0_, f32[2048,1024]{1,0:T(8,128)S(1)} %get-tuple-element.61.refs_2_.refs_1_, ...), custom_call_target="tpu_custom_call" | custom-call | flops 30000001024 | tf_op jit(solution)/shard_map/make_plan/pallas_call | solution.py:256
  108.0 0.9 collective-permute-start.25
  108.9 2.4 %collective-permute-start.26 = (bf16[1040,256]{1,0:T(8,128)(2,1)S(1)}, bf16[1040,256]{1,0:T(8,128)(2,1)S(1)}, u32[]{:S(2)}, u32[]{:S(2)}) collective-permute-start(bf16[1040,256]{1,0:T(8,128)(2,1)S(1)} %get-tuple-element.92), channel_id=1, source_target_pairs={{0,96},{32,0},{64,32},{96,64},{1,97},{33,1},{65,33},{97,65},{2,98}... | collective-permute-start | bytes 1597448 | tf_op jit(solution)/shard_map/ppermute | solution.py:412
  111.3 3.7 %make_plan.3 = (bf16[1024,2048]{1,0:T(8,128)(2,1)S(1)}, f32[8,128]{1,0:T(8,128)S(1)}, bf16[1040,256]{1,0:T(8,128)(2,1)S(1)}, bf16[1040,256]{1,0:T(8,128)(2,1)S(1)}) custom-call(s32[5]{0:T(128)S(1)} %stack.20.place_ref.refs_0_, f32[2048,512]{1,0:T(8,128)S(1)} %get-tuple-element.52.refs_1_.refs_0_, f32[2048,1024]{1,0:T(8,128)S(1)} %get-tuple-element.61.refs_2_.refs_1_, ...), custom_call_target="tpu_custom_call" | custom-call | flops 30000001024 | tf_op jit(solution)/shard_map/make_plan/pallas_call | solution.py:256
  115.1 3.2 %collective-permute-start.22 = (bf16[1040,256]{1,0:T(8,128)(2,1)S(1)}, bf16[1040,256]{1,0:T(8,128)(2,1)S(1)}, u32[]{:S(2)}, u32[]{:S(2)}) collective-permute-start(bf16[1040,256]{1,0:T(8,128)(2,1)S(1)} %get-tuple-element.82), channel_id=1, source_target_pairs={{0,96},{32,0},{64,32},{96,64},{1,97},{33,1},{65,33},{97,65},{2,98}... | collective-permute-start | bytes 1597448 | tf_op jit(solution)/shard_map/ppermute | solution.py:412
  118.3 6.0 %collective-permute-done.25.from_below.below = bf16[1040,256]{1,0:T(8,128)(2,1)S(1)} collective-permute-done((bf16[1040,256]{1,0:T(8,128)(2,1)S(1)}, bf16[1040,256]{1,0:T(8,128)(2,1)S(1)}, u32[]{:S(2)}, u32[]{:S(2)}) %collective-permute-start.25) | collective-permute-done | bytes 532512 | tf_op jit(solution)/shard_map/ppermute | solution.py:412
  124.3 1.3 late_sums.3
  125.5 0.7 collective-permute-start.27
  126.2 2.7 %collective-permute-start.28 = (bf16[528,256]{1,0:T(8,128)(2,1)S(1)}, bf16[528,256]{1,0:T(8,128)(2,1)S(1)}, u32[]{:S(2)}, u32[]{:S(2)}) collective-permute-start(bf16[528,256]{1,0:T(8,128)(2,1)S(1)} %get-tuple-element.96), channel_id=1, source_target_pairs={{0,96},{32,0},{64,32},{96,64},{1,97},{33,1},{65,33},{97,65},{2,98}... | collective-permute-start | bytes 811016 | tf_op jit(solution)/shard_map/ppermute | solution.py:412
  129.0 6.7 %collective-permute-done.21.from_below.refs_4_ = bf16[1040,256]{1,0:T(8,128)(2,1)S(1)} collective-permute-done((bf16[1040,256]{1,0:T(8,128)(2,1)S(1)}, bf16[1040,256]{1,0:T(8,128)(2,1)S(1)}, u32[]{:S(2)}, u32[]{:S(2)}) %collective-permute-start.21) | collective-permute-done | bytes 532512 | tf_op jit(solution)/shard_map/ppermute | solution.py:412
  135.7 1.3 late_sums.2
  137.0 0.7 collective-permute-start.23
  137.7 2.7 %collective-permute-start.24 = (bf16[528,256]{1,0:T(8,128)(2,1)S(1)}, bf16[528,256]{1,0:T(8,128)(2,1)S(1)}, u32[]{:S(2)}, u32[]{:S(2)}) collective-permute-start(bf16[528,256]{1,0:T(8,128)(2,1)S(1)} %get-tuple-element.88), channel_id=1, source_target_pairs={{0,96},{32,0},{64,32},{96,64},{1,97},{33,1},{65,33},{97,65},{2,98}... | collective-permute-start | bytes 811016 | tf_op jit(solution)/shard_map/ppermute | solution.py:412
  140.4 2.5 %own_sums.3 = (f32[1024,256]{1,0:T(8,128)S(1)}, bf16[1024,256]{1,0:T(8,128)(2,1)S(1)}) custom-call(s32[5]{0:T(128)S(1)} %stack.20.place_ref.refs_0_, bf16[1024,2048]{1,0:T(8,128)(2,1)S(1)} %get-tuple-element.90.plan_ref, bf16[1040,256]{1,0:T(8,128)(2,1)S(1)} %collective-permute-done.25.from_below.below, ...), custom_call_target="tpu_custom_call" | custom-call | flops 30000001024 | tf_op jit(solution)/shard_map/own_sums/pallas_call | solution.py:256
  142.9 1.8 %own_sums.2 = (f32[1024,256]{1,0:T(8,128)S(1)}, bf16[1024,256]{1,0:T(8,128)(2,1)S(1)}) custom-call(s32[5]{0:T(128)S(1)} %stack.20.place_ref.refs_0_, bf16[1024,2048]{1,0:T(8,128)(2,1)S(1)} %get-tuple-element.80.plan_ref, bf16[1040,256]{1,0:T(8,128)(2,1)S(1)} %collective-permute-done.21.from_below.refs_4_, ...), custom_call_target="tpu_custom_call" | custom-call | flops 30000001024 | tf_op jit(solution)/shard_map/own_sums/pallas_call | solution.py:256
  144.7 1.6 %finish.2 = (bf16[2048,256]{1,0:T(8,128)(2,1)}, f32[8,128]{1,0:T(8,128)S(1)}) custom-call(s32[5]{0:T(128)S(1)} %stack.20.place_ref.refs_0_, f32[1024,256]{1,0:T(8,128)S(1)} %get-tuple-element.94.own_ref, f32[16,128]{1,0:T(8,128)S(1)} %get-tuple-element.75.refs_5_.scale_ref.refs_2_, f32[8,128]{1,0:T(8,128)S(1)} %get-tuple-element.79.refs_6_.m_ref, ...), custom_call_target="tpu_custom_call" | custom-call | flops 30000001024 | tf_op jit(solution)/shard_map/finish/pallas_call | solution.py:391
  146.4 1.6 %finish.3 = (bf16[2048,256]{1,0:T(8,128)(2,1)}, f32[8,128]{1,0:T(8,128)S(1)}) custom-call(s32[5]{0:T(128)S(1)} %stack.20.place_ref.refs_0_, f32[1024,256]{1,0:T(8,128)S(1)} %get-tuple-element.85.refs_1_, f32[16,128]{1,0:T(8,128)S(1)} %get-tuple-element.75.refs_5_.scale_ref.refs_2_, ...), custom_call_target="tpu_custom_call", output_to_operand_aliasing={{0}: (10, {})} | custom-call | flops 30000001024 | tf_op jit(solution)/shard_map/finish/pallas_call | solution.py:391
  148.1 0.6 maximum_bitcast_fusion
  (22 shorter events, 0.3 us)
Async XLA Ops:
  0.6 6.9 %collective-permute-start = (bf16[64,1024]{1,0:T(8,128)(2,1)}, bf16[64,1024]{1,0:T(8,128)(2,1)S(1)}, u32[]{:S(2)}, u32[]{:S(2)}) collective-permute-start(bf16[64,1024]{1,0:T(8,128)(2,1)} %x_ref.1), channel_id=1, source_target_pairs={{0,8},{1,3},{2,10},{3,5},{4,12},{5,7},{6,14},{7,1},{8,16},{9,11},{... | collective-permute-start | bytes 393224 | tf_op jit(solution)/shard_map/ppermute | solution.py:425
  2.3 7.3 %collective-permute-start.1 = (bf16[64,1024]{1,0:T(8,128)(2,1)}, bf16[64,1024]{1,0:T(8,128)(2,1)S(1)}, u32[]{:S(2)}, u32[]{:S(2)}) collective-permute-start(bf16[64,1024]{1,0:T(8,128)(2,1)} %x_ref.1), channel_id=1, source_target_pairs={{0,16},{1,5},{2,18},{3,7},{4,20},{5,1},{6,22},{7,3},{8,24},{9,13},... | collective-permute-start | bytes 393224 | tf_op jit(solution)/shard_map/ppermute | solution.py:425
  5.0 5.2 %collective-permute-start.2 = (bf16[64,1024]{1,0:T(8,128)(2,1)}, bf16[64,1024]{1,0:T(8,128)(2,1)S(1)}, u32[]{:S(2)}, u32[]{:S(2)}) collective-permute-start(bf16[64,1024]{1,0:T(8,128)(2,1)} %x_ref.1), channel_id=1, source_target_pairs={{0,24},{1,7},{2,26},{3,1},{4,28},{5,3},{6,30},{7,5},{8,0},{9,15},{... | collective-permute-start | bytes 393224 | tf_op jit(solution)/shard_map/ppermute | solution.py:425
  10.8 4.3 %collective-permute-start.3 = (bf16[256,1024]{1,0:T(8,128)(2,1)S(1)}, bf16[256,1024]{1,0:T(8,128)(2,1)S(1)}, u32[]{:S(2)}, u32[]{:S(2)}) collective-permute-start(bf16[256,1024]{1,0:T(8,128)(2,1)S(1)} %in_order.1.refs_0_), channel_id=1, source_target_pairs={{0,1},{1,0},{2,3},{3,2},{4,5},{5,4},{6,7},{7,6},{8,9},{9,8},{10,11... | collective-permute-start | bytes 1572872 | tf_op jit(solution)/shard_map/ppermute | solution.py:412
  10.9 11.3 %collective-permute-start.4 = (bf16[256,1024]{1,0:T(8,128)(2,1)S(1)}, bf16[256,1024]{1,0:T(8,128)(2,1)S(1)}, u32[]{:S(2)}, u32[]{:S(2)}) collective-permute-start(bf16[256,1024]{1,0:T(8,128)(2,1)S(1)} %in_order.1.refs_0_), channel_id=1, source_target_pairs={{0,2},{1,9},{2,4},{3,11},{4,6},{5,13},{6,0},{7,15},{8,10},{9,17},{... | collective-permute-start | bytes 1572872 | tf_op jit(solution)/shard_map/ppermute | solution.py:425
  12.9 9.3 %collective-permute-start.5 = (bf16[256,1024]{1,0:T(8,128)(2,1)S(1)}, bf16[256,1024]{1,0:T(8,128)(2,1)S(1)}, u32[]{:S(2)}, u32[]{:S(2)}) collective-permute-start(bf16[256,1024]{1,0:T(8,128)(2,1)S(1)} %in_order.1.refs_0_), channel_id=1, source_target_pairs={{0,6},{1,25},{2,0},{3,27},{4,2},{5,29},{6,4},{7,31},{8,14},{9,1},{... | collective-permute-start | bytes 1572872 | tf_op jit(solution)/shard_map/ppermute | solution.py:425
  15.1 2.2 %copy-start = (bf16[2048,1024]{1,0:T(8,128)(2,1)S(1)}, bf16[2048,1024]{1,0:T(8,128)(2,1)}, u32[]{:S(2)}) copy-start(bf16[2048,1024]{1,0:T(8,128)(2,1)} %cents_ref.9) | copy-start | bytes 12582916
  22.1 4.0 %collective-permute-start.6 = (bf16[256,1024]{1,0:T(8,128)(2,1)S(1)}, bf16[256,1024]{1,0:T(8,128)(2,1)S(1)}, u32[]{:S(2)}, u32[]{:S(2)}) collective-permute-start(bf16[256,1024]{1,0:T(8,128)(2,1)S(1)} %collective-permute-done.4.refs_0_), channel_id=1, source_target_pairs={{0,1},{1,0},{2,3},{3,2},{4,5},{5,4},{6,7},{7,6},{8,9},{9,8},{10,11... | collective-permute-start | bytes 1572872 | tf_op jit(solution)/shard_map/ppermute | solution.py:412
  22.1 4.0 %collective-permute-start.7 = (bf16[256,1024]{1,0:T(8,128)(2,1)S(1)}, bf16[256,1024]{1,0:T(8,128)(2,1)S(1)}, u32[]{:S(2)}, u32[]{:S(2)}) collective-permute-start(bf16[256,1024]{1,0:T(8,128)(2,1)S(1)} %collective-permute-done.5.refs_1_), channel_id=1, source_target_pairs={{0,1},{1,0},{2,3},{3,2},{4,5},{5,4},{6,7},{7,6},{8,9},{9,8},{10,11... | collective-permute-start | bytes 1572872 | tf_op jit(solution)/shard_map/ppermute | solution.py:412
  22.7 8.8 %collective-permute-start.8 = (bf16[128,1024]{1,0:T(8,128)(2,1)S(1)}, bf16[128,1024]{1,0:T(8,128)(2,1)S(1)}, u32[]{:S(2)}, u32[]{:S(2)}) collective-permute-start(bf16[128,1024]{1,0:T(8,128)(2,1)S(1)} %slice.6), channel_id=1, source_target_pairs={{0,2},{1,9},{2,4},{3,11},{4,6},{5,13},{6,0},{7,15},{8,10},{9,17},{... | collective-permute-start | bytes 786440 | tf_op jit(solution)/shard_map/ppermute | solution.py:425
  24.6 6.9 %collective-permute-start.9 = (bf16[128,1024]{1,0:T(8,128)(2,1)S(1)}, bf16[128,1024]{1,0:T(8,128)(2,1)S(1)}, u32[]{:S(2)}, u32[]{:S(2)}) collective-permute-start(bf16[128,1024]{1,0:T(8,128)(2,1)S(1)} %slice.7), channel_id=1, source_target_pairs={{0,6},{1,25},{2,0},{3,27},{4,2},{5,29},{6,4},{7,31},{8,14},{9,1},{... | collective-permute-start | bytes 786440 | tf_op jit(solution)/shard_map/ppermute | solution.py:425
  31.5 1.6 %collective-permute-start.10 = (bf16[128,1024]{1,0:T(8,128)(2,1)S(1)}, bf16[128,1024]{1,0:T(8,128)(2,1)S(1)}, u32[]{:S(2)}, u32[]{:S(2)}) collective-permute-start(bf16[128,1024]{1,0:T(8,128)(2,1)S(1)} %collective-permute-done.8.refs_0_), channel_id=1, source_target_pairs={{0,1},{1,0},{2,3},{3,2},{4,5},{5,4},{6,7},{7,6},{8,9},{9,8},{10,11... | collective-permute-start | bytes 786440 | tf_op jit(solution)/shard_map/ppermute | solution.py:412
  31.6 1.9 %collective-permute-start.11 = (bf16[128,1024]{1,0:T(8,128)(2,1)S(1)}, bf16[128,1024]{1,0:T(8,128)(2,1)S(1)}, u32[]{:S(2)}, u32[]{:S(2)}) collective-permute-start(bf16[128,1024]{1,0:T(8,128)(2,1)S(1)} %collective-permute-done.9.refs_1_), channel_id=1, source_target_pairs={{0,1},{1,0},{2,3},{3,2},{4,5},{5,4},{6,7},{7,6},{8,9},{9,8},{10,11... | collective-permute-start | bytes 786440 | tf_op jit(solution)/shard_map/ppermute | solution.py:412
  36.6 6.7 %collective-permute-start.12 = (f32[16,128]{1,0:T(8,128)S(1)}, f32[16,128]{1,0:T(8,128)S(1)}, u32[]{:S(2)}, u32[]{:S(2)}) collective-permute-start(f32[16,128]{1,0:T(8,128)S(1)} %get-tuple-element.71.refs_4_), channel_id=1, source_target_pairs={{0,64},{32,96},{64,0},{96,32},{1,65},{33,97},{65,1},{97,33},{2,66}... | collective-permute-start | bytes 24584 | tf_op jit(solution)/shard_map/ppermute | solution.py:412
  40.0 4.9 %collective-permute-start.13 = (f32[16,128]{1,0:T(8,128)S(1)}, f32[16,128]{1,0:T(8,128)S(1)}, u32[]{:S(2)}, u32[]{:S(2)}) collective-permute-start(f32[16,128]{1,0:T(8,128)S(1)} %get-tuple-element.71.refs_4_), channel_id=1, source_target_pairs={{0,32},{32,64},{64,96},{96,0},{1,33},{33,65},{65,97},{97,1},{2,34}... | collective-permute-start | bytes 24584 | tf_op jit(solution)/shard_map/ppermute | solution.py:412
  40.7 4.2 %collective-permute-start.14 = (f32[16,128]{1,0:T(8,128)S(1)}, f32[16,128]{1,0:T(8,128)S(1)}, u32[]{:S(2)}, u32[]{:S(2)}) collective-permute-start(f32[16,128]{1,0:T(8,128)S(1)} %get-tuple-element.71.refs_4_), channel_id=1, source_target_pairs={{0,96},{32,0},{64,32},{96,64},{1,97},{33,1},{65,33},{97,65},{2,98}... | collective-permute-start | bytes 24584 | tf_op jit(solution)/shard_map/ppermute | solution.py:412
  62.2 5.2 %collective-permute-start.15 = (f32[16,128]{1,0:T(8,128)S(1)}, f32[16,128]{1,0:T(8,128)S(1)}, u32[]{:S(2)}, u32[]{:S(2)}) collective-permute-start(f32[16,128]{1,0:T(8,128)S(1)} %col_pass.2.refs_4_), channel_id=1, source_target_pairs={{0,64},{32,96},{64,0},{96,32},{1,65},{33,97},{65,1},{97,33},{2,66}... | collective-permute-start | bytes 24584 | tf_op jit(solution)/shard_map/ppermute | solution.py:412
  63.8 4.9 %collective-permute-start.16 = (f32[16,128]{1,0:T(8,128)S(1)}, f32[16,128]{1,0:T(8,128)S(1)}, u32[]{:S(2)}, u32[]{:S(2)}) collective-permute-start(f32[16,128]{1,0:T(8,128)S(1)} %col_pass.2.refs_4_), channel_id=1, source_target_pairs={{0,32},{32,64},{64,96},{96,0},{1,33},{33,65},{65,97},{97,1},{2,34}... | collective-permute-start | bytes 24584 | tf_op jit(solution)/shard_map/ppermute | solution.py:412
  66.4 3.7 %collective-permute-start.17 = (f32[16,128]{1,0:T(8,128)S(1)}, f32[16,128]{1,0:T(8,128)S(1)}, u32[]{:S(2)}, u32[]{:S(2)}) collective-permute-start(f32[16,128]{1,0:T(8,128)S(1)} %col_pass.2.refs_4_), channel_id=1, source_target_pairs={{0,96},{32,0},{64,32},{96,64},{1,97},{33,1},{65,33},{97,65},{2,98}... | collective-permute-start | bytes 24584 | tf_op jit(solution)/shard_map/ppermute | solution.py:412
  84.9 5.2 %collective-permute-start.18 = (f32[16,128]{1,0:T(8,128)S(1)}, f32[16,128]{1,0:T(8,128)S(1)}, u32[]{:S(2)}, u32[]{:S(2)}) collective-permute-start(f32[16,128]{1,0:T(8,128)S(1)} %col_pass.3.refs_4_), channel_id=1, source_target_pairs={{0,64},{32,96},{64,0},{96,32},{1,65},{33,97},{65,1},{97,33},{2,66}... | collective-permute-start | bytes 24584 | tf_op jit(solution)/shard_map/ppermute | solution.py:412
  85.7 4.9 %collective-permute-start.19 = (f32[16,128]{1,0:T(8,128)S(1)}, f32[16,128]{1,0:T(8,128)S(1)}, u32[]{:S(2)}, u32[]{:S(2)}) collective-permute-start(f32[16,128]{1,0:T(8,128)S(1)} %col_pass.3.refs_4_), channel_id=1, source_target_pairs={{0,32},{32,64},{64,96},{96,0},{1,33},{33,65},{65,97},{97,1},{2,34}... | collective-permute-start | bytes 24584 | tf_op jit(solution)/shard_map/ppermute | solution.py:412
  87.7 3.7 %collective-permute-start.20 = (f32[16,128]{1,0:T(8,128)S(1)}, f32[16,128]{1,0:T(8,128)S(1)}, u32[]{:S(2)}, u32[]{:S(2)}) collective-permute-start(f32[16,128]{1,0:T(8,128)S(1)} %col_pass.3.refs_4_), channel_id=1, source_target_pairs={{0,96},{32,0},{64,32},{96,64},{1,97},{33,1},{65,33},{97,65},{2,98}... | collective-permute-start | bytes 24584 | tf_op jit(solution)/shard_map/ppermute | solution.py:412
  108.0 16.2 %collective-permute-start.25 = (bf16[1040,256]{1,0:T(8,128)(2,1)S(1)}, bf16[1040,256]{1,0:T(8,128)(2,1)S(1)}, u32[]{:S(2)}, u32[]{:S(2)}) collective-permute-start(bf16[1040,256]{1,0:T(8,128)(2,1)S(1)} %get-tuple-element.91), channel_id=1, source_target_pairs={{0,32},{32,64},{64,96},{96,0},{1,33},{33,65},{65,97},{97,1},{2,34}... | collective-permute-start | bytes 1597448 | tf_op jit(solution)/shard_map/ppermute | solution.py:412
  108.9 15.4 %collective-permute-start.26 = (bf16[1040,256]{1,0:T(8,128)(2,1)S(1)}, bf16[1040,256]{1,0:T(8,128)(2,1)S(1)}, u32[]{:S(2)}, u32[]{:S(2)}) collective-permute-start(bf16[1040,256]{1,0:T(8,128)(2,1)S(1)} %get-tuple-element.92), channel_id=1, source_target_pairs={{0,96},{32,0},{64,32},{96,64},{1,97},{33,1},{65,33},{97,65},{2,98}... | collective-permute-start | bytes 1597448 | tf_op jit(solution)/shard_map/ppermute | solution.py:412
  115.0 20.7 %collective-permute-start.21 = (bf16[1040,256]{1,0:T(8,128)(2,1)S(1)}, bf16[1040,256]{1,0:T(8,128)(2,1)S(1)}, u32[]{:S(2)}, u32[]{:S(2)}) collective-permute-start(bf16[1040,256]{1,0:T(8,128)(2,1)S(1)} %get-tuple-element.81), channel_id=1, source_target_pairs={{0,32},{32,64},{64,96},{96,0},{1,33},{33,65},{65,97},{97,1},{2,34}... | collective-permute-start | bytes 1597448 | tf_op jit(solution)/shard_map/ppermute | solution.py:412
  115.1 20.6 %collective-permute-start.22 = (bf16[1040,256]{1,0:T(8,128)(2,1)S(1)}, bf16[1040,256]{1,0:T(8,128)(2,1)S(1)}, u32[]{:S(2)}, u32[]{:S(2)}) collective-permute-start(bf16[1040,256]{1,0:T(8,128)(2,1)S(1)} %get-tuple-element.82), channel_id=1, source_target_pairs={{0,96},{32,0},{64,32},{96,64},{1,97},{33,1},{65,33},{97,65},{2,98}... | collective-permute-start | bytes 1597448 | tf_op jit(solution)/shard_map/ppermute | solution.py:412
  125.5 19.2 %collective-permute-start.27 = (bf16[528,256]{1,0:T(8,128)(2,1)S(1)}, bf16[528,256]{1,0:T(8,128)(2,1)S(1)}, u32[]{:S(2)}, u32[]{:S(2)}) collective-permute-start(bf16[528,256]{1,0:T(8,128)(2,1)S(1)} %get-tuple-element.95), channel_id=1, source_target_pairs={{0,32},{32,64},{64,96},{96,0},{1,33},{33,65},{65,97},{97,1},{2,34}... | collective-permute-start | bytes 811016 | tf_op jit(solution)/shard_map/ppermute | solution.py:412
  126.2 18.5 %collective-permute-start.28 = (bf16[528,256]{1,0:T(8,128)(2,1)S(1)}, bf16[528,256]{1,0:T(8,128)(2,1)S(1)}, u32[]{:S(2)}, u32[]{:S(2)}) collective-permute-start(bf16[528,256]{1,0:T(8,128)(2,1)S(1)} %get-tuple-element.96), channel_id=1, source_target_pairs={{0,96},{32,0},{64,32},{96,64},{1,97},{33,1},{65,33},{97,65},{2,98}... | collective-permute-start | bytes 811016 | tf_op jit(solution)/shard_map/ppermute | solution.py:412
  137.0 9.5 %collective-permute-start.23 = (bf16[528,256]{1,0:T(8,128)(2,1)S(1)}, bf16[528,256]{1,0:T(8,128)(2,1)S(1)}, u32[]{:S(2)}, u32[]{:S(2)}) collective-permute-start(bf16[528,256]{1,0:T(8,128)(2,1)S(1)} %get-tuple-element.87), channel_id=1, source_target_pairs={{0,32},{32,64},{64,96},{96,0},{1,33},{33,65},{65,97},{97,1},{2,34}... | collective-permute-start | bytes 811016 | tf_op jit(solution)/shard_map/ppermute | solution.py:412
  137.7 8.8 %collective-permute-start.24 = (bf16[528,256]{1,0:T(8,128)(2,1)S(1)}, bf16[528,256]{1,0:T(8,128)(2,1)S(1)}, u32[]{:S(2)}, u32[]{:S(2)}) collective-permute-start(bf16[528,256]{1,0:T(8,128)(2,1)S(1)} %get-tuple-element.88), channel_id=1, source_target_pairs={{0,96},{32,0},{64,32},{96,64},{1,97},{33,1},{65,33},{97,65},{2,98}... | collective-permute-start | bytes 811016 | tf_op jit(solution)/shard_map/ppermute | solution.py:412

commit v5 on v4

--- a/solution.py
+++ b/solution.py
@@ -156,13 +156,15 @@
 
 
 def row_kernel(target, place_ref, *refs):
-    w_refs, (a_ref, b_ref, c_ref, d_ref, out_ref, scale_ref, lines_ref) = refs[:PARTS], refs[PARTS:]
+    w_refs, (a_ref, b_ref, c_ref, d_ref, out_ref, scale_ref, *wide, lines_ref) = refs[:PARTS], refs[PARTS:]
     scale_ref[...] = target / ((a_ref[...] + b_ref[...]) + (c_ref[...] + d_ref[...]))
     tiles = tiles_of(w_refs)
     accs = [None] * len(tiles)
     for b in range(w_refs[0].shape[0] // LANES):
         part = slice(b * LANES, (b + 1) * LANES)
         s = down(scale_ref[b : b + 1, :])
+        if wide:
+            wide[0][part, :] = s
         for j, (ref, t) in enumerate(tiles):
             p = ref[part, t : t + LANES] * s
             p = jnp.sum(p.reshape(LANES // 8, 8, LANES), axis=0)
@@ -175,16 +177,18 @@
         out_ref[q] = value
 
 
-def row_pass(target, place, w, masses, peers):
+def row_pass(target, place, w, masses, peers, last):
     n = w[0].shape[0]
+    wide = [pltpu.VMEM((n, LANES), jnp.float32)] if last else []
     lines = len(ORDER) * LINES
     return pl.pallas_call(
         lambda *refs: row_kernel(target, *refs),
         in_specs=[SM] + [VM] * (PARTS + 4),
-        out_specs=[VM, VM],
+        out_specs=[VM] * (2 + len(wide)),
         out_shape=[
             jax.ShapeDtypeStruct((peers, lines, LANES), jnp.bfloat16),
             jax.ShapeDtypeStruct((n // LANES, LANES), jnp.float32),
+            *wide,
         ],
         scratch_shapes=[pltpu.VMEM((lines + SPARE, LANES), jnp.float32)],
         compiler_params=params(8 * 1024 * 1024),
@@ -266,7 +270,7 @@
 
 
 def plan_kernel(first, place_ref, *refs):
-    w_refs, (sums_ref, scale_ref, mark_ref, u_ref, f_ref, d_ref, *refs) = refs[:PARTS], refs[PARTS:]
+    w_refs, (sums_ref, wide_ref, mark_ref, u_ref, f_ref, d_ref, *refs) = refs[:PARTS], refs[PARTS:]
     plan_ref, mass_ref, up_ref, down_ref, lines_ref = refs
     scale = local_scale(place_ref, sums_ref, lines_ref)
     tiles = tiles_of(w_refs)
@@ -277,7 +281,7 @@
         for at in range(top, top + rows, LANES):
             part = slice(first + at, first + at + LANES)
             line = (first + at) // LANES
-            s = down(scale_ref[line : line + 1, :])
+            s = wide_ref[part, :]
             acc = None
             for j, (ref, t) in enumerate(tiles):
                 p = ref[part, t : t + LANES] * scale[j]
@@ -292,7 +296,7 @@
     put_tail(down_ref, mass_ref[...])
 
 
-def make_plan(place, w, sums, scale, cuts, first, mark):
+def make_plan(place, w, sums, wide, cuts, first, mark):
     n = w[0].shape[0]
     m, share = cuts[0].shape
     part = jax.ShapeDtypeStruct((n // 2 + TAIL, share), jnp.bfloat16)
@@ -301,7 +305,7 @@
         "make_plan",
         [SM] + [VM] * (PARTS + 6),
         [pltpu.VMEM((n // 2, m), jnp.bfloat16), jax.ShapeDtypeStruct((n // 2 // LANES, LANES), jnp.float32), part, part],
-        (place, *[held(x) for x in w], sums, scale, mark, *[held(v) for v in cuts[1:]]),
+        (place, *[held(x) for x in w], sums, held(wide), mark, *[held(v) for v in cuts[1:]]),
         [pltpu.VMEM((sums.shape[1] + SPARE, LANES), jnp.float32)],
     )
 
@@ -454,15 +458,15 @@
     w = (w0, w1, w2)
 
     for step in range(ROUNDS):
-        sums, scale = row_pass(target, place, w, row_peers(colmass), peers)
+        sums, scale, *wide = row_pass(target, place, w, row_peers(colmass), peers, step == ROUNDS - 1)
         sums = lax.all_to_all(sums, CENTS, 0, 0, tiled=True)
         if step < ROUNDS - 1:
             colmass = col_pass(place, w, sums)
 
     mark = jnp.zeros((8, LANES), jnp.float32)
-    plan0, mass0, up0, down0 = make_plan(place, w, sums, scale, cuts, 0, mark)
+    plan0, mass0, up0, down0 = make_plan(place, w, sums, wide[0], cuts, 0, mark)
     up0, down0 = move(up0, "y", 1), move(down0, "y", 3)
-    plan1, mass1, up1, down1 = make_plan(place, w, sums, scale, cuts, n // 2, mass0)
+    plan1, mass1, up1, down1 = make_plan(place, w, sums, wide[0], cuts, n // 2, mass0)
     up1, down1 = move(up1, "y", 1), move(down1, "y", 3)
     late_up0, late_down0, mark0 = late_sums(plan0, up0, down0, cuts)
     late_up0, late_down0 = move(late_up0, "y", 1), move(late_down0, "y", 3)

time: 149 us -> 149 us (level)
  no operation moved by 1% of the time
where the time goes in v5:
time: 149 us
  starting transfers between devices  43.6 us (29%)
  Pallas kernels  39.2 us (26%)
  blocking collectives  36.3 us (24%)
  waiting for transfers between devices  25.9 us (17%)
  local copies, waits for them, and re-layouts  2.31 us (2%)
    all_to_all x3, blocking collectives, body(): sums = lax.all_to_all(sums, CENTS, 0, 0, tiled=True)  36.3 us
    ppermute x22, starting transfers between devices, move(): return lax.ppermute(x, axis, [(i, (i + by) % n) for i in range(n)])  30.1 us
    ppermute x22, waiting for transfers between devices, move(): return lax.ppermute(x, axis, [(i, (i + by) % n) for i in range(n)])  21.3 us
    pallas_call x6, Pallas kernels, call(): pl.pallas_call(kernel, in_specs=specs, out_specs=[VM] * len(out_shape), o...  14 us
    ppermute x7, starting transfers between devices, spread(): return lax.ppermute(x, CENTS, pairs)  13.5 us
    pallas_call x3, Pallas kernels, weigh(): pl.pallas_call(functools.partial(weigh_kernel, len(blocks), at, last), in...  11.4 us
    pallas_call x3, Pallas kernels, row_pass(): pl.pallas_call(lambda *refs: row_kernel(target, *refs), in_specs=[SM] + [...  5.39 us
    ppermute x7, waiting for transfers between devices, spread(): return lax.ppermute(x, CENTS, pairs)  4.61 us
  transfers between devices with their start and end apart: 29, of which 15 were waited for; matrix products, arithmetic and copies ran while one was open for 0% of the time, Pallas kernels for 14%

profile of v5, /device:TPU:0, one launch (start us, length us, event | category | flops | bytes accessed | tf_op | source)
XLA Modules:
  0.0 148.7 jit_solution(14269862276168899797)
XLA Ops:
  0.6 1.6 %collective-permute-start = (bf16[64,1024]{1,0:T(8,128)(2,1)}, bf16[64,1024]{1,0:T(8,128)(2,1)S(1)}, u32[]{:S(2)}, u32[]{:S(2)}) collective-permute-start(bf16[64,1024]{1,0:T(8,128)(2,1)} %x_ref.1), channel_id=1, source_target_pairs={{0,8},{1,3},{2,10},{3,5},{4,12},{5,7},{6,14},{7,1},{8,16},{9,11},{... | collective-permute-start | bytes 393224 | tf_op jit(solution)/shard_map/ppermute | solution.py:429
  2.3 2.7 %collective-permute-start.1 = (bf16[64,1024]{1,0:T(8,128)(2,1)}, bf16[64,1024]{1,0:T(8,128)(2,1)S(1)}, u32[]{:S(2)}, u32[]{:S(2)}) collective-permute-start(bf16[64,1024]{1,0:T(8,128)(2,1)} %x_ref.1), channel_id=1, source_target_pairs={{0,16},{1,5},{2,18},{3,7},{4,20},{5,1},{6,22},{7,3},{8,24},{9,13},... | collective-permute-start | bytes 393224 | tf_op jit(solution)/shard_map/ppermute | solution.py:429
  5.0 1.4 collective-permute-start.2
  6.4 0.9 lift.1.refs_0_
  7.4 0.1 stack.20.place_ref.refs_0_
  7.5 2.1 %collective-permute-done.1.refs_2_ = bf16[64,1024]{1,0:T(8,128)(2,1)S(1)} collective-permute-done((bf16[64,1024]{1,0:T(8,128)(2,1)}, bf16[64,1024]{1,0:T(8,128)(2,1)S(1)}, u32[]{:S(2)}, u32[]{:S(2)}) %collective-permute-start.1) | collective-permute-done | bytes 131104 | tf_op jit(solution)/shard_map/ppermute | solution.py:429
  9.6 0.6 collective-permute-done.2.refs_3_
  10.2 0.6 in_order.1.refs_0_
  10.8 0.1 collective-permute-start.3
  10.9 2.0 %collective-permute-start.4 = (bf16[256,1024]{1,0:T(8,128)(2,1)S(1)}, bf16[256,1024]{1,0:T(8,128)(2,1)S(1)}, u32[]{:S(2)}, u32[]{:S(2)}) collective-permute-start(bf16[256,1024]{1,0:T(8,128)(2,1)S(1)} %in_order.1.refs_0_), channel_id=1, source_target_pairs={{0,2},{1,9},{2,4},{3,11},{4,6},{5,13},{6,0},{7,15},{8,10},{9,17},{... | collective-permute-start | bytes 1572872 | tf_op jit(solution)/shard_map/ppermute | solution.py:429
  12.9 2.2 %collective-permute-start.5 = (bf16[256,1024]{1,0:T(8,128)(2,1)S(1)}, bf16[256,1024]{1,0:T(8,128)(2,1)S(1)}, u32[]{:S(2)}, u32[]{:S(2)}) collective-permute-start(bf16[256,1024]{1,0:T(8,128)(2,1)S(1)} %in_order.1.refs_0_), channel_id=1, source_target_pairs={{0,6},{1,25},{2,0},{3,27},{4,2},{5,29},{6,4},{7,31},{8,14},{9,1},{... | collective-permute-start | bytes 1572872 | tf_op jit(solution)/shard_map/ppermute | solution.py:429
  15.1 2.2 %copy-done = bf16[2048,1024]{1,0:T(8,128)(2,1)S(1)} copy-done((bf16[2048,1024]{1,0:T(8,128)(2,1)S(1)}, bf16[2048,1024]{1,0:T(8,128)(2,1)}, u32[]{:S(2)}) %copy-start) | copy-done | bytes 4194328
  17.2 3.0 %weigh.3 = (f32[2048,512]{1,0:T(8,128)S(1)}, bf16[2048,256]{1,0:T(8,128)(2,1)S(1)}, bf16[2048,256]{1,0:T(8,128)(2,1)S(1)}, bf16[2048,256]{1,0:T(8,128)(2,1)S(1)}...) custom-call(s32[5]{0:T(128)S(1)} %stack.20.place_ref.refs_0_, bf16[2048,1024]{1,0:T(8,128)(2,1)S(1)} %copy-done, ...), custom_call_target="tpu_custom_call" | custom-call | flops 30000001024 | tf_op jit(solution)/shard_map/weigh/pallas_call | solution.py:126
  20.2 1.9 %collective-permute-done.4.refs_0_ = bf16[256,1024]{1,0:T(8,128)(2,1)S(1)} collective-permute-done((bf16[256,1024]{1,0:T(8,128)(2,1)S(1)}, bf16[256,1024]{1,0:T(8,128)(2,1)S(1)}, u32[]{:S(2)}, u32[]{:S(2)}) %collective-permute-start.4) | collective-permute-done | bytes 524320 | tf_op jit(solution)/shard_map/ppermute | solution.py:429
  22.1 0.5 collective-permute-start.7
  22.7 1.9 %collective-permute-start.8 = (bf16[128,1024]{1,0:T(8,128)(2,1)S(1)}, bf16[128,1024]{1,0:T(8,128)(2,1)S(1)}, u32[]{:S(2)}, u32[]{:S(2)}) collective-permute-start(bf16[128,1024]{1,0:T(8,128)(2,1)S(1)} %slice.6), channel_id=1, source_target_pairs={{0,2},{1,9},{2,4},{3,11},{4,6},{5,13},{6,0},{7,15},{8,10},{9,17},{... | collective-permute-start | bytes 786440 | tf_op jit(solution)/shard_map/ppermute | solution.py:429
  24.6 1.6 %collective-permute-start.9 = (bf16[128,1024]{1,0:T(8,128)(2,1)S(1)}, bf16[128,1024]{1,0:T(8,128)(2,1)S(1)}, u32[]{:S(2)}, u32[]{:S(2)}) collective-permute-start(bf16[128,1024]{1,0:T(8,128)(2,1)S(1)} %slice.7), channel_id=1, source_target_pairs={{0,6},{1,25},{2,0},{3,27},{4,2},{5,29},{6,4},{7,31},{8,14},{9,1},{... | collective-permute-start | bytes 786440 | tf_op jit(solution)/shard_map/ppermute | solution.py:429
  26.2 5.3 %weigh.4 = (f32[2048,1024]{1,0:T(8,128)S(1)}, bf16[2048,256]{1,0:T(8,128)(2,1)S(1)}, bf16[2048,256]{1,0:T(8,128)(2,1)S(1)}, bf16[2048,256]{1,0:T(8,128)(2,1)S(1)...) custom-call(s32[5]{0:T(128)S(1)} %stack.20.place_ref.refs_0_, ...), custom_call_target="tpu_custom_call", output_to_operand_aliasing={{1}: (6, {}), {2}: (7, {}), {3}: (8, {}), {4}: (9, {}), {5}... | custom-call | flops 30000001024 | tf_op jit(solution)/shard_map/weigh/pallas_call | solution.py:126
  31.6 0.5 collective-permute-start.11
  32.1 1.0 collective-permute-done.10.refs_2_
  33.1 0.4 collective-permute-done.11.refs_3_
  33.5 3.1 %weigh.5 = (f32[2048,512]{1,0:T(8,128)S(1)}, bf16[2048,256]{1,0:T(8,128)(2,1)S(1)}, bf16[2048,256]{1,0:T(8,128)(2,1)S(1)}, bf16[2048,256]{1,0:T(8,128)(2,1)S(1)}...) custom-call(s32[5]{0:T(128)S(1)} %stack.20.place_ref.refs_0_, ...), custom_call_target="tpu_custom_call", output_to_operand_aliasing={{1}: (6, {}), {2}: (7, {}), {3}: (8, {}), {4}: (9, {}), {5}... | custom-call | flops 30000001024 | tf_op jit(solution)/shard_map/weigh/pallas_call | solution.py:126
  36.6 3.5 %collective-permute-start.12 = (f32[16,128]{1,0:T(8,128)S(1)}, f32[16,128]{1,0:T(8,128)S(1)}, u32[]{:S(2)}, u32[]{:S(2)}) collective-permute-start(f32[16,128]{1,0:T(8,128)S(1)} %get-tuple-element.72.refs_4_), channel_id=1, source_target_pairs={{0,64},{32,96},{64,0},{96,32},{1,65},{33,97},{65,1},{97,33},{2,66}... | collective-permute-start | bytes 24584 | tf_op jit(solution)/shard_map/ppermute | solution.py:416
  40.0 0.7 collective-permute-start.13
  40.7 2.6 %collective-permute-start.14 = (f32[16,128]{1,0:T(8,128)S(1)}, f32[16,128]{1,0:T(8,128)S(1)}, u32[]{:S(2)}, u32[]{:S(2)}) collective-permute-start(f32[16,128]{1,0:T(8,128)S(1)} %get-tuple-element.72.refs_4_), channel_id=1, source_target_pairs={{0,96},{32,0},{64,32},{96,64},{1,97},{33,1},{65,33},{97,65},{2,98}... | collective-permute-start | bytes 24584 | tf_op jit(solution)/shard_map/ppermute | solution.py:416
  43.3 1.6 %collective-permute-done.13.refs_6_ = f32[16,128]{1,0:T(8,128)S(1)} collective-permute-done((f32[16,128]{1,0:T(8,128)S(1)}, f32[16,128]{1,0:T(8,128)S(1)}, u32[]{:S(2)}, u32[]{:S(2)}) %collective-permute-start.13) | collective-permute-done | bytes 8224 | tf_op jit(solution)/shard_map/ppermute | solution.py:416
  44.9 1.8 %row_pass.3 = (bf16[32,16,128]{2,1,0:T(8,128)(2,1)S(1)}, f32[16,128]{1,0:T(8,128)}) custom-call(s32[5]{0:T(128)S(1)} %stack.20.place_ref.refs_0_, f32[2048,512]{1,0:T(8,128)S(1)} %get-tuple-element.53.refs_1_.refs_0_, f32[2048,1024]{1,0:T(8,128)S(1)} %get-tuple-element.62.refs_2_.refs_1_, f32[2048,512]{1,0:T(8,128)S(1)} %get-tuple-element.71.refs_3_.refs_2_, ...), custom_call_target="tpu_custom_call" | custom-call | tf_op jit(solution)/shard_map/row_pass/pallas_call | solution.py:184
  46.7 13.8 %all_to_all.15.refs_3_ = bf16[32,16,128]{2,1,0:T(8,128)(2,1)S(1)} all-to-all(bf16[32,16,128]{2,1,0:T(8,128)(2,1)S(1)} %get-tuple-element.73), channel_id=1, replica_groups=mesh['y'=4,'x'=4,'z'=4,'core'=2] {'x','z','core'}, dimensions={0} | all-to-all | bytes 262144 | tf_op jit(solution)/shard_map/all_to_all | solution.py:462
  60.5 1.8 %col_pass.2.refs_4_ = f32[16,128]{1,0:T(8,128)S(1)} custom-call(s32[5]{0:T(128)S(1)} %stack.20.place_ref.refs_0_, f32[2048,512]{1,0:T(8,128)S(1)} %get-tuple-element.53.refs_1_.refs_0_, f32[2048,1024]{1,0:T(8,128)S(1)} %get-tuple-element.62.refs_2_.refs_1_, f32[2048,512]{1,0:T(8,128)S(1)} %get-tuple-element.71.refs_3_.refs_2_, ...), custom_call_target="tpu_custom_call" | custom-call | tf_op jit(solution)/shard_map/col_pass/pallas_call | solution.py:223
  62.3 1.5 %collective-permute-start.15 = (f32[16,128]{1,0:T(8,128)S(1)}, f32[16,128]{1,0:T(8,128)S(1)}, u32[]{:S(2)}, u32[]{:S(2)}) collective-permute-start(f32[16,128]{1,0:T(8,128)S(1)} %col_pass.2.refs_4_), channel_id=1, source_target_pairs={{0,64},{32,96},{64,0},{96,32},{1,65},{33,97},{65,1},{97,33},{2,66}... | collective-permute-start | bytes 24584 | tf_op jit(solution)/shard_map/ppermute | solution.py:416
  63.8 2.6 %collective-permute-start.16 = (f32[16,128]{1,0:T(8,128)S(1)}, f32[16,128]{1,0:T(8,128)S(1)}, u32[]{:S(2)}, u32[]{:S(2)}) collective-permute-start(f32[16,128]{1,0:T(8,128)S(1)} %col_pass.2.refs_4_), channel_id=1, source_target_pairs={{0,32},{32,64},{64,96},{96,0},{1,33},{33,65},{65,97},{97,1},{2,34}... | collective-permute-start | bytes 24584 | tf_op jit(solution)/shard_map/ppermute | solution.py:416
  66.5 0.6 collective-permute-start.17
  67.1 0.5 collective-permute-done.15.refs_5_
  67.5 1.2 collective-permute-done.16.refs_6_
  68.7 1.4 collective-permute-done.17.refs_7_
  70.1 1.8 %row_pass.4 = (bf16[32,16,128]{2,1,0:T(8,128)(2,1)S(1)}, f32[16,128]{1,0:T(8,128)}) custom-call(s32[5]{0:T(128)S(1)} %stack.20.place_ref.refs_0_, f32[2048,512]{1,0:T(8,128)S(1)} %get-tuple-element.53.refs_1_.refs_0_, f32[2048,1024]{1,0:T(8,128)S(1)} %get-tuple-element.62.refs_2_.refs_1_, f32[2048,512]{1,0:T(8,128)S(1)} %get-tuple-element.71.refs_3_.refs_2_, ...), custom_call_target="tpu_custom_call" | custom-call | tf_op jit(solution)/shard_map/row_pass/pallas_call | solution.py:184
  71.9 11.3 %all_to_all.16.refs_3_ = bf16[32,16,128]{2,1,0:T(8,128)(2,1)S(1)} all-to-all(bf16[32,16,128]{2,1,0:T(8,128)(2,1)S(1)} %get-tuple-element.74), channel_id=1, replica_groups=mesh['y'=4,'x'=4,'z'=4,'core'=2] {'x','z','core'}, dimensions={0} | all-to-all | bytes 262144 | tf_op jit(solution)/shard_map/all_to_all | solution.py:462
  83.2 1.8 %col_pass.3.refs_4_ = f32[16,128]{1,0:T(8,128)S(1)} custom-call(s32[5]{0:T(128)S(1)} %stack.20.place_ref.refs_0_, f32[2048,512]{1,0:T(8,128)S(1)} %get-tuple-element.53.refs_1_.refs_0_, f32[2048,1024]{1,0:T(8,128)S(1)} %get-tuple-element.62.refs_2_.refs_1_, f32[2048,512]{1,0:T(8,128)S(1)} %get-tuple-element.71.refs_3_.refs_2_, ...), custom_call_target="tpu_custom_call" | custom-call | tf_op jit(solution)/shard_map/col_pass/pallas_call | solution.py:223
  85.0 0.8 collective-permute-start.18
  85.8 2.0 %collective-permute-start.19 = (f32[16,128]{1,0:T(8,128)S(1)}, f32[16,128]{1,0:T(8,128)S(1)}, u32[]{:S(2)}, u32[]{:S(2)}) collective-permute-start(f32[16,128]{1,0:T(8,128)S(1)} %col_pass.3.refs_4_), channel_id=1, source_target_pairs={{0,32},{32,64},{64,96},{96,0},{1,33},{33,65},{65,97},{97,1},{2,34}... | collective-permute-start | bytes 24584 | tf_op jit(solution)/shard_map/ppermute | solution.py:416
  87.8 1.2 collective-permute-start.20
  89.0 1.2 collective-permute-done.18.refs_5_
  90.2 0.4 collective-permute-done.19.refs_6_
  90.6 0.8 collective-permute-done.20.refs_7_
  91.4 1.8 %row_pass.5 = (bf16[32,16,128]{2,1,0:T(8,128)(2,1)S(1)}, f32[16,128]{1,0:T(8,128)S(1)}, f32[2048,128]{1,0:T(8,128)S(1)}) custom-call(s32[5]{0:T(128)S(1)} %stack.20.place_ref.refs_0_, f32[2048,512]{1,0:T(8,128)S(1)} %get-tuple-element.53.refs_1_.refs_0_, f32[2048,1024]{1,0:T(8,128)S(1)} %get-tuple-element.62.refs_2_.refs_1_, ...), custom_call_target="tpu_custom_call" | custom-call | tf_op jit(solution)/shard_map/row_pass/pallas_call | solution.py:184
  93.2 11.3 %all_to_all.17.refs_4_ = bf16[32,16,128]{2,1,0:T(8,128)(2,1)S(1)} all-to-all(bf16[32,16,128]{2,1,0:T(8,128)(2,1)S(1)} %get-tuple-element.75), channel_id=1, replica_groups=mesh['y'=4,'x'=4,'z'=4,'core'=2] {'x','z','core'}, dimensions={0} | all-to-all | bytes 262144 | tf_op jit(solution)/shard_map/all_to_all | solution.py:462
  104.5 3.6 %make_plan.2 = (bf16[1024,2048]{1,0:T(8,128)(2,1)S(1)}, f32[8,128]{1,0:T(8,128)S(1)}, bf16[1040,256]{1,0:T(8,128)(2,1)S(1)}, bf16[1040,256]{1,0:T(8,128)(2,1)S(1)}) custom-call(s32[5]{0:T(128)S(1)} %stack.20.place_ref.refs_0_, f32[2048,512]{1,0:T(8,128)S(1)} %get-tuple-element.53.refs_1_.refs_0_, f32[2048,1024]{1,0:T(8,128)S(1)} %get-tuple-element.62.refs_2_.refs_1_, ...), custom_call_target="tpu_custom_call" | custom-call | flops 30000001024 | tf_op jit(solution)/shard_map/make_plan/pallas_call | solution.py:260
  108.1 0.9 collective-permute-start.25
  109.0 2.4 %collective-permute-start.26 = (bf16[1040,256]{1,0:T(8,128)(2,1)S(1)}, bf16[1040,256]{1,0:T(8,128)(2,1)S(1)}, u32[]{:S(2)}, u32[]{:S(2)}) collective-permute-start(bf16[1040,256]{1,0:T(8,128)(2,1)S(1)} %get-tuple-element.94), channel_id=1, source_target_pairs={{0,96},{32,0},{64,32},{96,64},{1,97},{33,1},{65,33},{97,65},{2,98}... | collective-permute-start | bytes 1597448 | tf_op jit(solution)/shard_map/ppermute | solution.py:416
  111.4 3.6 %make_plan.3 = (bf16[1024,2048]{1,0:T(8,128)(2,1)S(1)}, f32[8,128]{1,0:T(8,128)S(1)}, bf16[1040,256]{1,0:T(8,128)(2,1)S(1)}, bf16[1040,256]{1,0:T(8,128)(2,1)S(1)}) custom-call(s32[5]{0:T(128)S(1)} %stack.20.place_ref.refs_0_, f32[2048,512]{1,0:T(8,128)S(1)} %get-tuple-element.53.refs_1_.refs_0_, f32[2048,1024]{1,0:T(8,128)S(1)} %get-tuple-element.62.refs_2_.refs_1_, ...), custom_call_target="tpu_custom_call" | custom-call | flops 30000001024 | tf_op jit(solution)/shard_map/make_plan/pallas_call | solution.py:260
  115.1 3.2 %collective-permute-start.22 = (bf16[1040,256]{1,0:T(8,128)(2,1)S(1)}, bf16[1040,256]{1,0:T(8,128)(2,1)S(1)}, u32[]{:S(2)}, u32[]{:S(2)}) collective-permute-start(bf16[1040,256]{1,0:T(8,128)(2,1)S(1)} %get-tuple-element.83), channel_id=1, source_target_pairs={{0,96},{32,0},{64,32},{96,64},{1,97},{33,1},{65,33},{97,65},{2,98}... | collective-permute-start | bytes 1597448 | tf_op jit(solution)/shard_map/ppermute | solution.py:416
  118.3 6.0 %collective-permute-done.25.from_below.below = bf16[1040,256]{1,0:T(8,128)(2,1)S(1)} collective-permute-done((bf16[1040,256]{1,0:T(8,128)(2,1)S(1)}, bf16[1040,256]{1,0:T(8,128)(2,1)S(1)}, u32[]{:S(2)}, u32[]{:S(2)}) %collective-permute-start.25) | collective-permute-done | bytes 532512 | tf_op jit(solution)/shard_map/ppermute | solution.py:416
  124.3 1.3 late_sums.3
  125.6 0.7 collective-permute-start.27
  126.3 2.7 %collective-permute-start.28 = (bf16[528,256]{1,0:T(8,128)(2,1)S(1)}, bf16[528,256]{1,0:T(8,128)(2,1)S(1)}, u32[]{:S(2)}, u32[]{:S(2)}) collective-permute-start(bf16[528,256]{1,0:T(8,128)(2,1)S(1)} %get-tuple-element.98), channel_id=1, source_target_pairs={{0,96},{32,0},{64,32},{96,64},{1,97},{33,1},{65,33},{97,65},{2,98}... | collective-permute-start | bytes 811016 | tf_op jit(solution)/shard_map/ppermute | solution.py:416
  129.0 6.7 %collective-permute-done.21.from_below.refs_4_ = bf16[1040,256]{1,0:T(8,128)(2,1)S(1)} collective-permute-done((bf16[1040,256]{1,0:T(8,128)(2,1)S(1)}, bf16[1040,256]{1,0:T(8,128)(2,1)S(1)}, u32[]{:S(2)}, u32[]{:S(2)}) %collective-permute-start.21) | collective-permute-done | bytes 532512 | tf_op jit(solution)/shard_map/ppermute | solution.py:416
  135.7 1.3 late_sums.2
  137.0 0.7 collective-permute-start.23
  137.7 2.7 %collective-permute-start.24 = (bf16[528,256]{1,0:T(8,128)(2,1)S(1)}, bf16[528,256]{1,0:T(8,128)(2,1)S(1)}, u32[]{:S(2)}, u32[]{:S(2)}) collective-permute-start(bf16[528,256]{1,0:T(8,128)(2,1)S(1)} %get-tuple-element.90), channel_id=1, source_target_pairs={{0,96},{32,0},{64,32},{96,64},{1,97},{33,1},{65,33},{97,65},{2,98}... | collective-permute-start | bytes 811016 | tf_op jit(solution)/shard_map/ppermute | solution.py:416
  140.4 2.5 %own_sums.3 = (f32[1024,256]{1,0:T(8,128)S(1)}, bf16[1024,256]{1,0:T(8,128)(2,1)S(1)}) custom-call(s32[5]{0:T(128)S(1)} %stack.20.place_ref.refs_0_, bf16[1024,2048]{1,0:T(8,128)(2,1)S(1)} %get-tuple-element.92.plan_ref, bf16[1040,256]{1,0:T(8,128)(2,1)S(1)} %collective-permute-done.25.from_below.below, ...), custom_call_target="tpu_custom_call" | custom-call | flops 30000001024 | tf_op jit(solution)/shard_map/own_sums/pallas_call | solution.py:260
  142.9 1.8 %own_sums.2 = (f32[1024,256]{1,0:T(8,128)S(1)}, bf16[1024,256]{1,0:T(8,128)(2,1)S(1)}) custom-call(s32[5]{0:T(128)S(1)} %stack.20.place_ref.refs_0_, bf16[1024,2048]{1,0:T(8,128)(2,1)S(1)} %get-tuple-element.81.plan_ref, bf16[1040,256]{1,0:T(8,128)(2,1)S(1)} %collective-permute-done.21.from_below.refs_4_, ...), custom_call_target="tpu_custom_call" | custom-call | flops 30000001024 | tf_op jit(solution)/shard_map/own_sums/pallas_call | solution.py:260
  144.8 1.6 %finish.2 = (bf16[2048,256]{1,0:T(8,128)(2,1)}, f32[8,128]{1,0:T(8,128)S(1)}) custom-call(s32[5]{0:T(128)S(1)} %stack.20.place_ref.refs_0_, f32[1024,256]{1,0:T(8,128)S(1)} %get-tuple-element.96.own_ref, f32[16,128]{1,0:T(8,128)S(1)} %get-tuple-element.87.scale_ref.refs_2_, f32[8,128]{1,0:T(8,128)S(1)} %get-tuple-element.80.refs_6_.m_ref, ...), custom_call_target="tpu_custom_call" | custom-call | flops 30000001024 | tf_op jit(solution)/shard_map/finish/pallas_call | solution.py:395
  146.5 1.6 %finish.3 = (bf16[2048,256]{1,0:T(8,128)(2,1)}, f32[8,128]{1,0:T(8,128)S(1)}) custom-call(s32[5]{0:T(128)S(1)} %stack.20.place_ref.refs_0_, f32[1024,256]{1,0:T(8,128)S(1)} %get-tuple-element.86.refs_1_, f32[16,128]{1,0:T(8,128)S(1)} %get-tuple-element.87.scale_ref.refs_2_, ...), custom_call_target="tpu_custom_call", output_to_operand_aliasing={{0}: (10, {})} | custom-call | flops 30000001024 | tf_op jit(solution)/shard_map/finish/pallas_call | solution.py:395
  148.1 0.6 maximum_bitcast_fusion
  (22 shorter events, 0.3 us)
Async XLA Ops:
  0.6 6.9 %collective-permute-start = (bf16[64,1024]{1,0:T(8,128)(2,1)}, bf16[64,1024]{1,0:T(8,128)(2,1)S(1)}, u32[]{:S(2)}, u32[]{:S(2)}) collective-permute-start(bf16[64,1024]{1,0:T(8,128)(2,1)} %x_ref.1), channel_id=1, source_target_pairs={{0,8},{1,3},{2,10},{3,5},{4,12},{5,7},{6,14},{7,1},{8,16},{9,11},{... | collective-permute-start | bytes 393224 | tf_op jit(solution)/shard_map/ppermute | solution.py:429
  2.3 7.3 %collective-permute-start.1 = (bf16[64,1024]{1,0:T(8,128)(2,1)}, bf16[64,1024]{1,0:T(8,128)(2,1)S(1)}, u32[]{:S(2)}, u32[]{:S(2)}) collective-permute-start(bf16[64,1024]{1,0:T(8,128)(2,1)} %x_ref.1), channel_id=1, source_target_pairs={{0,16},{1,5},{2,18},{3,7},{4,20},{5,1},{6,22},{7,3},{8,24},{9,13},... | collective-permute-start | bytes 393224 | tf_op jit(solution)/shard_map/ppermute | solution.py:429
  5.0 5.2 %collective-permute-start.2 = (bf16[64,1024]{1,0:T(8,128)(2,1)}, bf16[64,1024]{1,0:T(8,128)(2,1)S(1)}, u32[]{:S(2)}, u32[]{:S(2)}) collective-permute-start(bf16[64,1024]{1,0:T(8,128)(2,1)} %x_ref.1), channel_id=1, source_target_pairs={{0,24},{1,7},{2,26},{3,1},{4,28},{5,3},{6,30},{7,5},{8,0},{9,15},{... | collective-permute-start | bytes 393224 | tf_op jit(solution)/shard_map/ppermute | solution.py:429
  10.8 4.3 %collective-permute-start.3 = (bf16[256,1024]{1,0:T(8,128)(2,1)S(1)}, bf16[256,1024]{1,0:T(8,128)(2,1)S(1)}, u32[]{:S(2)}, u32[]{:S(2)}) collective-permute-start(bf16[256,1024]{1,0:T(8,128)(2,1)S(1)} %in_order.1.refs_0_), channel_id=1, source_target_pairs={{0,1},{1,0},{2,3},{3,2},{4,5},{5,4},{6,7},{7,6},{8,9},{9,8},{10,11... | collective-permute-start | bytes 1572872 | tf_op jit(solution)/shard_map/ppermute | solution.py:416
  10.9 11.3 %collective-permute-start.4 = (bf16[256,1024]{1,0:T(8,128)(2,1)S(1)}, bf16[256,1024]{1,0:T(8,128)(2,1)S(1)}, u32[]{:S(2)}, u32[]{:S(2)}) collective-permute-start(bf16[256,1024]{1,0:T(8,128)(2,1)S(1)} %in_order.1.refs_0_), channel_id=1, source_target_pairs={{0,2},{1,9},{2,4},{3,11},{4,6},{5,13},{6,0},{7,15},{8,10},{9,17},{... | collective-permute-start | bytes 1572872 | tf_op jit(solution)/shard_map/ppermute | solution.py:429
  12.9 9.3 %collective-permute-start.5 = (bf16[256,1024]{1,0:T(8,128)(2,1)S(1)}, bf16[256,1024]{1,0:T(8,128)(2,1)S(1)}, u32[]{:S(2)}, u32[]{:S(2)}) collective-permute-start(bf16[256,1024]{1,0:T(8,128)(2,1)S(1)} %in_order.1.refs_0_), channel_id=1, source_target_pairs={{0,6},{1,25},{2,0},{3,27},{4,2},{5,29},{6,4},{7,31},{8,14},{9,1},{... | collective-permute-start | bytes 1572872 | tf_op jit(solution)/shard_map/ppermute | solution.py:429
  15.1 2.2 %copy-start = (bf16[2048,1024]{1,0:T(8,128)(2,1)S(1)}, bf16[2048,1024]{1,0:T(8,128)(2,1)}, u32[]{:S(2)}) copy-start(bf16[2048,1024]{1,0:T(8,128)(2,1)} %cents_ref.9) | copy-start | bytes 12582916
  22.1 4.0 %collective-permute-start.6 = (bf16[256,1024]{1,0:T(8,128)(2,1)S(1)}, bf16[256,1024]{1,0:T(8,128)(2,1)S(1)}, u32[]{:S(2)}, u32[]{:S(2)}) collective-permute-start(bf16[256,1024]{1,0:T(8,128)(2,1)S(1)} %collective-permute-done.4.refs_0_), channel_id=1, source_target_pairs={{0,1},{1,0},{2,3},{3,2},{4,5},{5,4},{6,7},{7,6},{8,9},{9,8},{10,11... | collective-permute-start | bytes 1572872 | tf_op jit(solution)/shard_map/ppermute | solution.py:416
  22.1 4.0 %collective-permute-start.7 = (bf16[256,1024]{1,0:T(8,128)(2,1)S(1)}, bf16[256,1024]{1,0:T(8,128)(2,1)S(1)}, u32[]{:S(2)}, u32[]{:S(2)}) collective-permute-start(bf16[256,1024]{1,0:T(8,128)(2,1)S(1)} %collective-permute-done.5.refs_1_), channel_id=1, source_target_pairs={{0,1},{1,0},{2,3},{3,2},{4,5},{5,4},{6,7},{7,6},{8,9},{9,8},{10,11... | collective-permute-start | bytes 1572872 | tf_op jit(solution)/shard_map/ppermute | solution.py:416
  22.7 8.8 %collective-permute-start.8 = (bf16[128,1024]{1,0:T(8,128)(2,1)S(1)}, bf16[128,1024]{1,0:T(8,128)(2,1)S(1)}, u32[]{:S(2)}, u32[]{:S(2)}) collective-permute-start(bf16[128,1024]{1,0:T(8,128)(2,1)S(1)} %slice.6), channel_id=1, source_target_pairs={{0,2},{1,9},{2,4},{3,11},{4,6},{5,13},{6,0},{7,15},{8,10},{9,17},{... | collective-permute-start | bytes 786440 | tf_op jit(solution)/shard_map/ppermute | solution.py:429
  24.6 6.9 %collective-permute-start.9 = (bf16[128,1024]{1,0:T(8,128)(2,1)S(1)}, bf16[128,1024]{1,0:T(8,128)(2,1)S(1)}, u32[]{:S(2)}, u32[]{:S(2)}) collective-permute-start(bf16[128,1024]{1,0:T(8,128)(2,1)S(1)} %slice.7), channel_id=1, source_target_pairs={{0,6},{1,25},{2,0},{3,27},{4,2},{5,29},{6,4},{7,31},{8,14},{9,1},{... | collective-permute-start | bytes 786440 | tf_op jit(solution)/shard_map/ppermute | solution.py:429
  31.5 1.6 %collective-permute-start.10 = (bf16[128,1024]{1,0:T(8,128)(2,1)S(1)}, bf16[128,1024]{1,0:T(8,128)(2,1)S(1)}, u32[]{:S(2)}, u32[]{:S(2)}) collective-permute-start(bf16[128,1024]{1,0:T(8,128)(2,1)S(1)} %collective-permute-done.8.refs_0_), channel_id=1, source_target_pairs={{0,1},{1,0},{2,3},{3,2},{4,5},{5,4},{6,7},{7,6},{8,9},{9,8},{10,11... | collective-permute-start | bytes 786440 | tf_op jit(solution)/shard_map/ppermute | solution.py:416
  31.6 1.9 %collective-permute-start.11 = (bf16[128,1024]{1,0:T(8,128)(2,1)S(1)}, bf16[128,1024]{1,0:T(8,128)(2,1)S(1)}, u32[]{:S(2)}, u32[]{:S(2)}) collective-permute-start(bf16[128,1024]{1,0:T(8,128)(2,1)S(1)} %collective-permute-done.9.refs_1_), channel_id=1, source_target_pairs={{0,1},{1,0},{2,3},{3,2},{4,5},{5,4},{6,7},{7,6},{8,9},{9,8},{10,11... | collective-permute-start | bytes 786440 | tf_op jit(solution)/shard_map/ppermute | solution.py:416
  36.6 6.7 %collective-permute-start.12 = (f32[16,128]{1,0:T(8,128)S(1)}, f32[16,128]{1,0:T(8,128)S(1)}, u32[]{:S(2)}, u32[]{:S(2)}) collective-permute-start(f32[16,128]{1,0:T(8,128)S(1)} %get-tuple-element.72.refs_4_), channel_id=1, source_target_pairs={{0,64},{32,96},{64,0},{96,32},{1,65},{33,97},{65,1},{97,33},{2,66}... | collective-permute-start | bytes 24584 | tf_op jit(solution)/shard_map/ppermute | solution.py:416
  40.0 4.9 %collective-permute-start.13 = (f32[16,128]{1,0:T(8,128)S(1)}, f32[16,128]{1,0:T(8,128)S(1)}, u32[]{:S(2)}, u32[]{:S(2)}) collective-permute-start(f32[16,128]{1,0:T(8,128)S(1)} %get-tuple-element.72.refs_4_), channel_id=1, source_target_pairs={{0,32},{32,64},{64,96},{96,0},{1,33},{33,65},{65,97},{97,1},{2,34}... | collective-permute-start | bytes 24584 | tf_op jit(solution)/shard_map/ppermute | solution.py:416
  40.7 4.2 %collective-permute-start.14 = (f32[16,128]{1,0:T(8,128)S(1)}, f32[16,128]{1,0:T(8,128)S(1)}, u32[]{:S(2)}, u32[]{:S(2)}) collective-permute-start(f32[16,128]{1,0:T(8,128)S(1)} %get-tuple-element.72.refs_4_), channel_id=1, source_target_pairs={{0,96},{32,0},{64,32},{96,64},{1,97},{33,1},{65,33},{97,65},{2,98}... | collective-permute-start | bytes 24584 | tf_op jit(solution)/shard_map/ppermute | solution.py:416
  62.3 5.2 %collective-permute-start.15 = (f32[16,128]{1,0:T(8,128)S(1)}, f32[16,128]{1,0:T(8,128)S(1)}, u32[]{:S(2)}, u32[]{:S(2)}) collective-permute-start(f32[16,128]{1,0:T(8,128)S(1)} %col_pass.2.refs_4_), channel_id=1, source_target_pairs={{0,64},{32,96},{64,0},{96,32},{1,65},{33,97},{65,1},{97,33},{2,66}... | collective-permute-start | bytes 24584 | tf_op jit(solution)/shard_map/ppermute | solution.py:416
  63.8 4.9 %collective-permute-start.16 = (f32[16,128]{1,0:T(8,128)S(1)}, f32[16,128]{1,0:T(8,128)S(1)}, u32[]{:S(2)}, u32[]{:S(2)}) collective-permute-start(f32[16,128]{1,0:T(8,128)S(1)} %col_pass.2.refs_4_), channel_id=1, source_target_pairs={{0,32},{32,64},{64,96},{96,0},{1,33},{33,65},{65,97},{97,1},{2,34}... | collective-permute-start | bytes 24584 | tf_op jit(solution)/shard_map/ppermute | solution.py:416
  66.5 3.7 %collective-permute-start.17 = (f32[16,128]{1,0:T(8,128)S(1)}, f32[16,128]{1,0:T(8,128)S(1)}, u32[]{:S(2)}, u32[]{:S(2)}) collective-permute-start(f32[16,128]{1,0:T(8,128)S(1)} %col_pass.2.refs_4_), channel_id=1, source_target_pairs={{0,96},{32,0},{64,32},{96,64},{1,97},{33,1},{65,33},{97,65},{2,98}... | collective-permute-start | bytes 24584 | tf_op jit(solution)/shard_map/ppermute | solution.py:416
  85.0 5.2 %collective-permute-start.18 = (f32[16,128]{1,0:T(8,128)S(1)}, f32[16,128]{1,0:T(8,128)S(1)}, u32[]{:S(2)}, u32[]{:S(2)}) collective-permute-start(f32[16,128]{1,0:T(8,128)S(1)} %col_pass.3.refs_4_), channel_id=1, source_target_pairs={{0,64},{32,96},{64,0},{96,32},{1,65},{33,97},{65,1},{97,33},{2,66}... | collective-permute-start | bytes 24584 | tf_op jit(solution)/shard_map/ppermute | solution.py:416
  85.8 4.9 %collective-permute-start.19 = (f32[16,128]{1,0:T(8,128)S(1)}, f32[16,128]{1,0:T(8,128)S(1)}, u32[]{:S(2)}, u32[]{:S(2)}) collective-permute-start(f32[16,128]{1,0:T(8,128)S(1)} %col_pass.3.refs_4_), channel_id=1, source_target_pairs={{0,32},{32,64},{64,96},{96,0},{1,33},{33,65},{65,97},{97,1},{2,34}... | collective-permute-start | bytes 24584 | tf_op jit(solution)/shard_map/ppermute | solution.py:416
  87.8 3.7 %collective-permute-start.20 = (f32[16,128]{1,0:T(8,128)S(1)}, f32[16,128]{1,0:T(8,128)S(1)}, u32[]{:S(2)}, u32[]{:S(2)}) collective-permute-start(f32[16,128]{1,0:T(8,128)S(1)} %col_pass.3.refs_4_), channel_id=1, source_target_pairs={{0,96},{32,0},{64,32},{96,64},{1,97},{33,1},{65,33},{97,65},{2,98}... | collective-permute-start | bytes 24584 | tf_op jit(solution)/shard_map/ppermute | solution.py:416
  108.1 16.2 %collective-permute-start.25 = (bf16[1040,256]{1,0:T(8,128)(2,1)S(1)}, bf16[1040,256]{1,0:T(8,128)(2,1)S(1)}, u32[]{:S(2)}, u32[]{:S(2)}) collective-permute-start(bf16[1040,256]{1,0:T(8,128)(2,1)S(1)} %get-tuple-element.93), channel_id=1, source_target_pairs={{0,32},{32,64},{64,96},{96,0},{1,33},{33,65},{65,97},{97,1},{2,34}... | collective-permute-start | bytes 1597448 | tf_op jit(solution)/shard_map/ppermute | solution.py:416
  109.0 15.4 %collective-permute-start.26 = (bf16[1040,256]{1,0:T(8,128)(2,1)S(1)}, bf16[1040,256]{1,0:T(8,128)(2,1)S(1)}, u32[]{:S(2)}, u32[]{:S(2)}) collective-permute-start(bf16[1040,256]{1,0:T(8,128)(2,1)S(1)} %get-tuple-element.94), channel_id=1, source_target_pairs={{0,96},{32,0},{64,32},{96,64},{1,97},{33,1},{65,33},{97,65},{2,98}... | collective-permute-start | bytes 1597448 | tf_op jit(solution)/shard_map/ppermute | solution.py:416
  115.0 20.7 %collective-permute-start.21 = (bf16[1040,256]{1,0:T(8,128)(2,1)S(1)}, bf16[1040,256]{1,0:T(8,128)(2,1)S(1)}, u32[]{:S(2)}, u32[]{:S(2)}) collective-permute-start(bf16[1040,256]{1,0:T(8,128)(2,1)S(1)} %get-tuple-element.82), channel_id=1, source_target_pairs={{0,32},{32,64},{64,96},{96,0},{1,33},{33,65},{65,97},{97,1},{2,34}... | collective-permute-start | bytes 1597448 | tf_op jit(solution)/shard_map/ppermute | solution.py:416
  115.1 20.7 %collective-permute-start.22 = (bf16[1040,256]{1,0:T(8,128)(2,1)S(1)}, bf16[1040,256]{1,0:T(8,128)(2,1)S(1)}, u32[]{:S(2)}, u32[]{:S(2)}) collective-permute-start(bf16[1040,256]{1,0:T(8,128)(2,1)S(1)} %get-tuple-element.83), channel_id=1, source_target_pairs={{0,96},{32,0},{64,32},{96,64},{1,97},{33,1},{65,33},{97,65},{2,98}... | collective-permute-start | bytes 1597448 | tf_op jit(solution)/shard_map/ppermute | solution.py:416
  125.6 19.1 %collective-permute-start.27 = (bf16[528,256]{1,0:T(8,128)(2,1)S(1)}, bf16[528,256]{1,0:T(8,128)(2,1)S(1)}, u32[]{:S(2)}, u32[]{:S(2)}) collective-permute-start(bf16[528,256]{1,0:T(8,128)(2,1)S(1)} %get-tuple-element.97), channel_id=1, source_target_pairs={{0,32},{32,64},{64,96},{96,0},{1,33},{33,65},{65,97},{97,1},{2,34}... | collective-permute-start | bytes 811016 | tf_op jit(solution)/shard_map/ppermute | solution.py:416
  126.3 18.5 %collective-permute-start.28 = (bf16[528,256]{1,0:T(8,128)(2,1)S(1)}, bf16[528,256]{1,0:T(8,128)(2,1)S(1)}, u32[]{:S(2)}, u32[]{:S(2)}) collective-permute-start(bf16[528,256]{1,0:T(8,128)(2,1)S(1)} %get-tuple-element.98), channel_id=1, source_target_pairs={{0,96},{32,0},{64,32},{96,64},{1,97},{33,1},{65,33},{97,65},{2,98}... | collective-permute-start | bytes 811016 | tf_op jit(solution)/shard_map/ppermute | solution.py:416
  137.0 9.5 %collective-permute-start.23 = (bf16[528,256]{1,0:T(8,128)(2,1)S(1)}, bf16[528,256]{1,0:T(8,128)(2,1)S(1)}, u32[]{:S(2)}, u32[]{:S(2)}) collective-permute-start(bf16[528,256]{1,0:T(8,128)(2,1)S(1)} %get-tuple-element.89), channel_id=1, source_target_pairs={{0,32},{32,64},{64,96},{96,0},{1,33},{33,65},{65,97},{97,1},{2,34}... | collective-permute-start | bytes 811016 | tf_op jit(solution)/shard_map/ppermute | solution.py:416
  137.7 8.8 %collective-permute-start.24 = (bf16[528,256]{1,0:T(8,128)(2,1)S(1)}, bf16[528,256]{1,0:T(8,128)(2,1)S(1)}, u32[]{:S(2)}, u32[]{:S(2)}) collective-permute-start(bf16[528,256]{1,0:T(8,128)(2,1)S(1)} %get-tuple-element.90), channel_id=1, source_target_pairs={{0,96},{32,0},{64,32},{96,64},{1,97},{33,1},{65,33},{97,65},{2,98}... | collective-permute-start | bytes 811016 | tf_op jit(solution)/shard_map/ppermute | solution.py:416

commit v6 on v5

--- a/solution.py
+++ b/solution.py
@@ -274,7 +274,7 @@
     plan_ref, mass_ref, up_ref, down_ref, lines_ref = refs
     scale = local_scale(place_ref, sums_ref, lines_ref)
     tiles = tiles_of(w_refs)
-    rows = 2 * LANES
+    rows = 4 * LANES
     n = plan_ref.shape[0]
     half = n // 2
     for top in range(0, n, rows):

time: 149 us -> 149 us (level)
  no operation moved by 1% of the time
where the time goes in v6:
time: 149 us
  starting transfers between devices  43.6 us (29%)
  Pallas kernels  38.9 us (26%)
  blocking collectives  36.3 us (24%)
  waiting for transfers between devices  26 us (17%)
  local copies, waits for them, and re-layouts  2.31 us (2%)
    all_to_all x3, blocking collectives, body(): sums = lax.all_to_all(sums, CENTS, 0, 0, tiled=True)  36.3 us
    ppermute x22, starting transfers between devices, move(): return lax.ppermute(x, axis, [(i, (i + by) % n) for i in range(n)])  30.1 us
    ppermute x22, waiting for transfers between devices, move(): return lax.ppermute(x, axis, [(i, (i + by) % n) for i in range(n)])  21.4 us
    pallas_call x6, Pallas kernels, call(): pl.pallas_call(kernel, in_specs=specs, out_specs=[VM] * len(out_shape), o...  13.8 us
    ppermute x7, starting transfers between devices, spread(): return lax.ppermute(x, CENTS, pairs)  13.5 us
    pallas_call x3, Pallas kernels, weigh(): pl.pallas_call(functools.partial(weigh_kernel, len(blocks), at, last), in...  11.4 us
    pallas_call x3, Pallas kernels, row_pass(): pl.pallas_call(lambda *refs: row_kernel(target, *refs), in_specs=[SM] + [...  5.39 us
    ppermute x7, waiting for transfers between devices, spread(): return lax.ppermute(x, CENTS, pairs)  4.61 us
  transfers between devices with their start and end apart: 29, of which 15 were waited for; matrix products, arithmetic and copies ran while one was open for 0% of the time, Pallas kernels for 14%

profile of v6, /device:TPU:0, one launch (start us, length us, event | category | flops | bytes accessed | tf_op | source)
XLA Modules:
  0.0 148.6 jit_solution(7514457123248807638)
XLA Ops:
  0.6 1.6 %collective-permute-start = (bf16[64,1024]{1,0:T(8,128)(2,1)}, bf16[64,1024]{1,0:T(8,128)(2,1)S(1)}, u32[]{:S(2)}, u32[]{:S(2)}) collective-permute-start(bf16[64,1024]{1,0:T(8,128)(2,1)} %x_ref.1), channel_id=1, source_target_pairs={{0,8},{1,3},{2,10},{3,5},{4,12},{5,7},{6,14},{7,1},{8,16},{9,11},{... | collective-permute-start | bytes 393224 | tf_op jit(solution)/shard_map/ppermute | solution.py:429
  2.3 2.7 %collective-permute-start.1 = (bf16[64,1024]{1,0:T(8,128)(2,1)}, bf16[64,1024]{1,0:T(8,128)(2,1)S(1)}, u32[]{:S(2)}, u32[]{:S(2)}) collective-permute-start(bf16[64,1024]{1,0:T(8,128)(2,1)} %x_ref.1), channel_id=1, source_target_pairs={{0,16},{1,5},{2,18},{3,7},{4,20},{5,1},{6,22},{7,3},{8,24},{9,13},... | collective-permute-start | bytes 393224 | tf_op jit(solution)/shard_map/ppermute | solution.py:429
  5.0 1.4 collective-permute-start.2
  6.4 0.9 lift.1.refs_0_
  7.4 0.1 stack.20.place_ref.refs_0_
  7.5 2.1 %collective-permute-done.1.refs_2_ = bf16[64,1024]{1,0:T(8,128)(2,1)S(1)} collective-permute-done((bf16[64,1024]{1,0:T(8,128)(2,1)}, bf16[64,1024]{1,0:T(8,128)(2,1)S(1)}, u32[]{:S(2)}, u32[]{:S(2)}) %collective-permute-start.1) | collective-permute-done | bytes 131104 | tf_op jit(solution)/shard_map/ppermute | solution.py:429
  9.6 0.6 collective-permute-done.2.refs_3_
  10.2 0.6 in_order.1.refs_0_
  10.9 2.0 %collective-permute-start.4 = (bf16[256,1024]{1,0:T(8,128)(2,1)S(1)}, bf16[256,1024]{1,0:T(8,128)(2,1)S(1)}, u32[]{:S(2)}, u32[]{:S(2)}) collective-permute-start(bf16[256,1024]{1,0:T(8,128)(2,1)S(1)} %in_order.1.refs_0_), channel_id=1, source_target_pairs={{0,2},{1,9},{2,4},{3,11},{4,6},{5,13},{6,0},{7,15},{8,10},{9,17},{... | collective-permute-start | bytes 1572872 | tf_op jit(solution)/shard_map/ppermute | solution.py:429
  12.9 2.2 %collective-permute-start.5 = (bf16[256,1024]{1,0:T(8,128)(2,1)S(1)}, bf16[256,1024]{1,0:T(8,128)(2,1)S(1)}, u32[]{:S(2)}, u32[]{:S(2)}) collective-permute-start(bf16[256,1024]{1,0:T(8,128)(2,1)S(1)} %in_order.1.refs_0_), channel_id=1, source_target_pairs={{0,6},{1,25},{2,0},{3,27},{4,2},{5,29},{6,4},{7,31},{8,14},{9,1},{... | collective-permute-start | bytes 1572872 | tf_op jit(solution)/shard_map/ppermute | solution.py:429
  15.1 2.2 %copy-done = bf16[2048,1024]{1,0:T(8,128)(2,1)S(1)} copy-done((bf16[2048,1024]{1,0:T(8,128)(2,1)S(1)}, bf16[2048,1024]{1,0:T(8,128)(2,1)}, u32[]{:S(2)}) %copy-start) | copy-done | bytes 4194328
  17.2 3.0 %weigh.3 = (f32[2048,512]{1,0:T(8,128)S(1)}, bf16[2048,256]{1,0:T(8,128)(2,1)S(1)}, bf16[2048,256]{1,0:T(8,128)(2,1)S(1)}, bf16[2048,256]{1,0:T(8,128)(2,1)S(1)}...) custom-call(s32[5]{0:T(128)S(1)} %stack.20.place_ref.refs_0_, bf16[2048,1024]{1,0:T(8,128)(2,1)S(1)} %copy-done, ...), custom_call_target="tpu_custom_call" | custom-call | flops 30000001024 | tf_op jit(solution)/shard_map/weigh/pallas_call | solution.py:126
  20.2 1.9 %collective-permute-done.4.refs_0_ = bf16[256,1024]{1,0:T(8,128)(2,1)S(1)} collective-permute-done((bf16[256,1024]{1,0:T(8,128)(2,1)S(1)}, bf16[256,1024]{1,0:T(8,128)(2,1)S(1)}, u32[]{:S(2)}, u32[]{:S(2)}) %collective-permute-start.4) | collective-permute-done | bytes 524320 | tf_op jit(solution)/shard_map/ppermute | solution.py:429
  22.1 0.5 collective-permute-start.7
  22.7 1.9 %collective-permute-start.8 = (bf16[128,1024]{1,0:T(8,128)(2,1)S(1)}, bf16[128,1024]{1,0:T(8,128)(2,1)S(1)}, u32[]{:S(2)}, u32[]{:S(2)}) collective-permute-start(bf16[128,1024]{1,0:T(8,128)(2,1)S(1)} %slice.6), channel_id=1, source_target_pairs={{0,2},{1,9},{2,4},{3,11},{4,6},{5,13},{6,0},{7,15},{8,10},{9,17},{... | collective-permute-start | bytes 786440 | tf_op jit(solution)/shard_map/ppermute | solution.py:429
  24.6 1.6 %collective-permute-start.9 = (bf16[128,1024]{1,0:T(8,128)(2,1)S(1)}, bf16[128,1024]{1,0:T(8,128)(2,1)S(1)}, u32[]{:S(2)}, u32[]{:S(2)}) collective-permute-start(bf16[128,1024]{1,0:T(8,128)(2,1)S(1)} %slice.7), channel_id=1, source_target_pairs={{0,6},{1,25},{2,0},{3,27},{4,2},{5,29},{6,4},{7,31},{8,14},{9,1},{... | collective-permute-start | bytes 786440 | tf_op jit(solution)/shard_map/ppermute | solution.py:429
  26.2 5.3 %weigh.4 = (f32[2048,1024]{1,0:T(8,128)S(1)}, bf16[2048,256]{1,0:T(8,128)(2,1)S(1)}, bf16[2048,256]{1,0:T(8,128)(2,1)S(1)}, bf16[2048,256]{1,0:T(8,128)(2,1)S(1)...) custom-call(s32[5]{0:T(128)S(1)} %stack.20.place_ref.refs_0_, ...), custom_call_target="tpu_custom_call", output_to_operand_aliasing={{1}: (6, {}), {2}: (7, {}), {3}: (8, {}), {4}: (9, {}), {5}... | custom-call | flops 30000001024 | tf_op jit(solution)/shard_map/weigh/pallas_call | solution.py:126
  31.6 0.5 collective-permute-start.11
  32.1 1.0 collective-permute-done.10.refs_2_
  33.1 0.4 collective-permute-done.11.refs_3_
  33.5 3.1 %weigh.5 = (f32[2048,512]{1,0:T(8,128)S(1)}, bf16[2048,256]{1,0:T(8,128)(2,1)S(1)}, bf16[2048,256]{1,0:T(8,128)(2,1)S(1)}, bf16[2048,256]{1,0:T(8,128)(2,1)S(1)}...) custom-call(s32[5]{0:T(128)S(1)} %stack.20.place_ref.refs_0_, ...), custom_call_target="tpu_custom_call", output_to_operand_aliasing={{1}: (6, {}), {2}: (7, {}), {3}: (8, {}), {4}: (9, {}), {5}... | custom-call | flops 30000001024 | tf_op jit(solution)/shard_map/weigh/pallas_call | solution.py:126
  36.6 3.5 %collective-permute-start.12 = (f32[16,128]{1,0:T(8,128)S(1)}, f32[16,128]{1,0:T(8,128)S(1)}, u32[]{:S(2)}, u32[]{:S(2)}) collective-permute-start(f32[16,128]{1,0:T(8,128)S(1)} %get-tuple-element.72.refs_4_), channel_id=1, source_target_pairs={{0,64},{32,96},{64,0},{96,32},{1,65},{33,97},{65,1},{97,33},{2,66}... | collective-permute-start | bytes 24584 | tf_op jit(solution)/shard_map/ppermute | solution.py:416
  40.0 0.7 collective-permute-start.13
  40.7 2.6 %collective-permute-start.14 = (f32[16,128]{1,0:T(8,128)S(1)}, f32[16,128]{1,0:T(8,128)S(1)}, u32[]{:S(2)}, u32[]{:S(2)}) collective-permute-start(f32[16,128]{1,0:T(8,128)S(1)} %get-tuple-element.72.refs_4_), channel_id=1, source_target_pairs={{0,96},{32,0},{64,32},{96,64},{1,97},{33,1},{65,33},{97,65},{2,98}... | collective-permute-start | bytes 24584 | tf_op jit(solution)/shard_map/ppermute | solution.py:416
  43.3 1.6 %collective-permute-done.13.refs_6_ = f32[16,128]{1,0:T(8,128)S(1)} collective-permute-done((f32[16,128]{1,0:T(8,128)S(1)}, f32[16,128]{1,0:T(8,128)S(1)}, u32[]{:S(2)}, u32[]{:S(2)}) %collective-permute-start.13) | collective-permute-done | bytes 8224 | tf_op jit(solution)/shard_map/ppermute | solution.py:416
  44.9 1.8 %row_pass.3 = (bf16[32,16,128]{2,1,0:T(8,128)(2,1)S(1)}, f32[16,128]{1,0:T(8,128)}) custom-call(s32[5]{0:T(128)S(1)} %stack.20.place_ref.refs_0_, f32[2048,512]{1,0:T(8,128)S(1)} %get-tuple-element.53.refs_1_.refs_0_, f32[2048,1024]{1,0:T(8,128)S(1)} %get-tuple-element.62.refs_2_.refs_1_, f32[2048,512]{1,0:T(8,128)S(1)} %get-tuple-element.71.refs_3_.refs_2_, ...), custom_call_target="tpu_custom_call" | custom-call | tf_op jit(solution)/shard_map/row_pass/pallas_call | solution.py:184
  46.7 13.8 %all_to_all.15.refs_3_ = bf16[32,16,128]{2,1,0:T(8,128)(2,1)S(1)} all-to-all(bf16[32,16,128]{2,1,0:T(8,128)(2,1)S(1)} %get-tuple-element.73), channel_id=1, replica_groups=mesh['y'=4,'x'=4,'z'=4,'core'=2] {'x','z','core'}, dimensions={0} | all-to-all | bytes 262144 | tf_op jit(solution)/shard_map/all_to_all | solution.py:462
  60.5 1.8 %col_pass.2.refs_4_ = f32[16,128]{1,0:T(8,128)S(1)} custom-call(s32[5]{0:T(128)S(1)} %stack.20.place_ref.refs_0_, f32[2048,512]{1,0:T(8,128)S(1)} %get-tuple-element.53.refs_1_.refs_0_, f32[2048,1024]{1,0:T(8,128)S(1)} %get-tuple-element.62.refs_2_.refs_1_, f32[2048,512]{1,0:T(8,128)S(1)} %get-tuple-element.71.refs_3_.refs_2_, ...), custom_call_target="tpu_custom_call" | custom-call | tf_op jit(solution)/shard_map/col_pass/pallas_call | solution.py:223
  62.3 1.5 %collective-permute-start.15 = (f32[16,128]{1,0:T(8,128)S(1)}, f32[16,128]{1,0:T(8,128)S(1)}, u32[]{:S(2)}, u32[]{:S(2)}) collective-permute-start(f32[16,128]{1,0:T(8,128)S(1)} %col_pass.2.refs_4_), channel_id=1, source_target_pairs={{0,64},{32,96},{64,0},{96,32},{1,65},{33,97},{65,1},{97,33},{2,66}... | collective-permute-start | bytes 24584 | tf_op jit(solution)/shard_map/ppermute | solution.py:416
  63.8 2.6 %collective-permute-start.16 = (f32[16,128]{1,0:T(8,128)S(1)}, f32[16,128]{1,0:T(8,128)S(1)}, u32[]{:S(2)}, u32[]{:S(2)}) collective-permute-start(f32[16,128]{1,0:T(8,128)S(1)} %col_pass.2.refs_4_), channel_id=1, source_target_pairs={{0,32},{32,64},{64,96},{96,0},{1,33},{33,65},{65,97},{97,1},{2,34}... | collective-permute-start | bytes 24584 | tf_op jit(solution)/shard_map/ppermute | solution.py:416
  66.5 0.6 collective-permute-start.17
  67.1 0.5 collective-permute-done.15.refs_5_
  67.5 1.2 collective-permute-done.16.refs_6_
  68.7 1.4 collective-permute-done.17.refs_7_
  70.1 1.8 %row_pass.4 = (bf16[32,16,128]{2,1,0:T(8,128)(2,1)S(1)}, f32[16,128]{1,0:T(8,128)}) custom-call(s32[5]{0:T(128)S(1)} %stack.20.place_ref.refs_0_, f32[2048,512]{1,0:T(8,128)S(1)} %get-tuple-element.53.refs_1_.refs_0_, f32[2048,1024]{1,0:T(8,128)S(1)} %get-tuple-element.62.refs_2_.refs_1_, f32[2048,512]{1,0:T(8,128)S(1)} %get-tuple-element.71.refs_3_.refs_2_, ...), custom_call_target="tpu_custom_call" | custom-call | tf_op jit(solution)/shard_map/row_pass/pallas_call | solution.py:184
  71.9 11.3 %all_to_all.16.refs_3_ = bf16[32,16,128]{2,1,0:T(8,128)(2,1)S(1)} all-to-all(bf16[32,16,128]{2,1,0:T(8,128)(2,1)S(1)} %get-tuple-element.74), channel_id=1, replica_groups=mesh['y'=4,'x'=4,'z'=4,'core'=2] {'x','z','core'}, dimensions={0} | all-to-all | bytes 262144 | tf_op jit(solution)/shard_map/all_to_all | solution.py:462
  83.2 1.8 %col_pass.3.refs_4_ = f32[16,128]{1,0:T(8,128)S(1)} custom-call(s32[5]{0:T(128)S(1)} %stack.20.place_ref.refs_0_, f32[2048,512]{1,0:T(8,128)S(1)} %get-tuple-element.53.refs_1_.refs_0_, f32[2048,1024]{1,0:T(8,128)S(1)} %get-tuple-element.62.refs_2_.refs_1_, f32[2048,512]{1,0:T(8,128)S(1)} %get-tuple-element.71.refs_3_.refs_2_, ...), custom_call_target="tpu_custom_call" | custom-call | tf_op jit(solution)/shard_map/col_pass/pallas_call | solution.py:223
  85.0 0.8 collective-permute-start.18
  85.8 2.0 %collective-permute-start.19 = (f32[16,128]{1,0:T(8,128)S(1)}, f32[16,128]{1,0:T(8,128)S(1)}, u32[]{:S(2)}, u32[]{:S(2)}) collective-permute-start(f32[16,128]{1,0:T(8,128)S(1)} %col_pass.3.refs_4_), channel_id=1, source_target_pairs={{0,32},{32,64},{64,96},{96,0},{1,33},{33,65},{65,97},{97,1},{2,34}... | collective-permute-start | bytes 24584 | tf_op jit(solution)/shard_map/ppermute | solution.py:416
  87.8 1.2 collective-permute-start.20
  89.0 1.2 collective-permute-done.18.refs_5_
  90.2 0.4 collective-permute-done.19.refs_6_
  90.6 0.8 collective-permute-done.20.refs_7_
  91.4 1.8 %row_pass.5 = (bf16[32,16,128]{2,1,0:T(8,128)(2,1)S(1)}, f32[16,128]{1,0:T(8,128)S(1)}, f32[2048,128]{1,0:T(8,128)S(1)}) custom-call(s32[5]{0:T(128)S(1)} %stack.20.place_ref.refs_0_, f32[2048,512]{1,0:T(8,128)S(1)} %get-tuple-element.53.refs_1_.refs_0_, f32[2048,1024]{1,0:T(8,128)S(1)} %get-tuple-element.62.refs_2_.refs_1_, ...), custom_call_target="tpu_custom_call" | custom-call | tf_op jit(solution)/shard_map/row_pass/pallas_call | solution.py:184
  93.2 11.3 %all_to_all.17.refs_4_ = bf16[32,16,128]{2,1,0:T(8,128)(2,1)S(1)} all-to-all(bf16[32,16,128]{2,1,0:T(8,128)(2,1)S(1)} %get-tuple-element.75), channel_id=1, replica_groups=mesh['y'=4,'x'=4,'z'=4,'core'=2] {'x','z','core'}, dimensions={0} | all-to-all | bytes 262144 | tf_op jit(solution)/shard_map/all_to_all | solution.py:462
  104.5 3.5 %make_plan.2 = (bf16[1024,2048]{1,0:T(8,128)(2,1)S(1)}, f32[8,128]{1,0:T(8,128)S(1)}, bf16[1040,256]{1,0:T(8,128)(2,1)S(1)}, bf16[1040,256]{1,0:T(8,128)(2,1)S(1)}) custom-call(s32[5]{0:T(128)S(1)} %stack.20.place_ref.refs_0_, f32[2048,512]{1,0:T(8,128)S(1)} %get-tuple-element.53.refs_1_.refs_0_, f32[2048,1024]{1,0:T(8,128)S(1)} %get-tuple-element.62.refs_2_.refs_1_, ...), custom_call_target="tpu_custom_call" | custom-call | flops 30000001024 | tf_op jit(solution)/shard_map/make_plan/pallas_call | solution.py:260
  108.0 0.9 collective-permute-start.25
  108.9 2.4 %collective-permute-start.26 = (bf16[1040,256]{1,0:T(8,128)(2,1)S(1)}, bf16[1040,256]{1,0:T(8,128)(2,1)S(1)}, u32[]{:S(2)}, u32[]{:S(2)}) collective-permute-start(bf16[1040,256]{1,0:T(8,128)(2,1)S(1)} %get-tuple-element.94), channel_id=1, source_target_pairs={{0,96},{32,0},{64,32},{96,64},{1,97},{33,1},{65,33},{97,65},{2,98}... | collective-permute-start | bytes 1597448 | tf_op jit(solution)/shard_map/ppermute | solution.py:416
  111.3 3.5 %make_plan.3 = (bf16[1024,2048]{1,0:T(8,128)(2,1)S(1)}, f32[8,128]{1,0:T(8,128)S(1)}, bf16[1040,256]{1,0:T(8,128)(2,1)S(1)}, bf16[1040,256]{1,0:T(8,128)(2,1)S(1)}) custom-call(s32[5]{0:T(128)S(1)} %stack.20.place_ref.refs_0_, f32[2048,512]{1,0:T(8,128)S(1)} %get-tuple-element.53.refs_1_.refs_0_, f32[2048,1024]{1,0:T(8,128)S(1)} %get-tuple-element.62.refs_2_.refs_1_, ...), custom_call_target="tpu_custom_call" | custom-call | flops 30000001024 | tf_op jit(solution)/shard_map/make_plan/pallas_call | solution.py:260
  114.8 3.2 %collective-permute-start.22 = (bf16[1040,256]{1,0:T(8,128)(2,1)S(1)}, bf16[1040,256]{1,0:T(8,128)(2,1)S(1)}, u32[]{:S(2)}, u32[]{:S(2)}) collective-permute-start(bf16[1040,256]{1,0:T(8,128)(2,1)S(1)} %get-tuple-element.83), channel_id=1, source_target_pairs={{0,96},{32,0},{64,32},{96,64},{1,97},{33,1},{65,33},{97,65},{2,98}... | collective-permute-start | bytes 1597448 | tf_op jit(solution)/shard_map/ppermute | solution.py:416
  118.1 6.2 %collective-permute-done.25.from_below.below = bf16[1040,256]{1,0:T(8,128)(2,1)S(1)} collective-permute-done((bf16[1040,256]{1,0:T(8,128)(2,1)S(1)}, bf16[1040,256]{1,0:T(8,128)(2,1)S(1)}, u32[]{:S(2)}, u32[]{:S(2)}) %collective-permute-start.25) | collective-permute-done | bytes 532512 | tf_op jit(solution)/shard_map/ppermute | solution.py:416
  124.2 1.3 late_sums.3
  125.5 0.7 collective-permute-start.27
  126.2 2.7 %collective-permute-start.28 = (bf16[528,256]{1,0:T(8,128)(2,1)S(1)}, bf16[528,256]{1,0:T(8,128)(2,1)S(1)}, u32[]{:S(2)}, u32[]{:S(2)}) collective-permute-start(bf16[528,256]{1,0:T(8,128)(2,1)S(1)} %get-tuple-element.98), channel_id=1, source_target_pairs={{0,96},{32,0},{64,32},{96,64},{1,97},{33,1},{65,33},{97,65},{2,98}... | collective-permute-start | bytes 811016 | tf_op jit(solution)/shard_map/ppermute | solution.py:416
  128.9 6.7 %collective-permute-done.21.from_below.refs_4_ = bf16[1040,256]{1,0:T(8,128)(2,1)S(1)} collective-permute-done((bf16[1040,256]{1,0:T(8,128)(2,1)S(1)}, bf16[1040,256]{1,0:T(8,128)(2,1)S(1)}, u32[]{:S(2)}, u32[]{:S(2)}) %collective-permute-start.21) | collective-permute-done | bytes 532512 | tf_op jit(solution)/shard_map/ppermute | solution.py:416
  135.6 1.3 late_sums.2
  136.9 0.7 collective-permute-start.23
  137.6 2.7 %collective-permute-start.24 = (bf16[528,256]{1,0:T(8,128)(2,1)S(1)}, bf16[528,256]{1,0:T(8,128)(2,1)S(1)}, u32[]{:S(2)}, u32[]{:S(2)}) collective-permute-start(bf16[528,256]{1,0:T(8,128)(2,1)S(1)} %get-tuple-element.90), channel_id=1, source_target_pairs={{0,96},{32,0},{64,32},{96,64},{1,97},{33,1},{65,33},{97,65},{2,98}... | collective-permute-start | bytes 811016 | tf_op jit(solution)/shard_map/ppermute | solution.py:416
  140.3 2.5 %own_sums.3 = (f32[1024,256]{1,0:T(8,128)S(1)}, bf16[1024,256]{1,0:T(8,128)(2,1)S(1)}) custom-call(s32[5]{0:T(128)S(1)} %stack.20.place_ref.refs_0_, bf16[1024,2048]{1,0:T(8,128)(2,1)S(1)} %get-tuple-element.92.plan_ref, bf16[1040,256]{1,0:T(8,128)(2,1)S(1)} %collective-permute-done.25.from_below.below, ...), custom_call_target="tpu_custom_call" | custom-call | flops 30000001024 | tf_op jit(solution)/shard_map/own_sums/pallas_call | solution.py:260
  142.8 1.8 %own_sums.2 = (f32[1024,256]{1,0:T(8,128)S(1)}, bf16[1024,256]{1,0:T(8,128)(2,1)S(1)}) custom-call(s32[5]{0:T(128)S(1)} %stack.20.place_ref.refs_0_, bf16[1024,2048]{1,0:T(8,128)(2,1)S(1)} %get-tuple-element.81.plan_ref, bf16[1040,256]{1,0:T(8,128)(2,1)S(1)} %collective-permute-done.21.from_below.refs_4_, ...), custom_call_target="tpu_custom_call" | custom-call | flops 30000001024 | tf_op jit(solution)/shard_map/own_sums/pallas_call | solution.py:260
  144.7 1.6 %finish.2 = (bf16[2048,256]{1,0:T(8,128)(2,1)}, f32[8,128]{1,0:T(8,128)S(1)}) custom-call(s32[5]{0:T(128)S(1)} %stack.20.place_ref.refs_0_, f32[1024,256]{1,0:T(8,128)S(1)} %get-tuple-element.96.own_ref, f32[16,128]{1,0:T(8,128)S(1)} %get-tuple-element.87.scale_ref.refs_2_, f32[8,128]{1,0:T(8,128)S(1)} %get-tuple-element.80.refs_6_.m_ref, ...), custom_call_target="tpu_custom_call" | custom-call | flops 30000001024 | tf_op jit(solution)/shard_map/finish/pallas_call | solution.py:395
  146.3 0.1 collective-permute-done.23.refs_6_
  146.4 1.6 %finish.3 = (bf16[2048,256]{1,0:T(8,128)(2,1)}, f32[8,128]{1,0:T(8,128)S(1)}) custom-call(s32[5]{0:T(128)S(1)} %stack.20.place_ref.refs_0_, f32[1024,256]{1,0:T(8,128)S(1)} %get-tuple-element.86.refs_1_, f32[16,128]{1,0:T(8,128)S(1)} %get-tuple-element.87.scale_ref.refs_2_, ...), custom_call_target="tpu_custom_call", output_to_operand_aliasing={{0}: (10, {})} | custom-call | flops 30000001024 | tf_op jit(solution)/shard_map/finish/pallas_call | solution.py:395
  148.0 0.6 maximum_bitcast_fusion
  (22 shorter events, 0.3 us)
Async XLA Ops:
  0.6 6.9 %collective-permute-start = (bf16[64,1024]{1,0:T(8,128)(2,1)}, bf16[64,1024]{1,0:T(8,128)(2,1)S(1)}, u32[]{:S(2)}, u32[]{:S(2)}) collective-permute-start(bf16[64,1024]{1,0:T(8,128)(2,1)} %x_ref.1), channel_id=1, source_target_pairs={{0,8},{1,3},{2,10},{3,5},{4,12},{5,7},{6,14},{7,1},{8,16},{9,11},{... | collective-permute-start | bytes 393224 | tf_op jit(solution)/shard_map/ppermute | solution.py:429
  2.3 7.3 %collective-permute-start.1 = (bf16[64,1024]{1,0:T(8,128)(2,1)}, bf16[64,1024]{1,0:T(8,128)(2,1)S(1)}, u32[]{:S(2)}, u32[]{:S(2)}) collective-permute-start(bf16[64,1024]{1,0:T(8,128)(2,1)} %x_ref.1), channel_id=1, source_target_pairs={{0,16},{1,5},{2,18},{3,7},{4,20},{5,1},{6,22},{7,3},{8,24},{9,13},... | collective-permute-start | bytes 393224 | tf_op jit(solution)/shard_map/ppermute | solution.py:429
  5.0 5.2 %collective-permute-start.2 = (bf16[64,1024]{1,0:T(8,128)(2,1)}, bf16[64,1024]{1,0:T(8,128)(2,1)S(1)}, u32[]{:S(2)}, u32[]{:S(2)}) collective-permute-start(bf16[64,1024]{1,0:T(8,128)(2,1)} %x_ref.1), channel_id=1, source_target_pairs={{0,24},{1,7},{2,26},{3,1},{4,28},{5,3},{6,30},{7,5},{8,0},{9,15},{... | collective-permute-start | bytes 393224 | tf_op jit(solution)/shard_map/ppermute | solution.py:429
  10.8 4.3 %collective-permute-start.3 = (bf16[256,1024]{1,0:T(8,128)(2,1)S(1)}, bf16[256,1024]{1,0:T(8,128)(2,1)S(1)}, u32[]{:S(2)}, u32[]{:S(2)}) collective-permute-start(bf16[256,1024]{1,0:T(8,128)(2,1)S(1)} %in_order.1.refs_0_), channel_id=1, source_target_pairs={{0,1},{1,0},{2,3},{3,2},{4,5},{5,4},{6,7},{7,6},{8,9},{9,8},{10,11... | collective-permute-start | bytes 1572872 | tf_op jit(solution)/shard_map/ppermute | solution.py:416
  10.9 11.3 %collective-permute-start.4 = (bf16[256,1024]{1,0:T(8,128)(2,1)S(1)}, bf16[256,1024]{1,0:T(8,128)(2,1)S(1)}, u32[]{:S(2)}, u32[]{:S(2)}) collective-permute-start(bf16[256,1024]{1,0:T(8,128)(2,1)S(1)} %in_order.1.refs_0_), channel_id=1, source_target_pairs={{0,2},{1,9},{2,4},{3,11},{4,6},{5,13},{6,0},{7,15},{8,10},{9,17},{... | collective-permute-start | bytes 1572872 | tf_op jit(solution)/shard_map/ppermute | solution.py:429
  12.9 9.3 %collective-permute-start.5 = (bf16[256,1024]{1,0:T(8,128)(2,1)S(1)}, bf16[256,1024]{1,0:T(8,128)(2,1)S(1)}, u32[]{:S(2)}, u32[]{:S(2)}) collective-permute-start(bf16[256,1024]{1,0:T(8,128)(2,1)S(1)} %in_order.1.refs_0_), channel_id=1, source_target_pairs={{0,6},{1,25},{2,0},{3,27},{4,2},{5,29},{6,4},{7,31},{8,14},{9,1},{... | collective-permute-start | bytes 1572872 | tf_op jit(solution)/shard_map/ppermute | solution.py:429
  15.1 2.2 %copy-start = (bf16[2048,1024]{1,0:T(8,128)(2,1)S(1)}, bf16[2048,1024]{1,0:T(8,128)(2,1)}, u32[]{:S(2)}) copy-start(bf16[2048,1024]{1,0:T(8,128)(2,1)} %cents_ref.9) | copy-start | bytes 12582916
  22.1 4.0 %collective-permute-start.6 = (bf16[256,1024]{1,0:T(8,128)(2,1)S(1)}, bf16[256,1024]{1,0:T(8,128)(2,1)S(1)}, u32[]{:S(2)}, u32[]{:S(2)}) collective-permute-start(bf16[256,1024]{1,0:T(8,128)(2,1)S(1)} %collective-permute-done.4.refs_0_), channel_id=1, source_target_pairs={{0,1},{1,0},{2,3},{3,2},{4,5},{5,4},{6,7},{7,6},{8,9},{9,8},{10,11... | collective-permute-start | bytes 1572872 | tf_op jit(solution)/shard_map/ppermute | solution.py:416
  22.1 4.0 %collective-permute-start.7 = (bf16[256,1024]{1,0:T(8,128)(2,1)S(1)}, bf16[256,1024]{1,0:T(8,128)(2,1)S(1)}, u32[]{:S(2)}, u32[]{:S(2)}) collective-permute-start(bf16[256,1024]{1,0:T(8,128)(2,1)S(1)} %collective-permute-done.5.refs_1_), channel_id=1, source_target_pairs={{0,1},{1,0},{2,3},{3,2},{4,5},{5,4},{6,7},{7,6},{8,9},{9,8},{10,11... | collective-permute-start | bytes 1572872 | tf_op jit(solution)/shard_map/ppermute | solution.py:416
  22.7 8.8 %collective-permute-start.8 = (bf16[128,1024]{1,0:T(8,128)(2,1)S(1)}, bf16[128,1024]{1,0:T(8,128)(2,1)S(1)}, u32[]{:S(2)}, u32[]{:S(2)}) collective-permute-start(bf16[128,1024]{1,0:T(8,128)(2,1)S(1)} %slice.6), channel_id=1, source_target_pairs={{0,2},{1,9},{2,4},{3,11},{4,6},{5,13},{6,0},{7,15},{8,10},{9,17},{... | collective-permute-start | bytes 786440 | tf_op jit(solution)/shard_map/ppermute | solution.py:429
  24.6 6.9 %collective-permute-start.9 = (bf16[128,1024]{1,0:T(8,128)(2,1)S(1)}, bf16[128,1024]{1,0:T(8,128)(2,1)S(1)}, u32[]{:S(2)}, u32[]{:S(2)}) collective-permute-start(bf16[128,1024]{1,0:T(8,128)(2,1)S(1)} %slice.7), channel_id=1, source_target_pairs={{0,6},{1,25},{2,0},{3,27},{4,2},{5,29},{6,4},{7,31},{8,14},{9,1},{... | collective-permute-start | bytes 786440 | tf_op jit(solution)/shard_map/ppermute | solution.py:429
  31.5 1.6 %collective-permute-start.10 = (bf16[128,1024]{1,0:T(8,128)(2,1)S(1)}, bf16[128,1024]{1,0:T(8,128)(2,1)S(1)}, u32[]{:S(2)}, u32[]{:S(2)}) collective-permute-start(bf16[128,1024]{1,0:T(8,128)(2,1)S(1)} %collective-permute-done.8.refs_0_), channel_id=1, source_target_pairs={{0,1},{1,0},{2,3},{3,2},{4,5},{5,4},{6,7},{7,6},{8,9},{9,8},{10,11... | collective-permute-start | bytes 786440 | tf_op jit(solution)/shard_map/ppermute | solution.py:416
  31.6 1.9 %collective-permute-start.11 = (bf16[128,1024]{1,0:T(8,128)(2,1)S(1)}, bf16[128,1024]{1,0:T(8,128)(2,1)S(1)}, u32[]{:S(2)}, u32[]{:S(2)}) collective-permute-start(bf16[128,1024]{1,0:T(8,128)(2,1)S(1)} %collective-permute-done.9.refs_1_), channel_id=1, source_target_pairs={{0,1},{1,0},{2,3},{3,2},{4,5},{5,4},{6,7},{7,6},{8,9},{9,8},{10,11... | collective-permute-start | bytes 786440 | tf_op jit(solution)/shard_map/ppermute | solution.py:416
  36.6 6.7 %collective-permute-start.12 = (f32[16,128]{1,0:T(8,128)S(1)}, f32[16,128]{1,0:T(8,128)S(1)}, u32[]{:S(2)}, u32[]{:S(2)}) collective-permute-start(f32[16,128]{1,0:T(8,128)S(1)} %get-tuple-element.72.refs_4_), channel_id=1, source_target_pairs={{0,64},{32,96},{64,0},{96,32},{1,65},{33,97},{65,1},{97,33},{2,66}... | collective-permute-start | bytes 24584 | tf_op jit(solution)/shard_map/ppermute | solution.py:416
  40.0 4.9 %collective-permute-start.13 = (f32[16,128]{1,0:T(8,128)S(1)}, f32[16,128]{1,0:T(8,128)S(1)}, u32[]{:S(2)}, u32[]{:S(2)}) collective-permute-start(f32[16,128]{1,0:T(8,128)S(1)} %get-tuple-element.72.refs_4_), channel_id=1, source_target_pairs={{0,32},{32,64},{64,96},{96,0},{1,33},{33,65},{65,97},{97,1},{2,34}... | collective-permute-start | bytes 24584 | tf_op jit(solution)/shard_map/ppermute | solution.py:416
  40.7 4.2 %collective-permute-start.14 = (f32[16,128]{1,0:T(8,128)S(1)}, f32[16,128]{1,0:T(8,128)S(1)}, u32[]{:S(2)}, u32[]{:S(2)}) collective-permute-start(f32[16,128]{1,0:T(8,128)S(1)} %get-tuple-element.72.refs_4_), channel_id=1, source_target_pairs={{0,96},{32,0},{64,32},{96,64},{1,97},{33,1},{65,33},{97,65},{2,98}... | collective-permute-start | bytes 24584 | tf_op jit(solution)/shard_map/ppermute | solution.py:416
  62.3 5.2 %collective-permute-start.15 = (f32[16,128]{1,0:T(8,128)S(1)}, f32[16,128]{1,0:T(8,128)S(1)}, u32[]{:S(2)}, u32[]{:S(2)}) collective-permute-start(f32[16,128]{1,0:T(8,128)S(1)} %col_pass.2.refs_4_), channel_id=1, source_target_pairs={{0,64},{32,96},{64,0},{96,32},{1,65},{33,97},{65,1},{97,33},{2,66}... | collective-permute-start | bytes 24584 | tf_op jit(solution)/shard_map/ppermute | solution.py:416
  63.8 4.9 %collective-permute-start.16 = (f32[16,128]{1,0:T(8,128)S(1)}, f32[16,128]{1,0:T(8,128)S(1)}, u32[]{:S(2)}, u32[]{:S(2)}) collective-permute-start(f32[16,128]{1,0:T(8,128)S(1)} %col_pass.2.refs_4_), channel_id=1, source_target_pairs={{0,32},{32,64},{64,96},{96,0},{1,33},{33,65},{65,97},{97,1},{2,34}... | collective-permute-start | bytes 24584 | tf_op jit(solution)/shard_map/ppermute | solution.py:416
  66.5 3.7 %collective-permute-start.17 = (f32[16,128]{1,0:T(8,128)S(1)}, f32[16,128]{1,0:T(8,128)S(1)}, u32[]{:S(2)}, u32[]{:S(2)}) collective-permute-start(f32[16,128]{1,0:T(8,128)S(1)} %col_pass.2.refs_4_), channel_id=1, source_target_pairs={{0,96},{32,0},{64,32},{96,64},{1,97},{33,1},{65,33},{97,65},{2,98}... | collective-permute-start | bytes 24584 | tf_op jit(solution)/shard_map/ppermute | solution.py:416
  85.0 5.2 %collective-permute-start.18 = (f32[16,128]{1,0:T(8,128)S(1)}, f32[16,128]{1,0:T(8,128)S(1)}, u32[]{:S(2)}, u32[]{:S(2)}) collective-permute-start(f32[16,128]{1,0:T(8,128)S(1)} %col_pass.3.refs_4_), channel_id=1, source_target_pairs={{0,64},{32,96},{64,0},{96,32},{1,65},{33,97},{65,1},{97,33},{2,66}... | collective-permute-start | bytes 24584 | tf_op jit(solution)/shard_map/ppermute | solution.py:416
  85.8 4.9 %collective-permute-start.19 = (f32[16,128]{1,0:T(8,128)S(1)}, f32[16,128]{1,0:T(8,128)S(1)}, u32[]{:S(2)}, u32[]{:S(2)}) collective-permute-start(f32[16,128]{1,0:T(8,128)S(1)} %col_pass.3.refs_4_), channel_id=1, source_target_pairs={{0,32},{32,64},{64,96},{96,0},{1,33},{33,65},{65,97},{97,1},{2,34}... | collective-permute-start | bytes 24584 | tf_op jit(solution)/shard_map/ppermute | solution.py:416
  87.8 3.7 %collective-permute-start.20 = (f32[16,128]{1,0:T(8,128)S(1)}, f32[16,128]{1,0:T(8,128)S(1)}, u32[]{:S(2)}, u32[]{:S(2)}) collective-permute-start(f32[16,128]{1,0:T(8,128)S(1)} %col_pass.3.refs_4_), channel_id=1, source_target_pairs={{0,96},{32,0},{64,32},{96,64},{1,97},{33,1},{65,33},{97,65},{2,98}... | collective-permute-start | bytes 24584 | tf_op jit(solution)/shard_map/ppermute | solution.py:416
  108.0 16.2 %collective-permute-start.25 = (bf16[1040,256]{1,0:T(8,128)(2,1)S(1)}, bf16[1040,256]{1,0:T(8,128)(2,1)S(1)}, u32[]{:S(2)}, u32[]{:S(2)}) collective-permute-start(bf16[1040,256]{1,0:T(8,128)(2,1)S(1)} %get-tuple-element.93), channel_id=1, source_target_pairs={{0,32},{32,64},{64,96},{96,0},{1,33},{33,65},{65,97},{97,1},{2,34}... | collective-permute-start | bytes 1597448 | tf_op jit(solution)/shard_map/ppermute | solution.py:416
  108.9 15.3 %collective-permute-start.26 = (bf16[1040,256]{1,0:T(8,128)(2,1)S(1)}, bf16[1040,256]{1,0:T(8,128)(2,1)S(1)}, u32[]{:S(2)}, u32[]{:S(2)}) collective-permute-start(bf16[1040,256]{1,0:T(8,128)(2,1)S(1)} %get-tuple-element.94), channel_id=1, source_target_pairs={{0,96},{32,0},{64,32},{96,64},{1,97},{33,1},{65,33},{97,65},{2,98}... | collective-permute-start | bytes 1597448 | tf_op jit(solution)/shard_map/ppermute | solution.py:416
  114.8 20.9 %collective-permute-start.21 = (bf16[1040,256]{1,0:T(8,128)(2,1)S(1)}, bf16[1040,256]{1,0:T(8,128)(2,1)S(1)}, u32[]{:S(2)}, u32[]{:S(2)}) collective-permute-start(bf16[1040,256]{1,0:T(8,128)(2,1)S(1)} %get-tuple-element.82), channel_id=1, source_target_pairs={{0,32},{32,64},{64,96},{96,0},{1,33},{33,65},{65,97},{97,1},{2,34}... | collective-permute-start | bytes 1597448 | tf_op jit(solution)/shard_map/ppermute | solution.py:416
  114.8 20.8 %collective-permute-start.22 = (bf16[1040,256]{1,0:T(8,128)(2,1)S(1)}, bf16[1040,256]{1,0:T(8,128)(2,1)S(1)}, u32[]{:S(2)}, u32[]{:S(2)}) collective-permute-start(bf16[1040,256]{1,0:T(8,128)(2,1)S(1)} %get-tuple-element.83), channel_id=1, source_target_pairs={{0,96},{32,0},{64,32},{96,64},{1,97},{33,1},{65,33},{97,65},{2,98}... | collective-permute-start | bytes 1597448 | tf_op jit(solution)/shard_map/ppermute | solution.py:416
  125.5 19.1 %collective-permute-start.27 = (bf16[528,256]{1,0:T(8,128)(2,1)S(1)}, bf16[528,256]{1,0:T(8,128)(2,1)S(1)}, u32[]{:S(2)}, u32[]{:S(2)}) collective-permute-start(bf16[528,256]{1,0:T(8,128)(2,1)S(1)} %get-tuple-element.97), channel_id=1, source_target_pairs={{0,32},{32,64},{64,96},{96,0},{1,33},{33,65},{65,97},{97,1},{2,34}... | collective-permute-start | bytes 811016 | tf_op jit(solution)/shard_map/ppermute | solution.py:416
  126.2 18.4 %collective-permute-start.28 = (bf16[528,256]{1,0:T(8,128)(2,1)S(1)}, bf16[528,256]{1,0:T(8,128)(2,1)S(1)}, u32[]{:S(2)}, u32[]{:S(2)}) collective-permute-start(bf16[528,256]{1,0:T(8,128)(2,1)S(1)} %get-tuple-element.98), channel_id=1, source_target_pairs={{0,96},{32,0},{64,32},{96,64},{1,97},{33,1},{65,33},{97,65},{2,98}... | collective-permute-start | bytes 811016 | tf_op jit(solution)/shard_map/ppermute | solution.py:416
  136.9 9.5 %collective-permute-start.23 = (bf16[528,256]{1,0:T(8,128)(2,1)S(1)}, bf16[528,256]{1,0:T(8,128)(2,1)S(1)}, u32[]{:S(2)}, u32[]{:S(2)}) collective-permute-start(bf16[528,256]{1,0:T(8,128)(2,1)S(1)} %get-tuple-element.89), channel_id=1, source_target_pairs={{0,32},{32,64},{64,96},{96,0},{1,33},{33,65},{65,97},{97,1},{2,34}... | collective-permute-start | bytes 811016 | tf_op jit(solution)/shard_map/ppermute | solution.py:416
  137.6 8.8 %collective-permute-start.24 = (bf16[528,256]{1,0:T(8,128)(2,1)S(1)}, bf16[528,256]{1,0:T(8,128)(2,1)S(1)}, u32[]{:S(2)}, u32[]{:S(2)}) collective-permute-start(bf16[528,256]{1,0:T(8,128)(2,1)S(1)} %get-tuple-element.90), channel_id=1, source_target_pairs={{0,96},{32,0},{64,32},{96,64},{1,97},{33,1},{65,33},{97,65},{2,98}... | collective-permute-start | bytes 811016 | tf_op jit(solution)/shard_map/ppermute | solution.py:416
